TPU v7x, 256 devices: a whole 4x4x8 slice. The times are simulated.
256 devices in a mesh: depth: 16 (over y, x), area: 16 (over z, core).
Axes of the slice: x: 4, y: 4, z: 8, core: 2. Of those that a mesh axis runs over, the one named last changes fastest.
Arguments:
- states: float32 [8, 256, 256, 768], P(None, 'depth', 'area'), may hold values from 0 to 1
- tissue: int32 [64, 64, 192], P('depth', 'area'), may hold values 0 or 1
- fiber: int32 [64, 64, 192], P('depth', 'area'), may hold values from 0 to 7
Outputs:
- final_states: float32 [8, 256, 256, 768], P(None, 'depth', 'area')
- images: float32 [2, 2, 4, 256, 768], P(None, None, None, 'area', 'depth')
All inputs are finite; a program needn't handle non-finite values. No bound on the sum of `tissue` on one device may be relied on, other than what follows from the above.
Results may differ from a plain program's by a relative error of at most 0.0002.
Values sent between devices are 32-bit elements; how exact they have to be, the bound alone decides.
No kernel may reach another device: no remote copies, remote signals or barrier semaphores. Data moves between devices by JAX's collectives and lax.ppermute only.
A program may use at most 128 MiB of HBM per device.

v0:
```python
import math

import jax
import jax.numpy as jnp
from jax import lax
from jax.sharding import PartitionSpec as P

BLK = 4
CLASSES = 8
STEPS = 2


TIME_STEP = 0.15
SIGMA_LONG = 1.0
SIGMA_CROSS = 0.3
SLOPES = (8.0, -8.0, 6.0, 5.0, -5.0, -3.0)
MIDDLES = (0.2, 0.4, 0.3, 0.5, 0.6, 0.5)
RATES = (3.0, 0.5, 1.0, 0.8, 0.3, 0.1)
OPACITY = (0.012, 0.01)


def padded_2(x, sides, width):
    for axis, dim in sides:
        count, length = (lax.axis_size(axis), x.shape[dim])
        up = [(i, (i + 1) % count) for i in range(count - 1)]
        down = [(j, i) for i, j in up]
        last = lax.slice_in_dim(x, length - width, length, axis=dim)
        leading = lax.slice_in_dim(x, 0, width, axis=dim)
        before = lax.ppermute(last, axis, up)
        after = lax.ppermute(leading, axis, down)
        x = jnp.concatenate([before, x, after], axis=dim)
    return x


def side_by_side(arrays, axis, split_dim, concat_dim, along):
    widths = [a.shape[along] for a in arrays]
    both = jnp.concatenate(arrays, axis=along)
    out = lax.all_to_all(both, axis, split_axis=split_dim, concat_axis=concat_dim, tiled=True)
    return tuple(jnp.split(out, [sum(widths[:k]) for k in range(1, len(widths))], axis=along))


def spread_blocks(stacked):
    fields, first, second, third = stacked.shape
    columns = third * BLK
    onehot = (jnp.arange(columns)[None, :] // BLK == jnp.arange(third)[:, None]).astype(jnp.float32)
    along = jnp.dot(
        stacked.reshape(fields * first * second, third),
        onehot,
        precision=lax.Precision.HIGHEST,
        preferred_element_type=jnp.float32,
    )
    along = along.reshape(fields, first, 1, second, 1, columns)
    wide = jnp.broadcast_to(along, (fields, first, BLK, second, BLK, columns))
    return wide.reshape(fields, first * BLK, second * BLK, columns)


def block_fields(tissue, fiber):
    kind = fiber.astype(jnp.float32)
    polar = math.pi * (kind + 0.5) / CLASSES
    azimuth = 2.3 * kind
    along_x = jnp.cos(polar)
    along_y = jnp.sin(polar) * jnp.cos(azimuth)
    along_z = jnp.sin(polar) * jnp.sin(azimuth)
    spread = SIGMA_LONG - SIGMA_CROSS
    parts = [
        tissue.astype(jnp.float32),
        SIGMA_CROSS + spread * along_x * along_x,
        SIGMA_CROSS + spread * along_y * along_y,
        SIGMA_CROSS + spread * along_z * along_z,
        spread * along_x * along_y,
        spread * along_x * along_z,
        spread * along_y * along_z,
    ]
    wide = spread_blocks(jnp.stack(parts))
    return (wide[0], tuple((wide[k] for k in range(1, 7))))


def diffuse(padded, comps):
    centre = padded[1:-1, 1:-1, 1:-1]
    second_x = padded[2:, 1:-1, 1:-1] - 2.0 * centre + padded[:-2, 1:-1, 1:-1]
    second_y = padded[1:-1, 2:, 1:-1] - 2.0 * centre + padded[1:-1, :-2, 1:-1]
    second_z = padded[1:-1, 1:-1, 2:] - 2.0 * centre + padded[1:-1, 1:-1, :-2]
    cross_xy = 0.25 * (
        padded[2:, 2:, 1:-1]
        - padded[2:, :-2, 1:-1]
        - padded[:-2, 2:, 1:-1]
        + padded[:-2, :-2, 1:-1]
    )
    cross_xz = 0.25 * (
        padded[2:, 1:-1, 2:]
        - padded[2:, 1:-1, :-2]
        - padded[:-2, 1:-1, 2:]
        + padded[:-2, 1:-1, :-2]
    )
    cross_yz = 0.25 * (
        padded[1:-1, 2:, 2:]
        - padded[1:-1, 2:, :-2]
        - padded[1:-1, :-2, 2:]
        + padded[1:-1, :-2, :-2]
    )
    dxx, dyy, dzz, dxy, dxz, dyz = comps
    return (
        dxx * second_x
        + dyy * second_y
        + dzz * second_z
        + 2.0 * (dxy * cross_xy + dxz * cross_xz + dyz * cross_yz)
    )


def ionic(voltage, gates, calcium):
    fresh = []
    for k in range(6):
        steady = jax.nn.sigmoid(SLOPES[k] * (voltage - MIDDLES[k]))
        fresh.append(steady + (gates[k] - steady) * math.exp(-TIME_STEP * RATES[k]))
    current = (
        2.0 * fresh[0] * fresh[0] * fresh[0] * fresh[1] * (voltage - 1.2)
        + fresh[2] * fresh[2] * (voltage + 0.1)
        + 0.6 * fresh[3] * fresh[4] * (voltage - 0.9)
        + 0.2 * (1.0 + fresh[5]) * (voltage - 0.05)
    )
    volt_next = voltage - TIME_STEP * current
    calc_next = calcium + TIME_STEP * (1.5 * fresh[3] * fresh[4] * (1.0 - calcium) - 0.8 * calcium)
    return (volt_next, fresh, calc_next)


def emission(field, tissue_float, which):
    alpha = OPACITY[which] * tissue_float * jax.nn.sigmoid(6.0 * (field - 0.4))
    red = jax.nn.sigmoid(5.0 * (field - 0.5))
    green = jnp.exp(-6.0 * (field - 0.5) * (field - 0.5))
    return (alpha, (red, green, 1.0 - red))


def march(alpha, colours):
    through = jnp.cumprod(1.0 - alpha, axis=0)
    before = jnp.concatenate([jnp.ones_like(through[:1]), through[:-1]], axis=0)
    weight = before * alpha
    colour = jnp.stack([jnp.sum(weight * item, axis=0) for item in colours])
    return (colour, through[-1])


def composite(colour, through):
    return (colour, through)


def per_device(states, tissue, fiber):
    tissue_float, comps = block_fields(tissue, fiber)
    voltage = states[0]
    gates = [states[k] for k in range(1, 7)]
    calcium = states[7]
    pieces = []
    for step in range(STEPS):
        rimmed = padded_2(voltage * tissue_float, (("depth", 0), ("area", 1)), 1)
        padded = jnp.pad(rimmed, ((0, 0), (0, 0), (1, 1)))
        diffused = voltage + TIME_STEP * diffuse(padded, comps)
        volt_next, fresh, calc_next = ionic(diffused, gates, calcium)
        keep = 1.0 - tissue_float
        voltage = tissue_float * volt_next + keep * voltage
        gates = [tissue_float * item + keep * old for item, old in zip(fresh, gates)]
        calcium = tissue_float * calc_next + keep * calcium
        colours = []
        throughs = []
        for which, field in enumerate((voltage, calcium)):
            alpha, tints = emission(field, tissue_float, which)
            colour, through = march(alpha, tints)
            colours.append(colour)
            throughs.append(through[None])
        pieces.append(composite(jnp.stack(colours), jnp.stack(throughs)))
    colour_all = jnp.stack([item[0] for item in pieces])
    through_all = jnp.stack([item[1] for item in pieces])
    strip_colour, strip_through = side_by_side(
        (colour_all[None], through_all[None]), "depth", 5, 0, 3
    )
    passed = jnp.cumprod(strip_through, axis=0)
    before = jnp.concatenate([jnp.ones_like(passed[:1]), passed[:-1]], axis=0)
    colour_all = jnp.sum(before * strip_colour, axis=0)
    through_all = passed[-1]
    images = jnp.concatenate([colour_all, 1.0 - through_all], axis=2)
    final_states = jnp.stack([voltage] + gates + [calcium])
    return (final_states, images)


def solution(mesh):
    return jax.shard_map(
        per_device,
        mesh=mesh,
        in_specs=(
            P(None, "depth", "area", None),
            P("depth", "area", None),
            P("depth", "area", None),
        ),
        out_specs=(P(None, "depth", "area", None), P(None, None, None, "area", "depth")),
        check_vma=False,
    )
```

profile of v0, /device:TPU:97, one launch (start us, length us, event | category | flops | bytes accessed | tf_op | source)
XLA Modules:
  0.0 145.1 jit_solution(2516402242818971210)
XLA Ops:
  0.6 0.7 convert_element_type.10
  1.4 1.0 multiply_multiply_fusion.7
  3.8 1.2 bitcast_multiply_fusion.9
  5.0 1.3 collective-permute-start
  6.3 4.0 %collective-permute-start.1 = (f32[1,16,768]{2,1,0:T(8,128)S(1)}, f32[1,16,768]{2,1,0:T(8,128)S(1)}, u32[]{:S(2)}, u32[]{:S(2)}) collective-permute-start(f32[1,16,768]{2,1,0:T(8,128)S(1)} %get-tuple-element.44), channel_id=1, source_target_pairs={{0,16},{16,32},{32,48},{48,64},{64,80},{80,96},{96,112},{112,128},... | collective-permute-start | bytes 147464 | tf_op jit(solution)/shard_map/ppermute | solution.py:29
  10.4 1.1 collective-permute-done.1
  11.5 0.7 pad_maximum_fusion.12
  12.2 3.7 %collective-permute-start.2 = (f32[18,1,768]{2,1,0:T(1,128)}, f32[18,1,768]{2,1,0:T(1,128)S(1)}, u32[]{:S(2)}, u32[]{:S(2)}) collective-permute-start(f32[18,1,768]{2,1,0:T(1,128)} %get-tuple-element.41), channel_id=1, source_target_pairs={{1,0},{2,1},{3,2},{4,3},{5,4},{6,5},{7,6},{8,7},{9,8},{10,9},{11,1... | collective-permute-start | bytes 165896 | tf_op jit(solution)/shard_map/ppermute | solution.py:30
  15.9 4.7 %collective-permute-start.3 = (f32[18,1,768]{2,1,0:T(1,128)}, f32[18,1,768]{2,1,0:T(1,128)S(1)}, u32[]{:S(2)}, u32[]{:S(2)}) collective-permute-start(f32[18,1,768]{2,1,0:T(1,128)} %get-tuple-element.40), channel_id=1, source_target_pairs={{0,1},{1,2},{2,3},{3,4},{4,5},{5,6},{6,7},{7,8},{8,9},{9,10},{10,1... | collective-permute-start | bytes 165896 | tf_op jit(solution)/shard_map/ppermute | solution.py:29
  20.6 0.6 copy_bitcast_fusion.4
  21.8 1.2 broadcast_in_dim.51
  23.1 1.2 broadcast_in_dim.49
  24.4 1.2 broadcast_in_dim.47
  25.8 1.2 broadcast_in_dim.45
  27.1 1.2 broadcast_in_dim.43
  28.3 0.8 select_maximum_fusion.4
  30.1 6.6 %fusion.136 = (f32[16,16,768]{2,1,0:T(8,128)S(1)}, f32[16,16,768]{2,1,0:T(8,128)S(1)}, f32[16,16,768]{2,1,0:T(8,128)S(1)}, f32[16,16,768]{2,1,0:T(8,128)S(1)}, f32[16,16,768]{2,1,0:T(8,128)S(1)}) fusion(f32[16,16,768]{2,1,0:T(8,128)S(1)} %broadcast_in_dim.41, f32[8,16,16,768]{3,2,1,0:T(8,128)} %param.3, f32[16,16,768]{2,1,0:T(8,128)S(1)} %broadcast_in_dim.53, ...), kind=kLoop, calls=%fused_computation.284 | loop fusion | flops 21430272 | bytes 28409856 | tf_op jit(solution)/shard_map/mul | solution.py:152
  36.8 1.3 collective-permute-start.4
  38.1 4.6 %collective-permute-start.5 = (f32[1,16,768]{2,1,0:T(8,128)S(1)}, f32[1,16,768]{2,1,0:T(8,128)S(1)}, u32[]{:S(2)}, u32[]{:S(2)}) collective-permute-start(f32[1,16,768]{2,1,0:T(8,128)S(1)} %get-tuple-element.42), channel_id=1, source_target_pairs={{0,16},{16,32},{32,48},{48,64},{64,80},{80,96},{96,112},{112,128},... | collective-permute-start | bytes 147464 | tf_op jit(solution)/shard_map/ppermute | solution.py:29
  42.7 0.4 fusion.99
  43.1 0.7 collective-permute-done.5
  43.9 1.9 %collective-permute-start.6 = (f32[18,1,768]{2,1,0:T(1,128)S(1)}, f32[18,1,768]{2,1,0:T(1,128)S(1)}, u32[]{:S(2)}, u32[]{:S(2)}) collective-permute-start(f32[18,1,768]{2,1,0:T(1,128)S(1)} %get-tuple-element.37), channel_id=1, source_target_pairs={{1,0},{2,1},{3,2},{4,3},{5,4},{6,5},{7,6},{8,7},{9,8},{10,9},{11,1... | collective-permute-start | bytes 165896 | tf_op jit(solution)/shard_map/ppermute | solution.py:30
  45.8 5.0 %collective-permute-start.7 = (f32[18,1,768]{2,1,0:T(1,128)S(1)}, f32[18,1,768]{2,1,0:T(1,128)S(1)}, u32[]{:S(2)}, u32[]{:S(2)}) collective-permute-start(f32[18,1,768]{2,1,0:T(1,128)S(1)} %get-tuple-element.36), channel_id=1, source_target_pairs={{0,1},{1,2},{2,3},{3,4},{4,5},{5,6},{6,7},{7,8},{8,9},{9,10},{10,1... | collective-permute-start | bytes 165896 | tf_op jit(solution)/shard_map/ppermute | solution.py:29
  50.9 0.9 slice.397
  51.9 0.8 select_maximum_fusion
  53.0 0.9 copy-done.4
  53.9 7.2 %bitcast_dynamic-update-slice_fusion.7 = (f32[8,16,16,768]{3,2,1,0:T(8,128)}, f32[16,16,768]{2,1,0:T(8,128)}, f32[16,16,768]{2,1,0:T(8,128)S(1)}) fusion(f32[16,16,768]{2,1,0:T(8,128)S(1)} %get-tuple-element.30, f32[16,16,768]{2,1,0:T(8,128)S(1)} %broadcast_in_dim.41, f32[8,16,16,768]{3,2,1,0:T(8,128)S(1)} %bitcast.250, ...), kind=kLoop, calls=%fused_computation.138 | loop fusion | flops 31064064 | bytes 29196288
  61.1 1.5 %bitcast_dynamic-update-slice_fusion.6 = f32[8,16,16,768]{3,2,1,0:T(8,128)} fusion(f32[8,16,16,768]{3,2,1,0:T(8,128)} %get-tuple-element.26, f32[16,16,768]{2,1,0:T(8,128)S(1)} %broadcast_in_dim.41, f32[16,16,768]{2,1,0:T(8,128)S(1)} %get-tuple-element.28, f32[8,16,16,768]{3,2,1,0:T(8,128)S(1)} %bitcast.250, f32[16,16,768]{2,1,0:T(8,128)S(1)} %get-tuple-element.33), kind=kLoop, calls=%fused_computation.137 | loop fusion | flops 4521984 | bytes 3932160
  62.6 1.5 %bitcast_dynamic-update-slice_fusion.5 = f32[8,16,16,768]{3,2,1,0:T(8,128)} fusion(f32[8,16,16,768]{3,2,1,0:T(8,128)} %bitcast_dynamic-update-slice_fusion.6, f32[16,16,768]{2,1,0:T(8,128)S(1)} %broadcast_in_dim.41, f32[16,16,768]{2,1,0:T(8,128)S(1)} %get-tuple-element.28, f32[8,16,16,768]{3,2,1,0:T(8,128)S(1)} %bitcast.250, ...), kind=kLoop, calls=%fused_computation.136 | loop fusion | flops 4521984 | bytes 3932160
  64.1 1.5 %bitcast_dynamic-update-slice_fusion.4 = f32[8,16,16,768]{3,2,1,0:T(8,128)} fusion(f32[8,16,16,768]{3,2,1,0:T(8,128)} %bitcast_dynamic-update-slice_fusion.5, f32[16,16,768]{2,1,0:T(8,128)S(1)} %broadcast_in_dim.41, f32[16,16,768]{2,1,0:T(8,128)S(1)} %get-tuple-element.28, f32[8,16,16,768]{3,2,1,0:T(8,128)S(1)} %bitcast.250, ...), kind=kLoop, calls=%fused_computation.135 | loop fusion | flops 4521984 | bytes 3932160
  65.7 1.3 bitcast_dynamic-update-slice_fusion.3
  67.0 1.3 bitcast_dynamic-update-slice_fusion.2
  68.3 1.5 %bitcast_dynamic-update-slice_fusion.1 = f32[8,16,16,768]{3,2,1,0:T(8,128)} fusion(f32[8,16,16,768]{3,2,1,0:T(8,128)} %bitcast_dynamic-update-slice_fusion.2, f32[16,16,768]{2,1,0:T(8,128)S(1)} %broadcast_in_dim.41, f32[16,16,768]{2,1,0:T(8,128)S(1)} %get-tuple-element.28, f32[8,16,16,768]{3,2,1,0:T(8,128)S(1)} %bitcast.250, ...), kind=kLoop, calls=%fused_computation.132 | loop fusion | flops 4521984 | bytes 3932160
  69.8 2.1 %bitcast_dynamic-update-slice_fusion = (f32[8,16,16,768]{3,2,1,0:T(8,128)}, f32[16,16,768]{2,1,0:T(8,128)S(1)}, f32[16,16,768]{2,1,0:T(8,128)S(1)}) fusion(f32[8,16,16,768]{3,2,1,0:T(8,128)} %bitcast_dynamic-update-slice_fusion.1, f32[16,16,768]{2,1,0:T(8,128)S(1)} %broadcast_in_dim.41, f32[8,16,16,768]{3,2,1,0:T(8,128)S(1)} %bitcast.250, ...), kind=kLoop, calls=%fused_computation.122 | loop fusion | flops 8847360 | bytes 7864320 | tf_op jit(solution)/shard_map/stack | solution.py:178
  72.3 0.9 slice.400
  73.8 0.9 slice.399
  75.2 0.9 slice.398
  76.1 2.7 %copy.48 = f32[1,2,2,1,16,768]{4,3,2,1,0,5:T(1,128)} copy(f32[1,2,2,1,16,768]{5,4,2,1,3,0:T(8,128)S(1)} %maximum_bitcast_fusion.2) | data formatting | bytes 393216 | tf_op jit(solution)/shard_map/broadcast_in_dim | solution.py:171
  78.8 4.2 %multiply_reduce_fusion.7 = (f32[16,768]{1,0:T(8,128)S(1)}, f32[16,768]{1,0:T(8,128)S(1)}, f32[16,768]{1,0:T(8,128)S(1)}, f32[16,768]{1,0:T(8,128)S(1)}, f32[16,...) fusion(f32[16,16,768]{2,1,0:T(8,128)S(1)} %get-tuple-element.30, ...), kind=kLoop, calls=%fused_computation.193 | loop fusion | flops 16760832 | bytes 7471104 | tf_op jit(solution)/shard_map/reduce_sum | solution.py:137
  83.2 4.7 %copy.47 = f32[2,2,3,16,768]{3,2,1,0,4:T(4,128)} copy(f32[2,2,3,16,768]{4,3,2,1,0:T(8,128)S(1)} %pad_maximum_fusion.7) | data formatting | bytes 1179648 | tf_op jit(solution)/shard_map/stack | solution.py:168
  87.9 8.9 %fusion.144 = f32[768,1,2,2,4,16]{5,4,3,2,1,0:T(4,128)} fusion(f32[1,2,2,1,16,768]{4,3,2,1,0,5:T(1,128)S(1)} %copy-done.7, f32[1,2,2,3,16,768]{4,3,2,1,0,5:T(4,128)} %bitcast.251), kind=kLoop, calls=%fused_computation.288 | loop fusion | flops 196608 | bytes 1572864
  96.8 6.5 %reshape.97 = f32[16,1,12288]{2,1,0:T(1,128)S(1)} reshape(f32[768,1,2,2,4,16]{5,4,3,2,1,0:T(4,128)} %fusion.144) | data formatting | bytes 1572864
  103.3 24.8 %all_to_all.18 = f32[16,1,12288]{2,1,0:T(1,128)S(1)} all-to-all(f32[16,1,12288]{2,1,0:T(1,128)S(1)} %reshape.97), channel_id=1, replica_groups=mesh['depth'=16,'area'=16] {'depth'}, dimensions={0} | all-to-all | bytes 1572864 | tf_op jit(solution)/shard_map/all_to_all | solution.py:38
  128.1 0.5 broadcast.844
  128.6 2.5 %reduce = f32[16,12288]{1,0:T(8,128)S(1)} reduce(f32[16,1,12288]{2,1,0:T(1,128)S(1)} %all_to_all.18, f32[]{:T(128)} %broadcast.844), dimensions={1}, to_apply=%all_to_all.13.reduce_sub_computation | reduce | bytes 1572868 | tf_op jit(solution)/shard_map/all_to_all | solution.py:38
  131.1 6.1 %reshape.98 = f32[768,1,2,2,4,16]{5,4,3,2,1,0:T(4,128)} reshape(f32[16,12288]{1,0:T(8,128)S(1)} %reduce) | data formatting | bytes 1572864
  137.3 6.1 %copy.54 = f32[1,2,2,4,16,16,48]{6,5,4,3,2,1,0:T(8,128)S(1)} copy(f32[1,2,2,4,16,16,48]{4,3,2,1,6,5,0:T(4,128)} %bitcast.252) | data formatting | bytes 1572864 | tf_op jit(solution)/shard_map/all_to_all | solution.py:38
  144.4 0.7 pad_maximum_fusion.8
  (80 shorter events, 6.5 us)
Async XLA Ops:
  5.0 5.4 %collective-permute-start = (f32[1,16,768]{2,1,0:T(8,128)S(1)}, f32[1,16,768]{2,1,0:T(8,128)S(1)}, u32[]{:S(2)}, u32[]{:S(2)}) collective-permute-start(f32[1,16,768]{2,1,0:T(8,128)S(1)} %get-tuple-element.45), channel_id=1, source_target_pairs={{16,0},{32,16},{48,32},{64,48},{80,64},{96,80},{112,96},{128,112},... | collective-permute-start | bytes 147464 | tf_op jit(solution)/shard_map/ppermute | solution.py:30
  6.3 5.2 %collective-permute-start.1 = (f32[1,16,768]{2,1,0:T(8,128)S(1)}, f32[1,16,768]{2,1,0:T(8,128)S(1)}, u32[]{:S(2)}, u32[]{:S(2)}) collective-permute-start(f32[1,16,768]{2,1,0:T(8,128)S(1)} %get-tuple-element.44), channel_id=1, source_target_pairs={{0,16},{16,32},{32,48},{48,64},{64,80},{80,96},{96,112},{112,128},... | collective-permute-start | bytes 147464 | tf_op jit(solution)/shard_map/ppermute | solution.py:29
  12.2 16.1 %collective-permute-start.2 = (f32[18,1,768]{2,1,0:T(1,128)}, f32[18,1,768]{2,1,0:T(1,128)S(1)}, u32[]{:S(2)}, u32[]{:S(2)}) collective-permute-start(f32[18,1,768]{2,1,0:T(1,128)} %get-tuple-element.41), channel_id=1, source_target_pairs={{1,0},{2,1},{3,2},{4,3},{5,4},{6,5},{7,6},{8,7},{9,8},{10,9},{11,1... | collective-permute-start | bytes 165896 | tf_op jit(solution)/shard_map/ppermute | solution.py:30
  15.9 12.3 %collective-permute-start.3 = (f32[18,1,768]{2,1,0:T(1,128)}, f32[18,1,768]{2,1,0:T(1,128)S(1)}, u32[]{:S(2)}, u32[]{:S(2)}) collective-permute-start(f32[18,1,768]{2,1,0:T(1,128)} %get-tuple-element.40), channel_id=1, source_target_pairs={{0,1},{1,2},{2,3},{3,4},{4,5},{5,6},{6,7},{7,8},{8,9},{9,10},{10,1... | collective-permute-start | bytes 165896 | tf_op jit(solution)/shard_map/ppermute | solution.py:29
  24.3 1.3 copy-start.8
  28.3 1.1 copy-start
  28.3 1.4 copy-start.1
  28.3 1.6 %copy-start.2 = (f32[16,16,768]{2,1,0:T(8,128)S(1)}, f32[16,16,768]{2,1,0:T(8,128)}, u32[]{:S(2)}) copy-start(f32[16,16,768]{2,1,0:T(8,128)} %broadcast_in_dim.47) | copy-start | bytes 2359300
  28.3 1.8 %copy-start.3 = (f32[16,16,768]{2,1,0:T(8,128)S(1)}, f32[16,16,768]{2,1,0:T(8,128)}, u32[]{:S(2)}) copy-start(f32[16,16,768]{2,1,0:T(8,128)} %broadcast_in_dim.45) | copy-start | bytes 2359300
  29.1 23.8 %slice-start = ((s8[6291456]{0:T(1024)(128)(4,1)}), s8[4194304]{0:T(1024)(128)(4,1)S(1)}, s32[]{:S(2)}) async-start(s8[6291456]{0:T(1024)(128)(4,1)} %bitcast.249), calls=%async_computation.1 | async-start | bytes 8388608
  30.1 22.8 %slice-start.1 = ((s8[6291456]{0:T(1024)(128)(4,1)}), s8[2097152]{0:T(1024)(128)(4,1)S(1)}, s32[]{:S(2)}) async-start(s8[6291456]{0:T(1024)(128)(4,1)} %bitcast.249), calls=%async_computation.2 | async-start | bytes 4194304
  36.8 6.3 %collective-permute-start.4 = (f32[1,16,768]{2,1,0:T(8,128)S(1)}, f32[1,16,768]{2,1,0:T(8,128)S(1)}, u32[]{:S(2)}, u32[]{:S(2)}) collective-permute-start(f32[1,16,768]{2,1,0:T(8,128)S(1)} %get-tuple-element.43), channel_id=1, source_target_pairs={{16,0},{32,16},{48,32},{64,48},{80,64},{96,80},{112,96},{128,112},... | collective-permute-start | bytes 147464 | tf_op jit(solution)/shard_map/ppermute | solution.py:30
  38.1 5.8 %collective-permute-start.5 = (f32[1,16,768]{2,1,0:T(8,128)S(1)}, f32[1,16,768]{2,1,0:T(8,128)S(1)}, u32[]{:S(2)}, u32[]{:S(2)}) collective-permute-start(f32[1,16,768]{2,1,0:T(8,128)S(1)} %get-tuple-element.42), channel_id=1, source_target_pairs={{0,16},{16,32},{32,48},{48,64},{64,80},{80,96},{96,112},{112,128},... | collective-permute-start | bytes 147464 | tf_op jit(solution)/shard_map/ppermute | solution.py:29
  43.9 7.9 %collective-permute-start.6 = (f32[18,1,768]{2,1,0:T(1,128)S(1)}, f32[18,1,768]{2,1,0:T(1,128)S(1)}, u32[]{:S(2)}, u32[]{:S(2)}) collective-permute-start(f32[18,1,768]{2,1,0:T(1,128)S(1)} %get-tuple-element.37), channel_id=1, source_target_pairs={{1,0},{2,1},{3,2},{4,3},{5,4},{6,5},{7,6},{8,7},{9,8},{10,9},{11,1... | collective-permute-start | bytes 165896 | tf_op jit(solution)/shard_map/ppermute | solution.py:30
  45.8 6.1 %collective-permute-start.7 = (f32[18,1,768]{2,1,0:T(1,128)S(1)}, f32[18,1,768]{2,1,0:T(1,128)S(1)}, u32[]{:S(2)}, u32[]{:S(2)}) collective-permute-start(f32[18,1,768]{2,1,0:T(1,128)S(1)} %get-tuple-element.36), channel_id=1, source_target_pairs={{0,1},{1,2},{2,3},{3,4},{4,5},{5,6},{6,7},{7,8},{8,9},{9,10},{10,1... | collective-permute-start | bytes 165896 | tf_op jit(solution)/shard_map/ppermute | solution.py:29
  52.7 1.1 copy-start.4
  71.9 2.8 %copy-start.6 = (f32[16,16,768]{2,1,0:T(8,128)}, f32[16,16,768]{2,1,0:T(8,128)S(1)}, u32[]{:S(2)}) copy-start(f32[16,16,768]{2,1,0:T(8,128)S(1)} %get-tuple-element.25) | copy-start | bytes 2359300
  71.9 1.5 %copy-start.5 = (f32[16,16,768]{2,1,0:T(8,128)S(1)}, f32[16,16,768]{2,1,0:T(8,128)}, u32[]{:S(2)}) copy-start(f32[16,16,768]{2,1,0:T(8,128)} %get-tuple-element.27) | copy-start | bytes 2359300
  83.2 4.7 %copy-start.7 = (f32[1,2,2,1,16,768]{4,3,2,1,0,5:T(1,128)S(1)}, f32[1,2,2,1,16,768]{4,3,2,1,0,5:T(1,128)}, u32[]{:S(2)}) copy-start(f32[1,2,2,1,16,768]{4,3,2,1,0,5:T(1,128)} %copy.48) | copy-start | bytes 589828
where the time goes:
time: 146 us; the launch traced here: 145 us
  other arithmetic  49.1 us (34%)
  local copies, waits for them, and re-layouts  41.1 us (28%)
  starting transfers between devices  26.5 us (18%)
  blocking collectives  24.8 us (17%)
  waiting for transfers between devices  1.88 us (1%)
    unnamed x9, other arithmetic  24.8 us
    all_to_all x1, blocking collectives, side_by_side(): lax.all_to_all(both, axis, split_axis=split_dim, concat_axis=concat_dim,...  24.8 us
    ppermute x4, starting transfers between devices, padded_2(): before = lax.ppermute(last, axis, up)  18.3 us
    unnamed x28, local copies, waits for them, and re-layouts  15.1 us
    ppermute x4, starting transfers between devices, padded_2(): after = lax.ppermute(leading, axis, down)  8.21 us
    mul x2, other arithmetic, per_device(): rimmed = padded_2(voltage * tissue_float, (('depth', 0), ('area', 1)), 1)  7.85 us
    broadcast_in_dim x14, local copies, waits for them, and re-layouts, spread_blocks(): wide = jnp.broadcast_to(along, (fields, first, BLK, second, BLK, columns))  7.39 us
    all_to_all x2, local copies, waits for them, and re-layouts, side_by_side(): lax.all_to_all(both, axis, split_axis=split_dim, concat_axis=concat_dim,...  6.58 us
  transfers between devices with their start and end apart: 8, of which 3 were waited for; matrix products, arithmetic and copies ran while one was open for 6% of the time, Pallas kernels for 0%

commit v1 on v0

v1 whole, which is shorter than its diff:
```python
import math

import jax
import jax.numpy as jnp
from jax import lax
from jax.experimental import pallas as pl
from jax.experimental.pallas import tpu as pltpu
from jax.sharding import PartitionSpec as P

BLK = 4
CLASSES = 8
NX = 16
NY = 16
NZ = 768
STRIP = 48
HALF = STRIP // 2
PLANES = 4
CHUNK = 128

TIME_STEP = 0.15
SIGMA_LONG = 1.0
SIGMA_CROSS = 0.3
SLOPES = (8.0, -8.0, 6.0, 5.0, -5.0, -3.0)
MIDDLES = (0.2, 0.4, 0.3, 0.5, 0.6, 0.5)
RATES = (3.0, 0.5, 1.0, 0.8, 0.3, 0.1)
OPACITY = (0.012, 0.01)

f32 = jnp.float32
HIGHEST = lax.Precision.HIGHEST


def params(mib):
    return pltpu.CompilerParams(vmem_limit_bytes=mib * 2**20)


def is_even(axis):
    return lax.rem(lax.axis_index(axis), 2) == 0


def lane_spread(count):
    row = lax.broadcasted_iota(jnp.int32, (count, count * BLK), 0)
    column = lax.broadcasted_iota(jnp.int32, (count, count * BLK), 1)
    return row == lax.shift_right_logical(column, 2)


def row_spread(blocks):
    row = lax.broadcasted_iota(jnp.int32, (64, 16), 0)
    column = lax.broadcasted_iota(jnp.int32, (64, 16), 1)
    return jnp.dot((lax.shift_right_logical(row, 2) == column).astype(f32), blocks,
                   precision=HIGHEST, preferred_element_type=f32)


def faces_kernel(tissue_ref, v_ref, ev_ref, od_ref, row_lo_ref, row_hi_ref):
    tissue = tissue_ref[...].astype(f32)
    wide = jnp.dot(tissue.astype(jnp.bfloat16), lane_spread(NZ // BLK).astype(jnp.bfloat16),
                   preferred_element_type=f32)
    even = is_even("depth")
    row = lax.broadcasted_iota(jnp.int32, (NY, 1), 0)

    def mask_of(block):
        out = jnp.broadcast_to(wide[4 * block:4 * block + 1], (NY, NZ))
        for k in range(1, 4):
            out = jnp.where(row >= 4 * k, wide[4 * block + k:4 * block + k + 1], out)
        return out

    low = v_ref[0, 0] * mask_of(0)
    high = v_ref[0, NX - 1] * mask_of(3)
    ev_ref[...] = jnp.where(even, high, low)
    od_ref[...] = jnp.where(even, low, high)
    for x in range(NX):
        block = x // BLK
        row_lo_ref[x:x + 1] = v_ref[0, x, 0:1] * wide[4 * block:4 * block + 1]
        row_hi_ref[x:x + 1] = v_ref[0, x, NY - 1:NY] * wide[4 * block + 3:4 * block + 4]


def coefs_kernel(tissue_ref, fiber_ref, out_ref):
    kind = fiber_ref[...].astype(f32)
    polar = math.pi * (kind + 0.5) / CLASSES
    azimuth = 2.3 * kind
    along_x = jnp.cos(polar)
    ring = jnp.sin(polar)
    along_y = ring * jnp.cos(azimuth)
    along_z = ring * jnp.sin(azimuth)
    spread = SIGMA_LONG - SIGMA_CROSS
    t = TIME_STEP
    parts = (
        tissue_ref[...].astype(f32),
        t * (SIGMA_CROSS + spread * along_x * along_x),
        t * (SIGMA_CROSS + spread * along_y * along_y),
        t * (SIGMA_CROSS + spread * along_z * along_z),
        (0.5 * t) * (spread * along_x * along_y),
        (0.5 * t) * (spread * along_x * along_z),
        (0.5 * t) * (spread * along_y * along_z),
    )
    onehot = lane_spread(NZ // BLK).astype(f32)
    for k, part in enumerate(parts):
        out_ref[k] = jnp.dot(row_spread(part), onehot, precision=HIGHEST, preferred_element_type=f32)


def message_kernel(rcv_ev_ref, rcv_od_ref, row_lo_ref, row_hi_ref, ev_ref, od_ref):
    depth_even = is_even("depth")
    area_even = is_even("area")

    def pick(flag, a, b):
        return jnp.where(flag, a, b)

    lo = row_lo_ref[...]
    hi = row_hi_ref[...]
    ev_ref[0:NX] = pick(area_even, hi, lo)
    od_ref[0:NX] = pick(area_even, lo, hi)
    for place, first, second in ((NX, rcv_od_ref, rcv_ev_ref), (NX + 1, rcv_ev_ref, rcv_od_ref)):
        low = pick(depth_even, first[0:1], second[0:1])
        high = pick(depth_even, first[NY - 1:NY], second[NY - 1:NY])
        ev_ref[place:place + 1] = pick(area_even, high, low)
        od_ref[place:place + 1] = pick(area_even, low, high)


def z_sides(u):
    lane = lax.broadcasted_iota(jnp.int32, (1, NZ), 1)
    after = jnp.where(lane == NZ - 1, 0.0, pltpu.roll(u, NZ - 1, axis=1))
    before = jnp.where(lane == 0, 0.0, pltpu.roll(u, 1, axis=1))
    return after, before


def y_sides(u, row_lo, row_hi):
    row = lax.broadcasted_iota(jnp.int32, (NY, 1), 0)
    after = jnp.where(row == NY - 1, row_hi, pltpu.roll(u, NY - 1, axis=0))
    before = jnp.where(row == 0, row_lo, pltpu.roll(u, 1, axis=0))
    return after, before


def derive(v_ref, coefs_ref, depth_refs, area_refs, u_s, uy_s, uz_s, w_s, lo_s, hi_s, loz_s, hiz_s):
    depth_even = is_even("depth")
    area_even = is_even("area")
    lo_s[0:18] = jnp.where(area_even, area_refs[1][...], area_refs[0][...])
    hi_s[0:18] = jnp.where(area_even, area_refs[0][...], area_refs[1][...])
    for source, target in ((lo_s, loz_s), (hi_s, hiz_s)):
        after, before = z_sides(source[...])
        target[...] = after - before
    for place, where, flip in ((NX, 0, 1), (NX + 1, NX + 1, 0)):
        u = jnp.where(depth_even, depth_refs[flip][...], depth_refs[1 - flip][...])
        after, before = z_sides(u)
        uz_s[where] = after - before
        after, before = y_sides(u, lo_s[place:place + 1], hi_s[place:place + 1])
        uy_s[where] = after - before
        u_s[where] = u

    def plane(x, carry):
        rows = pl.ds(pl.multiple_of(lax.shift_right_logical(x, 2) * NY, NY), NY)
        u = v_ref[0, x] * coefs_ref[0, rows]
        u_s[x + 1] = u
        after, before = z_sides(u)
        uz = after - before
        uz_s[x + 1] = uz
        w = 0.52 * u + coefs_ref[3, rows] * (after + before)
        after, before = y_sides(u, lo_s[pl.ds(x, 1)], hi_s[pl.ds(x, 1)])
        uy_s[x + 1] = after - before
        w = w + coefs_ref[2, rows] * (after + before)
        after, before = y_sides(uz, loz_s[pl.ds(x, 1)], hiz_s[pl.ds(x, 1)])
        w_s[x] = w + coefs_ref[6, rows] * (after - before)
        return carry

    lax.fori_loop(0, NX, plane, 0)


def ionic(w, gates, calcium):
    fresh = []
    for k in range(6):
        keep = math.exp(-TIME_STEP * RATES[k])
        half = 0.5 * (1.0 - keep)
        t = jnp.tanh((0.5 * SLOPES[k]) * w - (0.5 * SLOPES[k] * MIDDLES[k]))
        fresh.append(half * t + (keep * gates[k] + half))
    both = fresh[3] * fresh[4]
    cube = fresh[0] * fresh[0] * fresh[0]
    loss = (
        (2.0 * TIME_STEP) * (cube * fresh[1]) * (w - 1.2)
        + TIME_STEP * (fresh[2] * fresh[2]) * (w + 0.1)
        + (0.6 * TIME_STEP) * both * (w - 0.9)
        + (0.2 * TIME_STEP) * (1.0 + fresh[5]) * (w - 0.05)
    )
    gain = (1.5 * TIME_STEP) * both
    calc_next = (1.0 - 0.8 * TIME_STEP) * calcium + gain * (1.0 - calcium)
    return w - loss, fresh, calc_next


def march(q, opaque, state):
    passed, red, green = state
    alpha = opaque * jnp.tanh(3.0 * q - 1.2) + opaque
    weight = passed * alpha
    off = q - 0.5
    red = red + weight * jnp.tanh(2.5 * off)
    green = green + weight * jnp.exp(-6.0 * (off * off))
    return passed - weight, red, green


def step_body(last, refs):
    (states_ref, v_ref, coefs_ref, dev_ref, dod_ref, aev_ref, aod_ref) = refs[:7]
    if last:
        earlier_ref, out_ref, strips_ref = refs[7:10]
        scratch = refs[10:]
    else:
        out_ref, shown_ref, ev_ref, od_ref, row_lo_ref, row_hi_ref = refs[7:13]
        scratch = refs[13:]
    u_s, uy_s, uz_s, w_s, lo_s, hi_s, loz_s, hiz_s, acc_s = scratch
    i = pl.program_id(0)

    @pl.when(i == 0)
    def _():
        derive(v_ref, coefs_ref, (dev_ref, dod_ref), (aev_ref, aod_ref),
               u_s, uy_s, uz_s, w_s, lo_s, hi_s, loz_s, hiz_s)
        for k in range(6):
            acc_s[k] = jnp.full((NY, NZ), 1.0 if k % 3 == 0 else 0.0, f32)

    rows = pl.ds(pl.multiple_of(i * NY, NY), NY)

    def chunk(j, carry):
        cols = pl.ds(pl.multiple_of(j * CHUNK, CHUNK), CHUNK)
        m = coefs_ref[0, rows, cols]
        inside = m > 0.5
        opaque = (0.5 * OPACITY[0] * m, 0.5 * OPACITY[1] * m)
        cxx = coefs_ref[1, rows, cols]
        cxy = coefs_ref[4, rows, cols]
        cxz = coefs_ref[5, rows, cols]
        marches = [tuple(acc_s[3 * f + k, :, cols] for k in range(3)) for f in range(2)]
        for p in range(PLANES):
            x = i * PLANES + p
            w = (
                w_s[x, :, cols]
                + cxx * (u_s[x + 2, :, cols] + u_s[x, :, cols])
                + cxy * (uy_s[x + 2, :, cols] - uy_s[x, :, cols])
                + cxz * (uz_s[x + 2, :, cols] - uz_s[x, :, cols])
            )
            old = [states_ref[k, p, :, cols] for k in range(8)]
            volt, fresh, calc = ionic(w, old[1:7], old[7])
            new = [jnp.where(inside, a, b) for a, b in zip([volt] + fresh + [calc], old)]
            for k in range(8):
                out_ref[k, p, :, cols] = new[k]
            marches = [march(q, o, s) for q, o, s in zip((new[0], new[7]), opaque, marches)]
        for f in range(2):
            for k in range(3):
                acc_s[3 * f + k, :, cols] = marches[f][k]
        return carry

    lax.fori_loop(0, NZ // CHUNK, chunk, 0)

    if not last:
        even = is_even("depth")
        for block in range(NX // PLANES):
            @pl.when(i == block)
            def _():
                for p in range(PLANES):
                    x = block * PLANES + p
                    first, final = block * NY, block * NY + NY - 1
                    row_lo_ref[x:x + 1] = out_ref[0, p, 0:1] * coefs_ref[0, first:first + 1]
                    row_hi_ref[x:x + 1] = out_ref[0, p, NY - 1:NY] * coefs_ref[0, final:final + 1]

        @pl.when(i == 0)
        def _():
            u = out_ref[0, 0] * coefs_ref[0, 0:NY]
            ev_ref[...] = jnp.where(even, ev_ref[...], u)
            od_ref[...] = jnp.where(even, u, od_ref[...])

        @pl.when(i == NX // PLANES - 1)
        def _():
            u = out_ref[0, PLANES - 1] * coefs_ref[0, 3 * NY:4 * NY]
            ev_ref[...] = jnp.where(even, u, ev_ref[...])
            od_ref[...] = jnp.where(even, od_ref[...], u)
            shown_ref[...] = acc_s[...]
    else:
        @pl.when(i == NX // PLANES - 1)
        def _():
            for k in range(3):
                stack = jnp.concatenate(
                    [earlier_ref[k], earlier_ref[3 + k], acc_s[k], acc_s[3 + k]], axis=0)
                stack = jnp.concatenate([stack, pltpu.roll(stack, NZ - HALF, axis=1)], axis=0)
                turned = stack.T
                for d in range(NZ // STRIP):
                    strips_ref[d, HALF * k:HALF * (k + 1)] = turned[STRIP * d:STRIP * d + HALF]


def composite_kernel(strips_ref, out_ref):
    count = strips_ref.shape[0]
    passed = jnp.ones((HALF, 128), f32)
    red = jnp.zeros((HALF, 128), f32)
    green = jnp.zeros((HALF, 128), f32)
    for s in range(count):
        red = red + passed * strips_ref[s, HALF:2 * HALF]
        green = green + passed * strips_ref[s, 2 * HALF:3 * HALF]
        passed = passed * strips_ref[s, 0:HALF]
    solid = 1.0 - passed
    red = 0.5 * (solid + red)
    whole = jnp.concatenate([red, green, solid - red, solid, jnp.zeros((32, 128), f32)], axis=0)
    turned = whole.T
    first, second = turned[0:64], turned[64:128]
    lane = lax.broadcasted_iota(jnp.int32, (1, 128), 1)
    for c in range(4):
        a = pltpu.roll(first, (128 - HALF * c) % 128, axis=1) if c else first
        b = pltpu.roll(second, (128 + HALF - HALF * c) % 128, axis=1) if c != 1 else second
        o = jnp.where(lane < HALF, a, b)
        for k in range(4):
            out_ref[k // 2, k % 2, c] = o[NY * k:NY * (k + 1), 0:STRIP]


def full(shape):
    return pl.BlockSpec(shape, lambda i: (0,) * len(shape))


def run_step(last, states, coefs, depth, area, earlier=None):
    block = pl.BlockSpec((8, PLANES, NY, NZ), lambda i: (0, i, 0, 0))
    in_specs = [block, full((1, NX, NY, NZ)), full((7, 64, NZ)), full((NY, NZ)), full((NY, NZ)),
                full((18, NZ)), full((18, NZ))]
    args = [states, states, coefs, *depth, *area]
    out_specs = [block]
    out_shape = [jax.ShapeDtypeStruct((8, NX, NY, NZ), f32)]
    if last:
        in_specs.append(full((6, NY, NZ)))
        args.append(earlier)
        shapes = [(NZ // STRIP, 3 * HALF, 128)]
    else:
        shapes = [(6, NY, NZ)] + [(NY, NZ)] * 4
    out_specs += [full(s) for s in shapes]
    out_shape += [jax.ShapeDtypeStruct(s, f32) for s in shapes]
    scratch = [pltpu.VMEM((NX + 2, NY, NZ), f32)] * 3 + [pltpu.VMEM((NX, NY, NZ), f32)]
    scratch += [pltpu.VMEM((24, NZ), f32)] * 4 + [pltpu.VMEM((6, NY, NZ), f32)]
    return pl.pallas_call(
        lambda *refs: step_body(last, refs),
        grid=(NX // PLANES,),
        in_specs=in_specs,
        out_specs=out_specs,
        out_shape=out_shape,
        scratch_shapes=scratch,
        compiler_params=params(24),
        name="step_last" if last else "step_first",
    )(*args)


def swaps(axis):
    count = lax.axis_size(axis)
    even = [(i, i ^ 1) for i in range(count) if i ^ 1 < count]
    odd = [(i, ((i - 1) ^ 1) + 1) for i in range(1, count) if ((i - 1) ^ 1) + 1 < count]
    return even, odd


def exchange(axis, pair):
    even, odd = swaps(axis)
    return lax.ppermute(pair[0], axis, even), lax.ppermute(pair[1], axis, odd)


def halos(pair, row_lo, row_hi):
    depth = exchange("depth", pair)
    messages = pl.pallas_call(
        message_kernel,
        out_shape=[jax.ShapeDtypeStruct((18, NZ), f32)] * 2,
        compiler_params=params(1),
        name="area_message",
    )(*depth, row_lo, row_hi)
    return depth, exchange("area", messages)


def per_device(states, tissue, fiber):
    tissue = tissue.reshape(16, NZ // BLK)
    fiber = fiber.reshape(16, NZ // BLK)
    plane = jax.ShapeDtypeStruct((NY, NZ), f32)
    ev, od, row_lo, row_hi = pl.pallas_call(
        faces_kernel,
        grid=(1,),
        in_specs=[full((16, NZ // BLK)), full((1, NX, NY, NZ))],
        out_specs=[full((NY, NZ))] * 4,
        out_shape=[plane] * 4,
        compiler_params=params(4),
        name="faces",
    )(tissue, states)
    depth, area = halos((ev, od), row_lo, row_hi)
    coefs = pl.pallas_call(
        coefs_kernel,
        out_shape=jax.ShapeDtypeStruct((7, 64, NZ), f32),
        compiler_params=params(8),
        name="coefficients",
    )(tissue, fiber)
    states, shown, ev, od, row_lo, row_hi = run_step(False, states, coefs, depth, area)
    depth, area = halos((ev, od), row_lo, row_hi)
    states, strips = run_step(True, states, coefs, depth, area, shown)
    strips = lax.all_to_all(strips, "depth", split_axis=0, concat_axis=0, tiled=True)
    images = pl.pallas_call(
        composite_kernel,
        out_shape=jax.ShapeDtypeStruct((2, 2, 4, NY, STRIP), f32),
        compiler_params=params(4),
        name="composite",
    )(strips)
    return states, images


def solution(mesh):
    return jax.shard_map(
        per_device,
        mesh=mesh,
        in_specs=(
            P(None, "depth", "area", None),
            P("depth", "area", None),
            P("depth", "area", None),
        ),
        out_specs=(P(None, "depth", "area", None), P(None, None, None, "area", "depth")),
        check_vma=False,
    )
```

time: 146 us -> 72.8 us (0.50)
  other arithmetic: 49.1 us -> 0 us
  local copies, waits for them, and re-layouts: 41.1 us -> 6.31 us
  Pallas kernels: 0 us -> 18.2 us
  starting transfers between devices: 26.5 us -> 18.1 us
  waiting for transfers between devices: 1.88 us -> 3.91 us
    unnamed x9 -> x0, other arithmetic: 24.8 us -> none
    pallas_call x0 -> x7, Pallas kernels: none -> 18.2 us  [the longest x2 14.4 us: run_step(): pl.pallas_call(lambda *refs: step_body(last, refs), grid=(NX // PLANES,),...]
    broadcast_in_dim x15 -> x0, local copies, waits for them, and re-layouts: 10.1 us -> none  [the longest x14 7.39 us: spread_blocks(): wide = jnp.broadcast_to(along, (fields, first, BLK, second, BLK, columns))]
    unnamed x28 -> x6, local copies, waits for them, and re-layouts: 15.1 us -> 5.57 us
    mul x3 -> x0, other arithmetic: 8.83 us -> none  [the longest x2 7.85 us: per_device(): rimmed = padded_2(voltage * tissue_float, (('depth', 0), ('area', 1)), 1)]
    ppermute x8, starting transfers between devices: 26.5 us -> 18.1 us  [exchange(): return (lax.ppermute(pair[0], axis, even), lax.ppermute(pair[1], axis, odd))]
    all_to_all x2 -> x0, local copies, waits for them, and re-layouts: 6.58 us -> none  [side_by_side(): lax.all_to_all(both, axis, split_axis=split_dim, concat_axis=concat_dim,...]
    another operation x13 -> x0, local copies, waits for them, and re-layouts: 5.01 us -> none  [the longest x1 4.69 us: per_device(): colour_all = jnp.stack([item[0] for item in pieces])]
  transfers between devices with their start and end apart: 8 -> 8, of which waited for: 3 -> 3; matrix products, arithmetic and copies ran while one was open for 6% -> 0% of each run, Pallas kernels for 0% -> 4%
where the time goes in v1:
time: 72.8 us; the launch traced here: 72.5 us
  blocking collectives  25.2 us (35%)
  Pallas kernels  18.2 us (25%)
  starting transfers between devices  18.1 us (25%)
  local copies, waits for them, and re-layouts  6.31 us (9%)
  waiting for transfers between devices  3.91 us (5%)
  between operations  0.77 us (1%)
    all_to_all x1, blocking collectives, per_device(): lax.all_to_all(strips, 'depth', split_axis=0, concat_axis=0, tiled=True)  25.2 us
    ppermute x8, starting transfers between devices, exchange(): return (lax.ppermute(pair[0], axis, even), lax.ppermute(pair[1], axis, odd))  18.1 us
    pallas_call x2, Pallas kernels, run_step(): pl.pallas_call(lambda *refs: step_body(last, refs), grid=(NX // PLANES,),...  14.4 us
    unnamed x6, local copies, waits for them, and re-layouts  5.57 us
    ppermute x8, waiting for transfers between devices, exchange(): return (lax.ppermute(pair[0], axis, even), lax.ppermute(pair[1], axis, odd))  3.91 us
    pallas_call x1, Pallas kernels, per_device(): pl.pallas_call(coefs_kernel, out_shape=jax.ShapeDtypeStruct((7, 64, NZ),...  2.69 us
  transfers between devices with their start and end apart: 8, of which 3 were waited for; matrix products, arithmetic and copies ran while one was open for 0% of the time, Pallas kernels for 4%

profile of v1, /device:TPU:97, one launch (start us, length us, event | category | flops | bytes accessed | tf_op | source)
XLA Modules:
  0.0 72.5 jit_solution(25317228582686259)
XLA Ops:
  0.6 0.0 copy-start.2
  0.6 0.7 %reshape.10.tissue_ref = s32[16,192]{1,0:T(8,128)S(1)} reshape(s32[4,4,192]{2,1,0:T(4,128)} %param.4) | data formatting | bytes 24576 | tf_op jit(solution)/shard_map/reshape | solution.py:361
  1.4 0.0 copy-start
  1.4 2.8 %copy-done = f32[8,16,16,768]{3,2,1,0:T(8,128)S(1)} copy-done((f32[8,16,16,768]{3,2,1,0:T(8,128)S(1)}, f32[8,16,16,768]{3,2,1,0:T(8,128)}, u32[]{:S(2)}) %copy-start) | copy-done | bytes 6291480
  4.2 0.2 faces.1
  4.3 1.3 %collective-permute-start = (f32[16,768]{1,0:T(8,128)S(1)}, f32[16,768]{1,0:T(8,128)S(1)}, u32[]{:S(2)}, u32[]{:S(2)}) collective-permute-start(f32[16,768]{1,0:T(8,128)S(1)} %get-tuple-element.18), channel_id=1, source_target_pairs={{0,16},{16,0},{32,48},{48,32},{64,80},{80,64},{96,112},{112,96},{1... | collective-permute-start | bytes 147464 | tf_op jit(solution)/shard_map/ppermute | solution.py:346
  5.6 0.7 collective-permute-start.1
  6.3 1.1 %collective-permute-done.rcv_ev_ref.refs_3_ = f32[16,768]{1,0:T(8,128)S(1)} collective-permute-done((f32[16,768]{1,0:T(8,128)S(1)}, f32[16,768]{1,0:T(8,128)S(1)}, u32[]{:S(2)}, u32[]{:S(2)}) %collective-permute-start) | collective-permute-done | bytes 49184 | tf_op jit(solution)/shard_map/ppermute | solution.py:346
  7.4 0.0 collective-permute-done.1.rcv_od_ref.refs_4_
  7.4 1.9 %collective-permute-start.2 = (f32[18,768]{1,0:T(8,128)S(1)}, f32[18,768]{1,0:T(8,128)S(1)}, u32[]{:S(2)}, u32[]{:S(2)}) collective-permute-start(f32[18,768]{1,0:T(8,128)S(1)} %get-tuple-element.22), channel_id=1, source_target_pairs={{0,1},{1,0},{2,3},{3,2},{4,5},{5,4},{6,7},{7,6},{8,9},{9,8},{10,11... | collective-permute-start | bytes 165896 | tf_op jit(solution)/shard_map/ppermute | solution.py:346
  9.3 4.7 %collective-permute-start.3 = (f32[18,768]{1,0:T(8,128)S(1)}, f32[18,768]{1,0:T(8,128)S(1)}, u32[]{:S(2)}, u32[]{:S(2)}) collective-permute-start(f32[18,768]{1,0:T(8,128)S(1)} %get-tuple-element.23), channel_id=1, source_target_pairs={{1,2},{2,1},{3,4},{4,3},{5,6},{6,5},{7,8},{8,7},{9,10},{10,9},{11,... | collective-permute-start | bytes 165896 | tf_op jit(solution)/shard_map/ppermute | solution.py:346
  14.0 0.0 copy-done.2
  14.0 2.7 %coefficients.1.refs_2_ = f32[7,64,768]{2,1,0:T(8,128)S(1)} custom-call(s32[16,192]{1,0:T(8,128)S(1)} %reshape.10.tissue_ref, s32[16,192]{1,0:T(8,128)S(1)} %reshape.11.fiber_ref), custom_call_target="tpu_custom_call" | custom-call | tf_op jit(solution)/shard_map/coefficients/pallas_call | solution.py:374
  16.7 0.0 collective-permute-done.2.refs_5_
  16.7 0.0 collective-permute-done.3.refs_6_
  16.7 0.0 copy-start.1
  16.7 2.8 %copy-done.1 = f32[8,16,16,768]{3,2,1,0:T(8,128)S(1)} copy-done((f32[8,16,16,768]{3,2,1,0:T(8,128)S(1)}, f32[8,16,16,768]{3,2,1,0:T(8,128)}, u32[]{:S(2)}) %copy-start.1) | copy-done | bytes 6291480
  19.5 6.6 %step_first.1 = (f32[8,16,16,768]{3,2,1,0:T(8,128)S(1)}, f32[6,16,768]{2,1,0:T(8,128)S(1)}, f32[16,768]{1,0:T(8,128)S(1)}, f32[16,768]{1,0:T(8,128)S(1)}, f32[16,768]{1,0:T(8,128)S(1)}, /*index=5*/f32[16,768]{1,0:T(8,128)S(1)}) custom-call(f32[8,16,16,768]{3,2,1,0:T(8,128)S(1)} %copy-done.1, f32[8,16,16,768]{3,2,1,0:T(8,128)S(1)} %copy-done.1, ...), custom_call_target="tpu_custom_call" | custom-call | tf_op jit(solution)/shard_map/step_first/pallas_call | solution.py:325
  26.1 3.8 %collective-permute-start.4 = (f32[16,768]{1,0:T(8,128)S(1)}, f32[16,768]{1,0:T(8,128)S(1)}, u32[]{:S(2)}, u32[]{:S(2)}) collective-permute-start(f32[16,768]{1,0:T(8,128)S(1)} %get-tuple-element.25), channel_id=1, source_target_pairs={{0,16},{16,0},{32,48},{48,32},{64,80},{80,64},{96,112},{112,96},{1... | collective-permute-start | bytes 147464 | tf_op jit(solution)/shard_map/ppermute | solution.py:346
  29.9 0.7 collective-permute-start.5
  30.6 0.8 %collective-permute-done.4.rcv_ev_ref.refs_3_ = f32[16,768]{1,0:T(8,128)S(1)} collective-permute-done((f32[16,768]{1,0:T(8,128)S(1)}, f32[16,768]{1,0:T(8,128)S(1)}, u32[]{:S(2)}, u32[]{:S(2)}) %collective-permute-start.4) | collective-permute-done | bytes 49184 | tf_op jit(solution)/shard_map/ppermute | solution.py:346
  31.4 0.0 collective-permute-done.5.rcv_od_ref.refs_4_
  31.4 0.1 collective-permute-start.6
  31.5 5.0 %collective-permute-start.7 = (f32[18,768]{1,0:T(8,128)S(1)}, f32[18,768]{1,0:T(8,128)S(1)}, u32[]{:S(2)}, u32[]{:S(2)}) collective-permute-start(f32[18,768]{1,0:T(8,128)S(1)} %get-tuple-element.30), channel_id=1, source_target_pairs={{1,2},{2,1},{3,4},{4,3},{5,6},{6,5},{7,8},{8,7},{9,10},{10,9},{11,... | collective-permute-start | bytes 165896 | tf_op jit(solution)/shard_map/ppermute | solution.py:346
  36.6 0.0 collective-permute-done.6.refs_5_
  36.6 2.0 %collective-permute-done.7.refs_6_ = f32[18,768]{1,0:T(8,128)S(1)} collective-permute-done((f32[18,768]{1,0:T(8,128)S(1)}, f32[18,768]{1,0:T(8,128)S(1)}, u32[]{:S(2)}, u32[]{:S(2)}) %collective-permute-start.7) | collective-permute-done | bytes 55328 | tf_op jit(solution)/shard_map/ppermute | solution.py:346
  38.6 7.8 %step_last.1 = (f32[8,16,16,768]{3,2,1,0:T(8,128)}, f32[16,72,128]{2,1,0:T(8,128)S(1)}) custom-call(f32[8,16,16,768]{3,2,1,0:T(8,128)S(1)} %get-tuple-element.24.refs_0_.refs_1_, f32[8,16,16,768]{3,2,1,0:T(8,128)S(1)} %get-tuple-element.24.refs_0_.refs_1_, f32[7,64,768]{2,1,0:T(8,128)S(1)} %coefficients.1.refs_2_, ...), custom_call_target="tpu_custom_call" | custom-call | tf_op jit(solution)/shard_map/step_last/pallas_call | solution.py:325
  46.4 25.2 %all_to_all.5.strips_ref = f32[16,72,128]{2,1,0:T(8,128)S(1)} all-to-all(f32[16,72,128]{2,1,0:T(8,128)S(1)} %get-tuple-element.33), channel_id=1, replica_groups=mesh['depth'=16,'area'=16] {'depth'}, dimensions={0} | all-to-all | bytes 1179648 | tf_op jit(solution)/shard_map/all_to_all | solution.py:383
  71.6 0.9 %composite.1 = f32[2,2,4,16,48]{4,3,2,1,0:T(8,128)} custom-call(f32[16,72,128]{2,1,0:T(8,128)S(1)} %all_to_all.5.strips_ref), custom_call_target="tpu_custom_call" | custom-call | tf_op jit(solution)/shard_map/composite/pallas_call | solution.py:384
  (3 shorter events, 0.0 us)
Async XLA Ops:
  0.6 13.3 %copy-start.2 = (s32[4,4,192]{2,1,0:T(4,128)S(1)}, s32[4,4,192]{2,1,0:T(4,128)}, u32[]{:S(2)}) copy-start(s32[4,4,192]{2,1,0:T(4,128)} %param.5) | copy-start | bytes 36868
  1.4 2.8 %copy-start = (f32[8,16,16,768]{3,2,1,0:T(8,128)S(1)}, f32[8,16,16,768]{3,2,1,0:T(8,128)}, u32[]{:S(2)}) copy-start(f32[8,16,16,768]{3,2,1,0:T(8,128)} %refs_1_.1) | copy-start | bytes 18874372
  4.3 3.0 %collective-permute-start = (f32[16,768]{1,0:T(8,128)S(1)}, f32[16,768]{1,0:T(8,128)S(1)}, u32[]{:S(2)}, u32[]{:S(2)}) collective-permute-start(f32[16,768]{1,0:T(8,128)S(1)} %get-tuple-element.18), channel_id=1, source_target_pairs={{0,16},{16,0},{32,48},{48,32},{64,80},{80,64},{96,112},{112,96},{1... | collective-permute-start | bytes 147464 | tf_op jit(solution)/shard_map/ppermute | solution.py:346
  5.6 1.7 %collective-permute-start.1 = (f32[16,768]{1,0:T(8,128)S(1)}, f32[16,768]{1,0:T(8,128)S(1)}, u32[]{:S(2)}, u32[]{:S(2)}) collective-permute-start(f32[16,768]{1,0:T(8,128)S(1)} %get-tuple-element.19), channel_id=1, source_target_pairs={{16,32},{32,16},{48,64},{64,48},{80,96},{96,80},{112,128},{128,112... | collective-permute-start | bytes 147464 | tf_op jit(solution)/shard_map/ppermute | solution.py:346
  7.4 9.3 %collective-permute-start.2 = (f32[18,768]{1,0:T(8,128)S(1)}, f32[18,768]{1,0:T(8,128)S(1)}, u32[]{:S(2)}, u32[]{:S(2)}) collective-permute-start(f32[18,768]{1,0:T(8,128)S(1)} %get-tuple-element.22), channel_id=1, source_target_pairs={{0,1},{1,0},{2,3},{3,2},{4,5},{5,4},{6,7},{7,6},{8,9},{9,8},{10,11... | collective-permute-start | bytes 165896 | tf_op jit(solution)/shard_map/ppermute | solution.py:346
  9.3 7.4 %collective-permute-start.3 = (f32[18,768]{1,0:T(8,128)S(1)}, f32[18,768]{1,0:T(8,128)S(1)}, u32[]{:S(2)}, u32[]{:S(2)}) collective-permute-start(f32[18,768]{1,0:T(8,128)S(1)} %get-tuple-element.23), channel_id=1, source_target_pairs={{1,2},{2,1},{3,4},{4,3},{5,6},{6,5},{7,8},{8,7},{9,10},{10,9},{11,... | collective-permute-start | bytes 165896 | tf_op jit(solution)/shard_map/ppermute | solution.py:346
  16.7 2.8 %copy-start.1 = (f32[8,16,16,768]{3,2,1,0:T(8,128)S(1)}, f32[8,16,16,768]{3,2,1,0:T(8,128)}, u32[]{:S(2)}) copy-start(f32[8,16,16,768]{3,2,1,0:T(8,128)} %refs_1_.1) | copy-start | bytes 18874372
  26.1 5.3 %collective-permute-start.4 = (f32[16,768]{1,0:T(8,128)S(1)}, f32[16,768]{1,0:T(8,128)S(1)}, u32[]{:S(2)}, u32[]{:S(2)}) collective-permute-start(f32[16,768]{1,0:T(8,128)S(1)} %get-tuple-element.25), channel_id=1, source_target_pairs={{0,16},{16,0},{32,48},{48,32},{64,80},{80,64},{96,112},{112,96},{1... | collective-permute-start | bytes 147464 | tf_op jit(solution)/shard_map/ppermute | solution.py:346
  29.9 1.5 %collective-permute-start.5 = (f32[16,768]{1,0:T(8,128)S(1)}, f32[16,768]{1,0:T(8,128)S(1)}, u32[]{:S(2)}, u32[]{:S(2)}) collective-permute-start(f32[16,768]{1,0:T(8,128)S(1)} %get-tuple-element.26), channel_id=1, source_target_pairs={{16,32},{32,16},{48,64},{64,48},{80,96},{96,80},{112,128},{128,112... | collective-permute-start | bytes 147464 | tf_op jit(solution)/shard_map/ppermute | solution.py:346
  31.4 5.1 %collective-permute-start.6 = (f32[18,768]{1,0:T(8,128)S(1)}, f32[18,768]{1,0:T(8,128)S(1)}, u32[]{:S(2)}, u32[]{:S(2)}) collective-permute-start(f32[18,768]{1,0:T(8,128)S(1)} %get-tuple-element.29), channel_id=1, source_target_pairs={{0,1},{1,0},{2,3},{3,2},{4,5},{5,4},{6,7},{7,6},{8,9},{9,8},{10,11... | collective-permute-start | bytes 165896 | tf_op jit(solution)/shard_map/ppermute | solution.py:346
  31.5 7.0 %collective-permute-start.7 = (f32[18,768]{1,0:T(8,128)S(1)}, f32[18,768]{1,0:T(8,128)S(1)}, u32[]{:S(2)}, u32[]{:S(2)}) collective-permute-start(f32[18,768]{1,0:T(8,128)S(1)} %get-tuple-element.30), channel_id=1, source_target_pairs={{1,2},{2,1},{3,4},{4,3},{5,6},{6,5},{7,8},{8,7},{9,10},{10,9},{11,... | collective-permute-start | bytes 165896 | tf_op jit(solution)/shard_map/ppermute | solution.py:346

commit v2 on v1

v2 whole, which is shorter than its diff:
```python
import math

import jax
import jax.numpy as jnp
from jax import lax
from jax.experimental import pallas as pl
from jax.experimental.pallas import tpu as pltpu
from jax.sharding import PartitionSpec as P

BLK = 4
CLASSES = 8
NX = 16
NY = 16
NZ = 768
STRIP = 48
HALF = STRIP // 2
GROUP = 7
CHUNK = 128

TIME_STEP = 0.15
SIGMA_LONG = 1.0
SIGMA_CROSS = 0.3
SLOPES = (8.0, -8.0, 6.0, 5.0, -5.0, -3.0)
MIDDLES = (0.2, 0.4, 0.3, 0.5, 0.6, 0.5)
RATES = (3.0, 0.5, 1.0, 0.8, 0.3, 0.1)
OPACITY = (0.012, 0.01)

f32 = jnp.float32


def params(mib):
    return pltpu.CompilerParams(vmem_limit_bytes=mib * 2**20)


def is_even(axis):
    return lax.rem(lax.axis_index(axis), 2) == 0


def lane_spread(count):
    row = lax.broadcasted_iota(jnp.int32, (count, count * BLK), 0)
    column = lax.broadcasted_iota(jnp.int32, (count, count * BLK), 1)
    return row == lax.shift_right_logical(column, 2)


def flat(ref):
    return jnp.concatenate([ref[k] for k in range(NX // BLK)], axis=0)


def spread_y(wide, start):
    row = lax.broadcasted_iota(jnp.int32, (NY, 1), 0)
    out = jnp.broadcast_to(wide[start:start + 1], (NY, wide.shape[1]))
    for k in range(1, NY // BLK):
        out = jnp.where(row >= BLK * k, wide[start + k:start + k + 1], out)
    return out


def choose(first, a, b):
    return jnp.where(first, a, b)


def faces_kernel(tissue_ref, v_ref, ev_ref, od_ref, ends_ref):
    wide = jnp.dot(flat(tissue_ref).astype(f32).astype(jnp.bfloat16),
                   lane_spread(NZ // BLK).astype(jnp.bfloat16), preferred_element_type=f32)
    even = is_even("area")
    for x in range(NX):
        row = x // BLK * BLK
        low = v_ref[0, x, 0:1] * wide[row:row + 1]
        high = v_ref[0, x, NY - 1:NY] * wide[row + 3:row + 4]
        ev_ref[x:x + 1] = choose(even, high, low)
        od_ref[x:x + 1] = choose(even, low, high)
    ends_ref[0] = v_ref[0, 0] * spread_y(wide, 0)
    ends_ref[1] = v_ref[0, NX - 1] * spread_y(wide, 12)


def class_tables():
    spread = SIGMA_LONG - SIGMA_CROSS
    tables = [[] for _ in range(6)]
    for kind in range(CLASSES):
        polar = math.pi * (kind + 0.5) / CLASSES
        azimuth = 2.3 * kind
        f = (math.cos(polar), math.sin(polar) * math.cos(azimuth), math.sin(polar) * math.sin(azimuth))
        for k in range(3):
            tables[k].append(TIME_STEP * (SIGMA_CROSS + spread * f[k] * f[k]))
        for k, (a, b) in enumerate(((0, 1), (0, 2), (1, 2))):
            tables[3 + k].append(0.5 * TIME_STEP * spread * f[a] * f[b])
    return tables


def coefs_kernel(tissue_ref, fiber_ref, out_ref):
    kind = flat(fiber_ref)
    parts = [flat(tissue_ref).astype(f32)]
    for table in class_tables():
        part = jnp.full(kind.shape, table[0], f32)
        for c in range(1, CLASSES):
            part = jnp.where(kind == c, table[c], part)
        parts.append(part)
    rest = jnp.concatenate(parts, axis=0)
    onehot = lane_spread(NZ // BLK).astype(jnp.bfloat16)
    wide = None
    for _ in range(3):
        piece = rest.astype(jnp.bfloat16)
        rest = rest - piece.astype(f32)
        product = jnp.dot(piece, onehot, preferred_element_type=f32)
        wide = product if wide is None else wide + product
    for k in range(7):
        for block in range(4):
            out_ref[k, NY * block:NY * (block + 1)] = spread_y(wide, 16 * k + 4 * block)


def message_kernel(area_ev_ref, area_od_ref, ends_ref, ev_ref, od_ref):
    area_even = is_even("area")
    depth_even = is_even("depth")
    ev_ref[0:NY] = choose(depth_even, ends_ref[1], ends_ref[0])
    od_ref[0:NY] = choose(depth_even, ends_ref[0], ends_ref[1])
    for place, first, second in ((NY, area_od_ref, area_ev_ref), (NY + 1, area_ev_ref, area_od_ref)):
        low = choose(area_even, first[0:1], second[0:1])
        high = choose(area_even, first[NX - 1:NX], second[NX - 1:NX])
        ev_ref[place:place + 1] = choose(depth_even, high, low)
        od_ref[place:place + 1] = choose(depth_even, low, high)


def z_sides(u):
    lane = lax.broadcasted_iota(jnp.int32, (1, NZ), 1)
    after = jnp.where(lane == NZ - 1, 0.0, pltpu.roll(u, NZ - 1, axis=1))
    before = jnp.where(lane == 0, 0.0, pltpu.roll(u, 1, axis=1))
    return after, before


def y_sides(u, row_lo, row_hi):
    row = lax.broadcasted_iota(jnp.int32, (NY, 1), 0)
    after = jnp.where(row == NY - 1, row_hi, pltpu.roll(u, NY - 1, axis=0))
    before = jnp.where(row == 0, row_lo, pltpu.roll(u, 1, axis=0))
    return after, before


def derive(v_ref, coefs_ref, ev_ref, od_ref, u_s, uy_s, uz_s, w_s, lo_s, hi_s, loz_s, hiz_s):
    even = is_even("area")
    lo_s[...] = choose(even, od_ref[...], ev_ref[...])
    hi_s[...] = choose(even, ev_ref[...], od_ref[...])
    for source, target in ((lo_s, loz_s), (hi_s, hiz_s)):
        after, before = z_sides(source[...])
        target[...] = after - before

    def plane(x, carry):
        rows = pl.ds(pl.multiple_of(lax.shift_right_logical(x, 2) * NY, NY), NY)
        u = v_ref[0, x] * coefs_ref[0, rows]
        u_s[x] = u
        after, before = z_sides(u)
        uz = after - before
        uz_s[x] = uz
        w = 0.52 * u + coefs_ref[3, rows] * (after + before)
        after, before = y_sides(u, lo_s[pl.ds(x, 1)], hi_s[pl.ds(x, 1)])
        uy_s[x] = after - before
        w = w + coefs_ref[2, rows] * (after + before)
        after, before = y_sides(uz, loz_s[pl.ds(x, 1)], hiz_s[pl.ds(x, 1)])
        w_s[x] = w + coefs_ref[6, rows] * (after - before)
        return carry

    lax.fori_loop(0, NX, plane, 0)


def ionic(w, gates, calcium):
    fresh = []
    for k in range(6):
        keep = math.exp(-TIME_STEP * RATES[k])
        half = 0.5 * (1.0 - keep)
        t = jnp.tanh((0.5 * SLOPES[k]) * w - (0.5 * SLOPES[k] * MIDDLES[k]))
        fresh.append(half * t + (keep * gates[k] + half))
    both = fresh[3] * fresh[4]
    cube = fresh[0] * fresh[0] * fresh[0]
    loss = (
        (2.0 * TIME_STEP) * (cube * fresh[1]) * (w - 1.2)
        + TIME_STEP * (fresh[2] * fresh[2]) * (w + 0.1)
        + (0.6 * TIME_STEP) * both * (w - 0.9)
        + (0.2 * TIME_STEP) * (1.0 + fresh[5]) * (w - 0.05)
    )
    gain = (1.5 * TIME_STEP) * both
    calc_next = (1.0 - 0.8 * TIME_STEP) * calcium + gain * (1.0 - calcium)
    return w - loss, fresh, calc_next


def march(q, opaque, state):
    passed, red, green = state
    alpha = opaque * jnp.tanh(3.0 * q - 1.2) + opaque
    weight = passed * alpha
    off = q - 0.5
    red = red + weight * jnp.tanh(2.5 * off)
    green = green + weight * jnp.exp(-6.0 * (off * off))
    return passed - weight, red, green


def advance(w, old, inside):
    volt, fresh, calc = ionic(w, old[1:7], old[7])
    return [jnp.where(inside, a, b) for a, b in zip([volt] + fresh + [calc], old)]


def show(new, m, marches):
    return [march(q, (0.5 * OPACITY[f]) * m, marches[f]) for f, q in enumerate((new[0], new[7]))]


def interior_kernel(states_ref, v_ref, coefs_ref, area_ev_ref, area_od_ref,
                    out_ref, shown_ref, base_ref, row_lo_ref, row_hi_ref,
                    u_s, uy_s, uz_s, w_s, lo_s, hi_s, loz_s, hiz_s):
    j = pl.program_id(0)

    @pl.when(j == 0)
    def _():
        derive(v_ref, coefs_ref, area_ev_ref, area_od_ref,
               u_s, uy_s, uz_s, w_s, lo_s, hi_s, loz_s, hiz_s)

    cols = pl.ds(pl.multiple_of(j * CHUNK, CHUNK), CHUNK)
    for end, x, beside, sign in ((0, 0, 1, 1.0), (1, NX - 1, NX - 2, -1.0)):
        rows = pl.ds(x // BLK * NY, NY)
        base_ref[end] = (
            w_s[x, :, cols]
            + coefs_ref[1, rows, cols] * u_s[beside, :, cols]
            + sign * (coefs_ref[4, rows, cols] * uy_s[beside, :, cols]
                      + coefs_ref[5, rows, cols] * uz_s[beside, :, cols])
        )

    def planes(g, carry):
        marches = carry
        for p in range(GROUP):
            x = 1 + g * GROUP + p
            rows = pl.ds(pl.multiple_of(lax.shift_right_logical(x, 2) * NY, NY), NY)
            m = coefs_ref[0, rows, cols]
            w = (
                w_s[x, :, cols]
                + coefs_ref[1, rows, cols] * (u_s[x + 1, :, cols] + u_s[x - 1, :, cols])
                + coefs_ref[4, rows, cols] * (uy_s[x + 1, :, cols] - uy_s[x - 1, :, cols])
                + coefs_ref[5, rows, cols] * (uz_s[x + 1, :, cols] - uz_s[x - 1, :, cols])
            )
            new = advance(w, [states_ref[k, x] for k in range(8)], m > 0.5)
            for k in range(8):
                out_ref[k, x] = new[k]
            marches = show(new, m, marches)
        return marches

    one = jnp.ones((NY, CHUNK), f32)
    zero = jnp.zeros((NY, CHUNK), f32)
    marches = lax.fori_loop(0, (NX - 2) // GROUP, planes, [(one, zero, zero)] * 2)
    for f in range(2):
        for k in range(3):
            shown_ref[3 * f + k] = marches[f][k]
    for x in range(1, NX - 1):
        first = x // BLK * NY
        final = first + NY - 1
        row_lo_ref[x:x + 1] = out_ref[0, x, 0:1] * coefs_ref[0, first:first + 1, cols]
        row_hi_ref[x:x + 1] = out_ref[0, x, NY - 1:NY] * coefs_ref[0, final:final + 1, cols]


def ends_body(last, refs):
    states_ref, base_ref, coefs_ref, depth_ev_ref, depth_od_ref, shown_ref = refs[:6]
    if last:
        earlier_ref, _, out_ref, strips_ref, acc_s, uy_s, uz_s = refs[6:]
    else:
        (row_lo_ref, row_hi_ref, _, out_ref, images_ref, ev_ref, od_ref, ends_ref,
         acc_s, uy_s, uz_s) = refs[6:]
    i = pl.program_id(0)
    back = i == 1
    sign = jnp.where(back, 1.0, -1.0)
    use_ev = is_even("depth") == back
    halo = choose(use_ev, depth_ev_ref[...], depth_od_ref[...])
    u = halo[0:NY]
    after, before = z_sides(u)
    uz_s[...] = sign * (after - before)
    after, before = y_sides(u, halo[NY:NY + 1], halo[NY + 1:NY + 2])
    uy_s[...] = sign * (after - before)

    @pl.when(i == 0)
    def _():
        for k in range(6):
            acc_s[k] = jnp.full((NY, NZ), 1.0 if k % 3 == 0 else 0.0, f32)

    for j in range(NZ // CHUNK):
        cols = slice(j * CHUNK, (j + 1) * CHUNK)
        m = coefs_ref[0, :, cols]
        w = (
            base_ref[0, :, cols]
            + coefs_ref[1, :, cols] * u[:, cols]
            + coefs_ref[4, :, cols] * uy_s[:, cols]
            + coefs_ref[5, :, cols] * uz_s[:, cols]
        )
        new = advance(w, [states_ref[k, 0, :, cols] for k in range(8)], m > 0.5)
        for k in range(8):
            out_ref[k, 0, :, cols] = new[k]
        marches = [tuple(acc_s[3 * f + k, :, cols] for k in range(3)) for f in range(2)]
        marches = show(new, m, marches)
        for f in range(2):
            for k in range(3):
                acc_s[3 * f + k, :, cols] = marches[f][k]
        if not last:
            ends_ref[0, :, cols] = m * new[0]

    @pl.when(i == 0)
    def _():
        for f in range(2):
            passed = acc_s[3 * f]
            for k in (1, 2):
                acc_s[3 * f + k] = acc_s[3 * f + k] + passed * shown_ref[3 * f + k]
            acc_s[3 * f] = passed * shown_ref[3 * f]

    if not last:
        even = is_even("area")

        @pl.when(i == 0)
        def _():
            lo, hi = row_lo_ref[...], row_hi_ref[...]
            ev_ref[...] = choose(even, hi, lo)
            od_ref[...] = choose(even, lo, hi)

        for end, x in ((0, 0), (1, NX - 1)):
            @pl.when(i == end)
            def _():
                lo, hi = ends_ref[0, 0:1], ends_ref[0, NY - 1:NY]
                ev_ref[x:x + 1] = choose(even, hi, lo)
                od_ref[x:x + 1] = choose(even, lo, hi)

        @pl.when(back)
        def _():
            images_ref[...] = acc_s[...]
    else:
        @pl.when(back)
        def _():
            for k in range(3):
                stack = jnp.concatenate(
                    [earlier_ref[k], earlier_ref[3 + k], acc_s[k], acc_s[3 + k]], axis=0)
                stack = jnp.concatenate([stack, pltpu.roll(stack, NZ - HALF, axis=1)], axis=0)
                turned = stack.T
                for d in range(NZ // STRIP):
                    strips_ref[d, HALF * k:HALF * (k + 1)] = turned[STRIP * d:STRIP * d + HALF]


def composite_kernel(strips_ref, out_ref):
    count = strips_ref.shape[0]
    passed = jnp.ones((HALF, 128), f32)
    red = jnp.zeros((HALF, 128), f32)
    green = jnp.zeros((HALF, 128), f32)
    for s in range(count):
        red = red + passed * strips_ref[s, HALF:2 * HALF]
        green = green + passed * strips_ref[s, 2 * HALF:3 * HALF]
        passed = passed * strips_ref[s, 0:HALF]
    solid = 1.0 - passed
    red = 0.5 * (solid + red)
    whole = jnp.concatenate([red, green, solid - red, solid, jnp.zeros((32, 128), f32)], axis=0)
    turned = whole.T
    first, second = turned[0:64], turned[64:128]
    lane = lax.broadcasted_iota(jnp.int32, (1, 128), 1)
    for c in range(4):
        a = pltpu.roll(first, (128 - HALF * c) % 128, axis=1) if c else first
        b = pltpu.roll(second, (128 + HALF - HALF * c) % 128, axis=1) if c != 1 else second
        o = jnp.where(lane < HALF, a, b)
        for k in range(4):
            out_ref[k // 2, k % 2, c] = o[NY * k:NY * (k + 1), 0:STRIP]


def full(shape):
    return pl.BlockSpec(shape, lambda *_: (0,) * len(shape))


def interior(states, coefs, area):
    block = pl.BlockSpec((8, NX, NY, CHUNK), lambda j: (0, 0, 0, j))
    row = pl.BlockSpec((NX, CHUNK), lambda j: (0, j))
    voxels = NX * NY * NZ
    return pl.pallas_call(
        interior_kernel,
        grid=(NZ // CHUNK,),
        in_specs=[block, full((1, NX, NY, NZ)), full((7, 64, NZ)), full((NX, NZ)), full((NX, NZ))],
        out_specs=[block, pl.BlockSpec((6, NY, CHUNK), lambda j: (0, 0, j)),
                   pl.BlockSpec((2, NY, CHUNK), lambda j: (0, 0, j)), row, row],
        out_shape=[jax.ShapeDtypeStruct(s, f32) for s in
                   ((8, NX, NY, NZ), (6, NY, NZ), (2, NY, NZ), (NX, NZ), (NX, NZ))],
        scratch_shapes=[pltpu.VMEM((NX, NY, NZ), f32)] * 4 + [pltpu.VMEM((NX, NZ), f32)] * 4,
        compiler_params=params(24),
        cost_estimate=pl.CostEstimate(flops=400 * voxels, bytes_accessed=64 * voxels,
                                      transcendentals=12 * voxels),
        name="interior",
    )(states, states, coefs, *area)


def ends(last, states, base, coefs, depth, shown, extra, new):
    plane = pl.BlockSpec((8, 1, NY, NZ), lambda i: (0, (NX - 1) * i, 0, 0))
    end = pl.BlockSpec((1, NY, NZ), lambda i: (i, 0, 0))
    in_specs = [plane, end, pl.BlockSpec((7, NY, NZ), lambda i: (0, 3 * i, 0)),
                full((NY + 2, NZ)), full((NY + 2, NZ)), full((6, NY, NZ))]
    in_specs += [full(item.shape) for item in extra] + [pl.BlockSpec(memory_space=pl.ANY)]
    args = [states, base, coefs, *depth, shown, *extra, new]
    out_specs = [plane]
    out_shape = [new.shape]
    if last:
        out_shape += [(NZ // STRIP, 3 * HALF, 128)]
        out_specs += [full(out_shape[1])]
    else:
        out_shape += [(6, NY, NZ), (NX, NZ), (NX, NZ), (2, NY, NZ)]
        out_specs += [full((6, NY, NZ)), full((NX, NZ)), full((NX, NZ)), end]
    return pl.pallas_call(
        lambda *refs: ends_body(last, refs),
        grid=(2,),
        in_specs=in_specs,
        out_specs=out_specs,
        out_shape=[jax.ShapeDtypeStruct(s, f32) for s in out_shape],
        scratch_shapes=[pltpu.VMEM((6, NY, NZ), f32)] + [pltpu.VMEM((NY, NZ), f32)] * 2,
        input_output_aliases={len(args) - 1: 0},
        compiler_params=params(16),
        name="ends_last" if last else "ends_first",
    )(*args)


def swaps(axis):
    count = lax.axis_size(axis)
    even = [(i, i ^ 1) for i in range(count) if i ^ 1 < count]
    odd = [(i, ((i - 1) ^ 1) + 1) for i in range(1, count) if ((i - 1) ^ 1) + 1 < count]
    return even, odd


def exchange(axis, pair):
    even, odd = swaps(axis)
    return lax.ppermute(pair[0], axis, even), lax.ppermute(pair[1], axis, odd)


def depth_halo(area, ends_planes):
    messages = pl.pallas_call(
        message_kernel,
        out_shape=[jax.ShapeDtypeStruct((NY + 2, NZ), f32)] * 2,
        compiler_params=params(1),
        name="depth_message",
    )(*area, ends_planes)
    return exchange("depth", messages)


def per_device(states, tissue, fiber):
    blocks = (NX // BLK, NY // BLK, NZ // BLK)
    ev, od, planes = pl.pallas_call(
        faces_kernel,
        grid=(1,),
        in_specs=[full(blocks), full((1, NX, NY, NZ))],
        out_specs=[full((NX, NZ)), full((NX, NZ)), full((2, NY, NZ))],
        out_shape=[jax.ShapeDtypeStruct(s, f32) for s in ((NX, NZ), (NX, NZ), (2, NY, NZ))],
        compiler_params=params(58),
        name="faces",
    )(tissue, states)
    area = exchange("area", (ev, od))
    coefs = pl.pallas_call(
        coefs_kernel,
        out_shape=jax.ShapeDtypeStruct((7, 64, NZ), f32),
        compiler_params=params(8),
        name="coefficients",
    )(tissue, fiber)
    depth = depth_halo(area, planes)
    new, shown, base, row_lo, row_hi = interior(states, coefs, area)
    states, images, ev, od, planes = ends(
        False, states, base, coefs, depth, shown, (row_lo, row_hi), new)
    area = exchange("area", (ev, od))
    depth = depth_halo(area, planes)
    new, shown, base, _, _ = interior(states, coefs, area)
    states, strips = ends(True, states, base, coefs, depth, shown, (images,), new)
    strips = lax.all_to_all(strips, "depth", split_axis=0, concat_axis=0, tiled=True)
    images = pl.pallas_call(
        composite_kernel,
        out_shape=jax.ShapeDtypeStruct((2, 2, 4, NY, STRIP), f32),
        compiler_params=params(4),
        name="composite",
    )(strips)
    return states, images


def solution(mesh):
    return jax.shard_map(
        per_device,
        mesh=mesh,
        in_specs=(
            P(None, "depth", "area", None),
            P("depth", "area", None),
            P("depth", "area", None),
        ),
        out_specs=(P(None, "depth", "area", None), P(None, None, None, "area", "depth")),
        check_vma=False,
    )
```

time: 72.8 us -> 66.7 us (0.916)
  blocking collectives: 25.2 us -> 21.1 us
  local copies, waits for them, and re-layouts: 6.31 us -> 3.69 us
  Pallas kernels: 18.2 us -> 20.2 us
  starting transfers between devices: 18.1 us -> 16.7 us
    pallas_call x5 -> x7, Pallas kernels: 14.6 us -> 18.8 us  [the longest x2 13.5 us: interior(): pl.pallas_call(interior_kernel, grid=(NZ // CHUNK,), in_specs=[block, ful...]
    all_to_all x1, blocking collectives: 25.2 us -> 21.1 us  [per_device(): lax.all_to_all(strips, 'depth', split_axis=0, concat_axis=0, tiled=True)]
    pallas_call x1, Pallas kernels: 2.69 us -> 0.41 us  [per_device(): pl.pallas_call(coefs_kernel, out_shape=jax.ShapeDtypeStruct((7, 64, NZ),...]
    unnamed x6 -> x12, local copies, waits for them, and re-layouts: 5.57 us -> 3.69 us
    ppermute x8, starting transfers between devices: 18.1 us -> 16.7 us  [exchange(): return (lax.ppermute(pair[0], axis, even), lax.ppermute(pair[1], axis, odd))]
    reshape x2 -> x0, local copies, waits for them, and re-layouts: 0.74 us -> none  [the longest x1 0.73 us: per_device(): tissue = tissue.reshape(16, NZ // BLK)]
  transfers between devices with their start and end apart: 8 -> 8, of which waited for: 3 -> 2; matrix products, arithmetic and copies ran while one was open for 0% -> 0% of each run, Pallas kernels for 4% -> 21%
where the time goes in v2:
time: 66.7 us; the launch traced here: 66.4 us
  blocking collectives  21.1 us (32%)
  Pallas kernels  20.2 us (30%)
  starting transfers between devices  16.7 us (25%)
  waiting for transfers between devices  3.93 us (6%)
  local copies, waits for them, and re-layouts  3.69 us (6%)
  between operations  0.82 us (1%)
    all_to_all x1, blocking collectives, per_device(): lax.all_to_all(strips, 'depth', split_axis=0, concat_axis=0, tiled=True)  21.1 us
    ppermute x8, starting transfers between devices, exchange(): return (lax.ppermute(pair[0], axis, even), lax.ppermute(pair[1], axis, odd))  16.7 us
    pallas_call x2, Pallas kernels, interior(): pl.pallas_call(interior_kernel, grid=(NZ // CHUNK,), in_specs=[block, ful...  13.5 us
    ppermute x8, waiting for transfers between devices, exchange(): return (lax.ppermute(pair[0], axis, even), lax.ppermute(pair[1], axis, odd))  3.93 us
    unnamed x12, local copies, waits for them, and re-layouts  3.69 us
    pallas_call x2, Pallas kernels, ends(): pl.pallas_call(lambda *refs: ends_body(last, refs), grid=(2,), in_specs=i...  3.12 us
    pallas_call x1, Pallas kernels, per_device(): pl.pallas_call(faces_kernel, grid=(1,), in_specs=[full(blocks), full((1,...  2.16 us
  transfers between devices with their start and end apart: 8, of which 2 were waited for; matrix products, arithmetic and copies ran while one was open for 0% of the time, Pallas kernels for 21%

profile of v2, /device:TPU:97, one launch (start us, length us, event | category | flops | bytes accessed | tf_op | source)
XLA Modules:
  0.0 66.4 jit_solution(3123100434227069743)
XLA Ops:
  0.6 0.0 copy-start.2
  0.6 0.0 copy-start.3
  0.6 0.0 slice-start
  0.7 2.2 %faces.1 = (f32[16,768]{1,0:T(8,128)}, f32[16,768]{1,0:T(8,128)}, f32[2,16,768]{2,1,0:T(8,128)}) custom-call(s32[4,4,192]{2,1,0:T(4,128)} %tissue_ref.3, f32[8,16,16,768]{3,2,1,0:T(8,128)} %refs_0_.1), custom_call_target="tpu_custom_call" | custom-call | tf_op jit(solution)/shard_map/faces/pallas_call | solution.py:433
  2.8 0.7 %collective-permute-start = (f32[16,768]{1,0:T(8,128)}, f32[16,768]{1,0:T(8,128)S(1)}, u32[]{:S(2)}, u32[]{:S(2)}) collective-permute-start(f32[16,768]{1,0:T(8,128)} %get-tuple-element.24), channel_id=1, source_target_pairs={{0,1},{1,0},{2,3},{3,2},{4,5},{5,4},{6,7},{7,6},{8,9},{9,8},{10,11... | collective-permute-start | bytes 147464 | tf_op jit(solution)/shard_map/ppermute | solution.py:418
  3.5 4.6 %collective-permute-start.1 = (f32[16,768]{1,0:T(8,128)}, f32[16,768]{1,0:T(8,128)S(1)}, u32[]{:S(2)}, u32[]{:S(2)}) collective-permute-start(f32[16,768]{1,0:T(8,128)} %get-tuple-element.25), channel_id=1, source_target_pairs={{1,2},{2,1},{3,4},{4,3},{5,6},{6,5},{7,8},{8,7},{9,10},{10,9},{11,... | collective-permute-start | bytes 147464 | tf_op jit(solution)/shard_map/ppermute | solution.py:418
  8.1 0.0 collective-permute-done.area_ev_ref
  8.1 2.2 %collective-permute-done.1.area_od_ref = f32[16,768]{1,0:T(8,128)S(1)} collective-permute-done((f32[16,768]{1,0:T(8,128)}, f32[16,768]{1,0:T(8,128)S(1)}, u32[]{:S(2)}, u32[]{:S(2)}) %collective-permute-start.1) | collective-permute-done | bytes 49184 | tf_op jit(solution)/shard_map/ppermute | solution.py:418
  10.3 0.0 copy-start.1
  10.3 0.9 %copy-done.1 = f32[2,16,768]{2,1,0:T(8,128)S(1)} copy-done((f32[2,16,768]{2,1,0:T(8,128)S(1)}, f32[2,16,768]{2,1,0:T(8,128)}, u32[]{:S(2)}) %copy-start.1) | copy-done | bytes 98328
  11.2 1.3 %collective-permute-start.2 = (f32[18,768]{1,0:T(8,128)S(1)}, f32[18,768]{1,0:T(8,128)S(1)}, u32[]{:S(2)}, u32[]{:S(2)}) collective-permute-start(f32[18,768]{1,0:T(8,128)S(1)} %get-tuple-element.28), channel_id=1, source_target_pairs={{0,16},{16,0},{32,48},{48,32},{64,80},{80,64},{96,112},{112,96},{1... | collective-permute-start | bytes 165896 | tf_op jit(solution)/shard_map/ppermute | solution.py:418
  12.5 0.7 collective-permute-start.3
  13.2 0.0 copy-done.2
  13.2 0.0 copy-done.3
  13.2 0.4 coefficients.1.coefs_ref.refs_2_
  13.6 0.0 copy-start
  13.6 2.8 %copy-done = f32[8,16,16,768]{3,2,1,0:T(8,128)S(1)} copy-done((f32[8,16,16,768]{3,2,1,0:T(8,128)S(1)}, f32[8,16,16,768]{3,2,1,0:T(8,128)}, u32[]{:S(2)}) %copy-start) | copy-done | bytes 6291480
  16.4 0.0 slice-start.1
  16.4 6.2 %interior.2 = (f32[8,16,16,768]{3,2,1,0:T(8,128)S(1)}, f32[6,16,768]{2,1,0:T(8,128)S(1)}, f32[2,16,768]{2,1,0:T(8,128)S(1)}, f32[16,768]{1,0:T(8,128)S(1)}, f32[16,768]{1,0:T(8,128)S(1)}) custom-call(f32[8,16,16,768]{3,2,1,0:T(8,128)S(1)} %copy-done, f32[8,16,16,768]{3,2,1,0:T(8,128)S(1)} %copy-done, f32[7,64,768]{2,1,0:T(8,128)S(1)} %coefficients.1.coefs_ref.refs_2_, ...), custom_call_target="tpu_custom_call" | custom-call | flops 78643200 | bytes 12582912 | tf_op jit(solution)/shard_map/interior/pallas_call | solution.py:365
  22.6 0.0 collective-permute-done.2.refs_3_
  22.6 0.0 collective-permute-done.3.refs_4_
  22.6 0.0 slice-done
  22.6 0.0 slice-done.1
  22.7 1.0 %ends_first.1 = (f32[8,16,16,768]{3,2,1,0:T(8,128)S(1)}, f32[6,16,768]{2,1,0:T(8,128)S(1)}, f32[16,768]{1,0:T(8,128)S(1)}, f32[16,768]{1,0:T(8,128)S(1)}, f32[2,16,768]{2,1,0:T(8,128)S(1)}) custom-call(f32[8,16,16,768]{3,2,1,0:T(8,128)S(1)} %bitcast.1, f32[2,16,768]{2,1,0:T(8,128)S(1)} %get-tuple-element.26.refs_1_, ...), custom_call_target="tpu_custom_call", output_to_operand_aliasing={{0}: (8, {})} | custom-call | tf_op jit(solution)/shard_map/ends_first/pallas_call | solution.py:396
  23.6 0.1 collective-permute-start.4
  23.7 4.9 %collective-permute-start.5 = (f32[16,768]{1,0:T(8,128)S(1)}, f32[16,768]{1,0:T(8,128)S(1)}, u32[]{:S(2)}, u32[]{:S(2)}) collective-permute-start(f32[16,768]{1,0:T(8,128)S(1)} %get-tuple-element.36), channel_id=1, source_target_pairs={{1,2},{2,1},{3,4},{4,3},{5,6},{6,5},{7,8},{8,7},{9,10},{10,9},{11,... | collective-permute-start | bytes 147464 | tf_op jit(solution)/shard_map/ppermute | solution.py:418
  28.7 0.0 collective-permute-done.4.area_ev_ref
  28.7 1.7 %collective-permute-done.5.area_od_ref = f32[16,768]{1,0:T(8,128)S(1)} collective-permute-done((f32[16,768]{1,0:T(8,128)S(1)}, f32[16,768]{1,0:T(8,128)S(1)}, u32[]{:S(2)}, u32[]{:S(2)}) %collective-permute-start.5) | collective-permute-done | bytes 49184 | tf_op jit(solution)/shard_map/ppermute | solution.py:418
  30.5 3.7 %collective-permute-start.6 = (f32[18,768]{1,0:T(8,128)S(1)}, f32[18,768]{1,0:T(8,128)S(1)}, u32[]{:S(2)}, u32[]{:S(2)}) collective-permute-start(f32[18,768]{1,0:T(8,128)S(1)} %get-tuple-element.39), channel_id=1, source_target_pairs={{0,16},{16,0},{32,48},{48,32},{64,80},{80,64},{96,112},{112,96},{1... | collective-permute-start | bytes 165896 | tf_op jit(solution)/shard_map/ppermute | solution.py:418
  34.2 0.7 collective-permute-start.7
  34.9 7.3 %interior.3 = (f32[8,16,16,768]{3,2,1,0:T(8,128)}, f32[6,16,768]{2,1,0:T(8,128)S(1)}, f32[2,16,768]{2,1,0:T(8,128)S(1)}, f32[16,768]{1,0:T(8,128)}, f32[16,768]{1,0:T(8,128)}) custom-call(f32[8,16,16,768]{3,2,1,0:T(8,128)S(1)} %get-tuple-element.34.states_ref.v_ref.refs_0_, f32[8,16,16,768]{3,2,1,0:T(8,128)S(1)} %get-tuple-element.34.states_ref.v_ref.refs_0_, ...), custom_call_target="tpu_custom_call" | custom-call | flops 78643200 | bytes 12582912 | tf_op jit(solution)/shard_map/interior/pallas_call | solution.py:365
  42.2 0.0 collective-permute-done.6.refs_3_
  42.2 0.0 collective-permute-done.7.refs_4_
  42.2 2.1 %ends_last.1 = (f32[8,16,16,768]{3,2,1,0:T(8,128)}, f32[16,72,128]{2,1,0:T(8,128)S(1)}) custom-call(f32[8,16,16,768]{3,2,1,0:T(8,128)S(1)} %get-tuple-element.34.states_ref.v_ref.refs_0_, f32[2,16,768]{2,1,0:T(8,128)S(1)} %get-tuple-element.37.refs_1_, f32[7,64,768]{2,1,0:T(8,128)S(1)} %coefficients.1.coefs_ref.refs_2_, ...), custom_call_target="tpu_custom_call", output_to_operand_aliasing={{0}: (7, {})} | custom-call | tf_op jit(solution)/shard_map/ends_last/pallas_call | solution.py:396
  44.4 21.1 %all_to_all.5.strips_ref = f32[16,72,128]{2,1,0:T(8,128)S(1)} all-to-all(f32[16,72,128]{2,1,0:T(8,128)S(1)} %get-tuple-element.45), channel_id=1, replica_groups=mesh['depth'=16,'area'=16] {'depth'}, dimensions={0} | all-to-all | bytes 1179648 | tf_op jit(solution)/shard_map/all_to_all | solution.py:457
  65.5 0.9 %composite.1 = f32[2,2,4,16,48]{4,3,2,1,0:T(8,128)} custom-call(f32[16,72,128]{2,1,0:T(8,128)S(1)} %all_to_all.5.strips_ref), custom_call_target="tpu_custom_call" | custom-call | tf_op jit(solution)/shard_map/composite/pallas_call | solution.py:458
  (3 shorter events, 0.0 us)
Async XLA Ops:
  0.6 12.6 %copy-start.2 = (s32[4,4,192]{2,1,0:T(4,128)S(1)}, s32[4,4,192]{2,1,0:T(4,128)}, u32[]{:S(2)}) copy-start(s32[4,4,192]{2,1,0:T(4,128)} %tissue_ref.3) | copy-start | bytes 36868
  0.6 12.6 %copy-start.3 = (s32[4,4,192]{2,1,0:T(4,128)S(1)}, s32[4,4,192]{2,1,0:T(4,128)}, u32[]{:S(2)}) copy-start(s32[4,4,192]{2,1,0:T(4,128)} %fiber_ref.1) | copy-start | bytes 36868
  0.6 22.0 %slice-start = ((s8[6291456]{0:T(1024)(128)(4,1)}), s8[2097152]{0:T(1024)(128)(4,1)S(1)}, s32[]{:S(2)}) async-start(s8[6291456]{0:T(1024)(128)(4,1)} %bitcast), calls=%async_computation.1 | async-start | bytes 4194304
  2.8 5.3 %collective-permute-start = (f32[16,768]{1,0:T(8,128)}, f32[16,768]{1,0:T(8,128)S(1)}, u32[]{:S(2)}, u32[]{:S(2)}) collective-permute-start(f32[16,768]{1,0:T(8,128)} %get-tuple-element.24), channel_id=1, source_target_pairs={{0,1},{1,0},{2,3},{3,2},{4,5},{5,4},{6,7},{7,6},{8,9},{9,8},{10,11... | collective-permute-start | bytes 147464 | tf_op jit(solution)/shard_map/ppermute | solution.py:418
  3.5 6.8 %collective-permute-start.1 = (f32[16,768]{1,0:T(8,128)}, f32[16,768]{1,0:T(8,128)S(1)}, u32[]{:S(2)}, u32[]{:S(2)}) collective-permute-start(f32[16,768]{1,0:T(8,128)} %get-tuple-element.25), channel_id=1, source_target_pairs={{1,2},{2,1},{3,4},{4,3},{5,6},{6,5},{7,8},{8,7},{9,10},{10,9},{11,... | collective-permute-start | bytes 147464 | tf_op jit(solution)/shard_map/ppermute | solution.py:418
  10.3 0.9 %copy-start.1 = (f32[2,16,768]{2,1,0:T(8,128)S(1)}, f32[2,16,768]{2,1,0:T(8,128)}, u32[]{:S(2)}) copy-start(f32[2,16,768]{2,1,0:T(8,128)} %get-tuple-element.27.ends_ref) | copy-start | bytes 294916
  11.2 11.4 %collective-permute-start.2 = (f32[18,768]{1,0:T(8,128)S(1)}, f32[18,768]{1,0:T(8,128)S(1)}, u32[]{:S(2)}, u32[]{:S(2)}) collective-permute-start(f32[18,768]{1,0:T(8,128)S(1)} %get-tuple-element.28), channel_id=1, source_target_pairs={{0,16},{16,0},{32,48},{48,32},{64,80},{80,64},{96,112},{112,96},{1... | collective-permute-start | bytes 165896 | tf_op jit(solution)/shard_map/ppermute | solution.py:418
  12.5 10.1 %collective-permute-start.3 = (f32[18,768]{1,0:T(8,128)S(1)}, f32[18,768]{1,0:T(8,128)S(1)}, u32[]{:S(2)}, u32[]{:S(2)}) collective-permute-start(f32[18,768]{1,0:T(8,128)S(1)} %get-tuple-element.29), channel_id=1, source_target_pairs={{16,32},{32,16},{48,64},{64,48},{80,96},{96,80},{112,128},{128,112... | collective-permute-start | bytes 165896 | tf_op jit(solution)/shard_map/ppermute | solution.py:418
  13.6 2.8 %copy-start = (f32[8,16,16,768]{3,2,1,0:T(8,128)S(1)}, f32[8,16,16,768]{3,2,1,0:T(8,128)}, u32[]{:S(2)}) copy-start(f32[8,16,16,768]{3,2,1,0:T(8,128)} %refs_0_.1) | copy-start | bytes 18874372
  16.4 6.2 %slice-start.1 = ((s8[6291456]{0:T(1024)(128)(4,1)}), s8[4194304]{0:T(1024)(128)(4,1)S(1)}, s32[]{:S(2)}) async-start(s8[6291456]{0:T(1024)(128)(4,1)} %bitcast), calls=%async_computation.2 | async-start | bytes 8388608
  23.6 5.0 %collective-permute-start.4 = (f32[16,768]{1,0:T(8,128)S(1)}, f32[16,768]{1,0:T(8,128)S(1)}, u32[]{:S(2)}, u32[]{:S(2)}) collective-permute-start(f32[16,768]{1,0:T(8,128)S(1)} %get-tuple-element.35), channel_id=1, source_target_pairs={{0,1},{1,0},{2,3},{3,2},{4,5},{5,4},{6,7},{7,6},{8,9},{9,8},{10,11... | collective-permute-start | bytes 147464 | tf_op jit(solution)/shard_map/ppermute | solution.py:418
  23.7 6.7 %collective-permute-start.5 = (f32[16,768]{1,0:T(8,128)S(1)}, f32[16,768]{1,0:T(8,128)S(1)}, u32[]{:S(2)}, u32[]{:S(2)}) collective-permute-start(f32[16,768]{1,0:T(8,128)S(1)} %get-tuple-element.36), channel_id=1, source_target_pairs={{1,2},{2,1},{3,4},{4,3},{5,6},{6,5},{7,8},{8,7},{9,10},{10,9},{11,... | collective-permute-start | bytes 147464 | tf_op jit(solution)/shard_map/ppermute | solution.py:418
  30.5 11.7 %collective-permute-start.6 = (f32[18,768]{1,0:T(8,128)S(1)}, f32[18,768]{1,0:T(8,128)S(1)}, u32[]{:S(2)}, u32[]{:S(2)}) collective-permute-start(f32[18,768]{1,0:T(8,128)S(1)} %get-tuple-element.39), channel_id=1, source_target_pairs={{0,16},{16,0},{32,48},{48,32},{64,80},{80,64},{96,112},{112,96},{1... | collective-permute-start | bytes 165896 | tf_op jit(solution)/shard_map/ppermute | solution.py:418
  34.2 8.0 %collective-permute-start.7 = (f32[18,768]{1,0:T(8,128)S(1)}, f32[18,768]{1,0:T(8,128)S(1)}, u32[]{:S(2)}, u32[]{:S(2)}) collective-permute-start(f32[18,768]{1,0:T(8,128)S(1)} %get-tuple-element.40), channel_id=1, source_target_pairs={{16,32},{32,16},{48,64},{64,48},{80,96},{96,80},{112,128},{128,112... | collective-permute-start | bytes 165896 | tf_op jit(solution)/shard_map/ppermute | solution.py:418

commit v3 on v2

v3 whole, which is shorter than its diff:
```python
import math

import jax
import jax.numpy as jnp
from jax import lax
from jax.experimental import pallas as pl
from jax.experimental.pallas import tpu as pltpu
from jax.sharding import PartitionSpec as P

BLK = 4
CLASSES = 8
NX = 16
NY = 16
NZ = 768
STRIP = 48
HALF = STRIP // 2
CHUNK = 128
MID = 8
FACES_MIB = 4
INTERIOR_MIB = 4

TIME_STEP = 0.15
SIGMA_LONG = 1.0
SIGMA_CROSS = 0.3
SLOPES = (8.0, -8.0, 6.0, 5.0, -5.0, -3.0)
MIDDLES = (0.2, 0.4, 0.3, 0.5, 0.6, 0.5)
RATES = (3.0, 0.5, 1.0, 0.8, 0.3, 0.1)
OPACITY = (0.012, 0.01)

f32 = jnp.float32


def params(mib):
    return pltpu.CompilerParams(vmem_limit_bytes=mib * 2**20)


def is_even(axis):
    return lax.rem(lax.axis_index(axis), 2) == 0


def lane_spread(count):
    row = lax.broadcasted_iota(jnp.int32, (count, count * BLK), 0)
    column = lax.broadcasted_iota(jnp.int32, (count, count * BLK), 1)
    return row == lax.shift_right_logical(column, 2)


def flat(ref):
    return jnp.concatenate([ref[k] for k in range(NX // BLK)], axis=0)


def spread_y(wide, start):
    row = lax.broadcasted_iota(jnp.int32, (NY, 1), 0)
    out = jnp.broadcast_to(wide[start:start + 1], (NY, wide.shape[1]))
    for k in range(1, NY // BLK):
        out = jnp.where(row >= BLK * k, wide[start + k:start + k + 1], out)
    return out


def choose(first, a, b):
    return jnp.where(first, a, b)


def faces_kernel(tissue_ref, states_ref, u_ref, ev_ref, od_ref, v_s, sem):
    load = pltpu.make_async_copy(states_ref.at[0], v_s, sem)
    load.start()
    wide = jnp.dot(flat(tissue_ref).astype(f32).astype(jnp.bfloat16),
                   lane_spread(NZ // BLK).astype(jnp.bfloat16), preferred_element_type=f32)
    masks = [spread_y(wide, BLK * block) for block in range(NX // BLK)]
    load.wait()
    for x in range(NX):
        u_ref[x] = v_s[x] * masks[x // BLK]
    area_rows(u_ref, ev_ref, od_ref)


def area_rows(u_ref, ev_ref, od_ref):
    even = is_even("area")
    for x in range(NX):
        low = u_ref[x, 0:1]
        high = u_ref[x, NY - 1:NY]
        ev_ref[x:x + 1] = choose(even, high, low)
        od_ref[x:x + 1] = choose(even, low, high)


def class_tables():
    spread = SIGMA_LONG - SIGMA_CROSS
    tables = [[] for _ in range(6)]
    for kind in range(CLASSES):
        polar = math.pi * (kind + 0.5) / CLASSES
        azimuth = 2.3 * kind
        f = (math.cos(polar), math.sin(polar) * math.cos(azimuth), math.sin(polar) * math.sin(azimuth))
        for k in range(3):
            tables[k].append(TIME_STEP * (SIGMA_CROSS + spread * f[k] * f[k]))
        for k, (a, b) in enumerate(((0, 1), (0, 2), (1, 2))):
            tables[3 + k].append(0.5 * TIME_STEP * spread * f[a] * f[b])
    return tables


def coefs_kernel(tissue_ref, fiber_ref, out_ref):
    kind = flat(fiber_ref)
    parts = [flat(tissue_ref).astype(f32)]
    for table in class_tables():
        part = jnp.full(kind.shape, table[0], f32)
        for c in range(1, CLASSES):
            part = jnp.where(kind == c, table[c], part)
        parts.append(part)
    rest = jnp.concatenate(parts, axis=0)
    onehot = lane_spread(NZ // BLK).astype(jnp.bfloat16)
    wide = None
    for _ in range(3):
        piece = rest.astype(jnp.bfloat16)
        rest = rest - piece.astype(f32)
        product = jnp.dot(piece, onehot, preferred_element_type=f32)
        wide = product if wide is None else wide + product
    for k in range(7):
        for block in range(4):
            out_ref[k, NY * block:NY * (block + 1)] = spread_y(wide, 16 * k + 4 * block)


def message_kernel(area_ev_ref, area_od_ref, u_ref, ev_ref, od_ref):
    area_even = is_even("area")
    depth_even = is_even("depth")
    ev_ref[0:NY] = choose(depth_even, u_ref[NX - 1], u_ref[0])
    od_ref[0:NY] = choose(depth_even, u_ref[0], u_ref[NX - 1])
    for place, first, second in ((NY, area_od_ref, area_ev_ref), (NY + 1, area_ev_ref, area_od_ref)):
        low = choose(area_even, first[0:1], second[0:1])
        high = choose(area_even, first[NX - 1:NX], second[NX - 1:NX])
        ev_ref[place:place + 1] = choose(depth_even, high, low)
        od_ref[place:place + 1] = choose(depth_even, low, high)


def z_sides(u):
    lane = lax.broadcasted_iota(jnp.int32, (1, NZ), 1)
    after = jnp.where(lane == NZ - 1, 0.0, pltpu.roll(u, NZ - 1, axis=1))
    before = jnp.where(lane == 0, 0.0, pltpu.roll(u, 1, axis=1))
    return after, before


def y_sides(u, row_lo, row_hi):
    row = lax.broadcasted_iota(jnp.int32, (NY, 1), 0)
    after = jnp.where(row == NY - 1, row_hi, pltpu.roll(u, NY - 1, axis=0))
    before = jnp.where(row == 0, row_lo, pltpu.roll(u, 1, axis=0))
    return after, before


def derive(planes, u_ref, coefs_ref, ev_ref, od_ref, uy_ref, uz_ref, w_ref):
    even = is_even("area")
    row_lo = choose(even, od_ref[...], ev_ref[...])
    row_hi = choose(even, ev_ref[...], od_ref[...])
    after, before = z_sides(row_lo)
    rowz_lo = after - before
    after, before = z_sides(row_hi)
    rowz_hi = after - before
    for x in planes:
        rows = slice(x // BLK * NY, x // BLK * NY + NY)
        row = slice(x, x + 1)
        u = u_ref[x]
        after, before = z_sides(u)
        uz = after - before
        uz_ref[x] = uz
        w = 0.52 * u + coefs_ref[3, rows] * (after + before)
        after, before = y_sides(u, row_lo[row], row_hi[row])
        uy_ref[x] = after - before
        w = w + coefs_ref[2, rows] * (after + before)
        after, before = y_sides(uz, rowz_lo[row], rowz_hi[row])
        w_ref[x] = w + coefs_ref[6, rows] * (after - before)


def ionic(w, gates, calcium):
    fresh = []
    for k in range(6):
        keep = math.exp(-TIME_STEP * RATES[k])
        half = 0.5 * (1.0 - keep)
        t = jnp.tanh((0.5 * SLOPES[k]) * w - (0.5 * SLOPES[k] * MIDDLES[k]))
        fresh.append(half * t + (keep * gates[k] + half))
    both = fresh[3] * fresh[4]
    cube = fresh[0] * fresh[0] * fresh[0]
    loss = (
        (2.0 * TIME_STEP) * (cube * fresh[1]) * (w - 1.2)
        + TIME_STEP * (fresh[2] * fresh[2]) * (w + 0.1)
        + (0.6 * TIME_STEP) * both * (w - 0.9)
        + (0.2 * TIME_STEP) * (1.0 + fresh[5]) * (w - 0.05)
    )
    gain = (1.5 * TIME_STEP) * both
    calc_next = (1.0 - 0.8 * TIME_STEP) * calcium + gain * (1.0 - calcium)
    return w - loss, fresh, calc_next


def march(q, opaque, state):
    passed, red, green = state
    alpha = opaque * jnp.tanh(3.0 * q - 1.2) + opaque
    weight = passed * alpha
    off = q - 0.5
    red = red + weight * jnp.tanh(2.5 * off)
    green = green + weight * jnp.exp(-6.0 * (off * off))
    return passed - weight, red, green


def advance(w, old, inside):
    volt, fresh, calc = ionic(w, old[1:7], old[7])
    return [jnp.where(inside, a, b) for a, b in zip([volt] + fresh + [calc], old)]


def show(new, m, marches):
    return [march(q, (0.5 * OPACITY[f]) * m, marches[f]) for f, q in enumerate((new[0], new[7]))]


def interior_planes(planes, marches_of, s_ref, u_ref, next_ref, coefs_ref, uy_ref, uz_ref, w_ref, shown_ref):
    def chunk(j, carry):
        cols = pl.ds(pl.multiple_of(j * CHUNK, CHUNK), CHUNK)
        marches = marches_of(cols)
        for x in planes:
            rows = slice(x // BLK * NY, x // BLK * NY + NY)
            m = coefs_ref[0, rows, cols]
            w = (
                w_ref[x, :, cols]
                + coefs_ref[1, rows, cols] * (u_ref[x + 1, :, cols] + u_ref[x - 1, :, cols])
                + coefs_ref[4, rows, cols] * (uy_ref[x + 1, :, cols] - uy_ref[x - 1, :, cols])
                + coefs_ref[5, rows, cols] * (uz_ref[x + 1, :, cols] - uz_ref[x - 1, :, cols])
            )
            new = advance(w, [s_ref[k, x, :, cols] for k in range(8)], m > 0.5)
            for k in range(8):
                s_ref[k, x, :, cols] = new[k]
            next_ref[x, :, cols] = m * new[0]
            marches = show(new, m, marches)
        for f in range(2):
            for k in range(3):
                shown_ref[3 * f + k, :, cols] = marches[f][k]
        return carry

    lax.fori_loop(0, NZ // CHUNK, chunk, 0)


def base_of(x, beside, sign, u_ref, coefs_ref, uy_ref, uz_ref, w_ref):
    rows = slice(x // BLK * NY, x // BLK * NY + NY)
    return (
        w_ref[x]
        + coefs_ref[1, rows] * u_ref[beside]
        + sign * (coefs_ref[4, rows] * uy_ref[beside] + coefs_ref[5, rows] * uz_ref[beside])
    )


def front_body(last, refs):
    states_ref, u_ref, coefs_ref, area_ev_ref, area_od_ref, _ = refs[:6]
    s_ref, next_ref, uy_ref, uz_ref, w_ref, shown_ref, base_ref, _ = refs[6:14]
    loads = []
    if last:
        final_ref, sem = refs[14:]
    else:
        (sem,) = refs[14:]
        for k in range(2):
            half = pl.ds(k * MID, MID)
            loads.append(pltpu.make_async_copy(states_ref.at[:, half], s_ref.at[:, half], sem.at[k]))
            loads[k].start()
    derive(range(MID + 1), u_ref, coefs_ref, area_ev_ref, area_od_ref, uy_ref, uz_ref, w_ref)
    base_ref[...] = base_of(0, 1, 1.0, u_ref, coefs_ref, uy_ref, uz_ref, w_ref)
    if not last:
        loads[0].wait()
    one = jnp.ones((NY, CHUNK), f32)
    zero = jnp.zeros((NY, CHUNK), f32)
    interior_planes(range(1, MID), lambda cols: [(one, zero, zero)] * 2,
                    s_ref, u_ref, next_ref, coefs_ref, uy_ref, uz_ref, w_ref, shown_ref)
    if last:
        done = pl.ds(1, MID - 1)
        store = pltpu.make_async_copy(s_ref.at[:, done], final_ref.at[:, done], sem)
        store.start()
        store.wait()
    else:
        loads[1].wait()


def back_body(last, refs):
    u_ref, coefs_ref, area_ev_ref, area_od_ref = refs[:4]
    outs = refs[11:] if last else refs[10:]
    s_ref, next_ref, uy_ref, uz_ref, w_ref, shown_ref, base_ref = outs[:7]
    derive(range(MID + 1, NX), u_ref, coefs_ref, area_ev_ref, area_od_ref, uy_ref, uz_ref, w_ref)
    base_ref[...] = base_of(NX - 1, NX - 2, -1.0, u_ref, coefs_ref, uy_ref, uz_ref, w_ref)
    interior_planes(range(MID, NX - 1),
                    lambda cols: [tuple(shown_ref[3 * f + k, :, cols] for k in range(3)) for f in range(2)],
                    s_ref, u_ref, next_ref, coefs_ref, uy_ref, uz_ref, w_ref, shown_ref)
    if last:
        final_ref, sem = outs[7:]
        done = pl.ds(MID, NX - 1 - MID)
        store = pltpu.make_async_copy(s_ref.at[:, done], final_ref.at[:, done], sem)
        store.start()
        store.wait()


def ends_body(last, refs):
    base_lo_ref, base_hi_ref, coefs_ref, depth_ev_ref, depth_od_ref, shown_ref = refs[:6]
    if last:
        earlier_ref, _, _, s_ref, final_ref, strips_ref, acc_s, uy_s, uz_s, sem = refs[6:]
    else:
        _, _, s_ref, next_ref, acc_s, ev_ref, od_ref, uy_s, uz_s = refs[6:]
    even = is_even("depth")
    stores = []
    for end, x, base_ref, sign in ((0, 0, base_lo_ref, -1.0), (1, NX - 1, base_hi_ref, 1.0)):
        if end == 1:
            use_ev = even
        else:
            use_ev = jnp.logical_not(even)
        rows = slice(x // BLK * NY, x // BLK * NY + NY)
        halo = choose(use_ev, depth_ev_ref[...], depth_od_ref[...])
        u = halo[0:NY]
        after, before = z_sides(u)
        uz_s[...] = sign * (after - before)
        after, before = y_sides(u, halo[NY:NY + 1], halo[NY + 1:NY + 2])
        uy_s[...] = sign * (after - before)
        for j in range(NZ // CHUNK):
            cols = slice(j * CHUNK, (j + 1) * CHUNK)
            m = coefs_ref[0, rows, cols]
            w = (
                base_ref[:, cols]
                + coefs_ref[1, rows, cols] * u[:, cols]
                + coefs_ref[4, rows, cols] * uy_s[:, cols]
                + coefs_ref[5, rows, cols] * uz_s[:, cols]
            )
            new = advance(w, [s_ref[k, x, :, cols] for k in range(8)], m > 0.5)
            for k in range(8):
                s_ref[k, x, :, cols] = new[k]
            if not last:
                next_ref[x, :, cols] = m * new[0]
            if end == 0:
                one = jnp.ones((NY, CHUNK), f32)
                zero = jnp.zeros((NY, CHUNK), f32)
                marches = show(new, m, [(one, zero, zero)] * 2)
            else:
                marches = [tuple(acc_s[3 * f + k, :, cols] for k in range(3)) for f in range(2)]
                marches = show(new, m, marches)
            for f in range(2):
                passed, red, green = marches[f]
                if end == 0:
                    red = red + passed * shown_ref[3 * f + 1, :, cols]
                    green = green + passed * shown_ref[3 * f + 2, :, cols]
                    passed = passed * shown_ref[3 * f, :, cols]
                for k, item in enumerate((passed, red, green)):
                    acc_s[3 * f + k, :, cols] = item
        if last:
            stores.append(pltpu.make_async_copy(s_ref.at[:, x], final_ref.at[:, x], sem.at[end]))
            stores[end].start()
    if not last:
        area_rows(next_ref, ev_ref, od_ref)
    else:
        for k in range(3):
            stack = jnp.concatenate(
                [earlier_ref[k], earlier_ref[3 + k], acc_s[k], acc_s[3 + k]], axis=0)
            stack = jnp.concatenate([stack, pltpu.roll(stack, NZ - HALF, axis=1)], axis=0)
            turned = stack.T
            for d in range(NZ // STRIP):
                strips_ref[d, HALF * k:HALF * (k + 1)] = turned[STRIP * d:STRIP * d + HALF]
        for store in stores:
            store.wait()


def composite_kernel(strips_ref, out_ref):
    count = strips_ref.shape[0]
    passed = jnp.ones((HALF, 128), f32)
    red = jnp.zeros((HALF, 128), f32)
    green = jnp.zeros((HALF, 128), f32)
    for s in range(count):
        red = red + passed * strips_ref[s, HALF:2 * HALF]
        green = green + passed * strips_ref[s, 2 * HALF:3 * HALF]
        passed = passed * strips_ref[s, 0:HALF]
    solid = 1.0 - passed
    red = 0.5 * (solid + red)
    whole = jnp.concatenate([red, green, solid - red, solid, jnp.zeros((32, 128), f32)], axis=0)
    turned = whole.T
    first, second = turned[0:64], turned[64:128]
    lane = lax.broadcasted_iota(jnp.int32, (1, 128), 1)
    for c in range(4):
        a = pltpu.roll(first, (128 - HALF * c) % 128, axis=1) if c else first
        b = pltpu.roll(second, (128 + HALF - HALF * c) % 128, axis=1) if c != 1 else second
        o = jnp.where(lane < HALF, a, b)
        for k in range(4):
            out_ref[k // 2, k % 2, c] = o[NY * k:NY * (k + 1), 0:STRIP]


VOLUME = (8, NX, NY, NZ)
FIELD = (NX, NY, NZ)
PLANE = (NY, NZ)
SHOWN = (6, NY, NZ)
COPY = pltpu.SemaphoreType.DMA


def shapes_of(*shapes):
    return [jax.ShapeDtypeStruct(s, f32) for s in shapes]


def kept_in(space, *shapes):
    return [space(s, f32) for s in shapes]


def anywhere():
    return pl.BlockSpec(memory_space=pl.ANY)


def inside():
    return pl.BlockSpec(memory_space=pltpu.VMEM)


def cost():
    voxels = NX * NY * NZ // 2
    return pl.CostEstimate(flops=400 * voxels, bytes_accessed=32 * voxels, transcendentals=12 * voxels)


def interior_front(last, states, u, coefs, area, passing):
    out_shape = kept_in(pltpu.VMEM, VOLUME, FIELD, FIELD, FIELD, FIELD, SHOWN, PLANE) + shapes_of(passing.shape)
    out_specs = [inside()] * 7 + [anywhere()]
    aliases = {5: 7}
    if last:
        aliases[0] = 0
        out_shape += kept_in(pltpu.HBM, VOLUME)
        out_specs += [anywhere()]
        scratch = [COPY]
    else:
        scratch = [COPY((2,))]
    return pl.pallas_call(
        lambda *refs: front_body(last, refs),
        in_specs=[inside() if last else anywhere()] + [inside()] * 4 + [anywhere()],
        out_specs=out_specs,
        out_shape=out_shape,
        scratch_shapes=scratch,
        input_output_aliases=aliases,
        compiler_params=params(INTERIOR_MIB),
        cost_estimate=cost(),
        name="front_last" if last else "front_first",
    )(states, u, coefs, *area, passing)


def interior_back(last, u, coefs, area, kept):
    out_shape = kept_in(pltpu.VMEM, VOLUME, FIELD, FIELD, FIELD, FIELD, SHOWN, PLANE)
    out_specs = [inside()] * 7
    in_specs = [inside()] * 10
    aliases = {4 + k: k for k in range(6)}
    scratch = []
    if last:
        in_specs += [anywhere()]
        out_shape += kept_in(pltpu.HBM, VOLUME)
        out_specs += [anywhere()]
        aliases[10] = 7
        scratch = [COPY]
    return pl.pallas_call(
        lambda *refs: back_body(last, refs),
        in_specs=in_specs,
        out_specs=out_specs,
        out_shape=out_shape,
        scratch_shapes=scratch,
        input_output_aliases=aliases,
        compiler_params=params(INTERIOR_MIB),
        cost_estimate=cost(),
        name="back_last" if last else "back_first",
    )(u, coefs, *area, *kept)


def ends(last, bases, coefs, depth, shown, rest):
    args = [*bases, coefs, *depth, shown, *rest]
    in_specs = [inside()] * len(args)
    if last:
        in_specs[-1] = anywhere()
        out_shape = kept_in(pltpu.VMEM, VOLUME) + kept_in(pltpu.HBM, VOLUME) + shapes_of((NZ // STRIP, 3 * HALF, 128))
        out_specs = [inside(), anywhere(), inside()]
        scratch = [pltpu.VMEM(SHOWN, f32)]
    else:
        out_shape = kept_in(pltpu.VMEM, VOLUME, FIELD, SHOWN, (NX, NZ), (NX, NZ))
        out_specs = [inside()] * 5
        scratch = []
    scratch += [pltpu.VMEM(PLANE, f32)] * 2
    if last:
        scratch += [COPY((2,))]
    return pl.pallas_call(
        lambda *refs: ends_body(last, refs),
        in_specs=in_specs,
        out_specs=out_specs,
        out_shape=out_shape,
        scratch_shapes=scratch,
        input_output_aliases={len(args) - 2: 0, len(args) - 1: 1},
        compiler_params=params(4),
        name="ends_last" if last else "ends_first",
    )(*args)


def depth_messages(area, u):
    return pl.pallas_call(
        message_kernel,
        out_shape=shapes_of((NY + 2, NZ), (NY + 2, NZ)),
        compiler_params=params(1),
        name="depth_message",
    )(*area, u)


def swaps(axis):
    count = lax.axis_size(axis)
    even = [(i, i ^ 1) for i in range(count) if i ^ 1 < count]
    odd = [(i, ((i - 1) ^ 1) + 1) for i in range(1, count) if ((i - 1) ^ 1) + 1 < count]
    return even, odd


def swap(axis, which, message):
    return lax.ppermute(message, axis, swaps(axis)[which])


def half_step(last, states, u, coefs, area):
    messages = depth_messages(area, u)
    even = swap("depth", 0, messages[0])
    states, after, uy, uz, w, shown, low, passing, *final = interior_front(
        last, states, u, coefs, area, messages[1])
    odd = swap("depth", 1, passing)
    kept = (states, after, uy, uz, w, shown, *final)
    states, after, _, _, _, shown, high, *final = interior_back(last, u, coefs, area, kept)
    return states, after, shown, (low, high), (even, odd), final


def per_device(states, tissue, fiber):
    states = pltpu.with_memory_space_constraint(states, pltpu.HBM)
    u, ev, od = pl.pallas_call(
        faces_kernel,
        in_specs=[inside(), anywhere()],
        out_shape=kept_in(pltpu.VMEM, FIELD, (NX, NZ), (NX, NZ)),
        scratch_shapes=[pltpu.VMEM(FIELD, f32), COPY],
        compiler_params=params(FACES_MIB),
        name="faces",
    )(tissue, states)
    area = swap("area", 0, ev), swap("area", 1, od)
    coefs = pl.pallas_call(
        coefs_kernel,
        out_shape=jax.ShapeDtypeStruct((7, 64, NZ), f32),
        compiler_params=params(4),
        name="coefficients",
    )(tissue, fiber)
    states, u, shown, bases, depth, _ = half_step(False, states, u, coefs, area)
    states, u, images, ev, od = ends(False, bases, coefs, depth, shown, (states, u))
    area = swap("area", 0, ev), swap("area", 1, od)
    states, _, shown, bases, depth, final = half_step(True, states, u, coefs, area)
    _, states, strips = ends(True, bases, coefs, depth, shown, (images, states, final[0]))
    strips = lax.all_to_all(strips, "depth", split_axis=0, concat_axis=0, tiled=True)
    images = pl.pallas_call(
        composite_kernel,
        out_shape=jax.ShapeDtypeStruct((2, 2, 4, NY, STRIP), f32),
        compiler_params=params(4),
        name="composite",
    )(strips)
    return states, images


def solution(mesh):
    return jax.shard_map(
        per_device,
        mesh=mesh,
        in_specs=(
            P(None, "depth", "area", None),
            P("depth", "area", None),
            P("depth", "area", None),
        ),
        out_specs=(P(None, "depth", "area", None), P(None, None, None, "area", "depth")),
        check_vma=False,
    )
```

time: 66.7 us -> 62 us (0.930)
  Pallas kernels: 20.2 us -> 16.6 us
  local copies, waits for them, and re-layouts: 3.69 us -> 0.71 us
  blocking collectives: 21.1 us -> 23 us
    pallas_call x7 -> x9, Pallas kernels: 18.8 us -> 15.3 us  [the longest x2 6.93 us: interior_front(): pl.pallas_call(lambda *refs: front_body(last, refs), in_specs=[inside() i...]
    unnamed x12 -> x4, local copies, waits for them, and re-layouts: 3.69 us -> 0.71 us
    all_to_all x1, blocking collectives: 21.1 us -> 23 us  [per_device(): lax.all_to_all(strips, 'depth', split_axis=0, concat_axis=0, tiled=True)]
where the time goes in v3:
time: 62 us; the launch traced here: 61.6 us
  blocking collectives  23 us (37%)
  starting transfers between devices  17.2 us (28%)
  Pallas kernels  16.6 us (27%)
  waiting for transfers between devices  3.27 us (5%)
  between operations  0.81 us (1%)
  local copies, waits for them, and re-layouts  0.71 us (1%)
    all_to_all x1, blocking collectives, per_device(): lax.all_to_all(strips, 'depth', split_axis=0, concat_axis=0, tiled=True)  23 us
    ppermute x8, starting transfers between devices, swap(): return lax.ppermute(message, axis, swaps(axis)[which])  17.2 us
    pallas_call x2, Pallas kernels, interior_front(): pl.pallas_call(lambda *refs: front_body(last, refs), in_specs=[inside() i...  6.93 us
    pallas_call x2, Pallas kernels, interior_back(): pl.pallas_call(lambda *refs: back_body(last, refs), in_specs=in_specs, ou...  5.34 us
    ppermute x8, waiting for transfers between devices, swap(): return lax.ppermute(message, axis, swaps(axis)[which])  3.27 us
    pallas_call x2, Pallas kernels, ends(): pl.pallas_call(lambda *refs: ends_body(last, refs), in_specs=in_specs, ou...  1.78 us
    pallas_call x1, Pallas kernels, per_device(): pl.pallas_call(faces_kernel, in_specs=[inside(), anywhere()], out_shape=k...  1.24 us
  transfers between devices with their start and end apart: 8, of which 2 were waited for; matrix products, arithmetic and copies ran while one was open for 0% of the time, Pallas kernels for 21%

profile of v3, /device:TPU:97, one launch (start us, length us, event | category | flops | bytes accessed | tf_op | source)
XLA Modules:
  0.0 61.6 jit_solution(5520475008457831411)
XLA Ops:
  0.6 0.0 copy-start
  0.6 0.7 %copy-done = s32[4,4,192]{2,1,0:T(4,128)S(1)} copy-done((s32[4,4,192]{2,1,0:T(4,128)S(1)}, s32[4,4,192]{2,1,0:T(4,128)}, u32[]{:S(2)}) %copy-start) | copy-done | bytes 12312
  1.3 0.0 copy-start.1
  1.4 1.2 %faces.1 = (f32[16,16,768]{2,1,0:T(8,128)S(1)}, f32[16,768]{1,0:T(8,128)S(1)}, f32[16,768]{1,0:T(8,128)S(1)}) custom-call(s32[4,4,192]{2,1,0:T(4,128)S(1)} %copy-done, f32[8,16,16,768]{3,2,1,0:T(8,128)} %refs_0_.1), custom_call_target="tpu_custom_call" | custom-call | tf_op jit(solution)/shard_map/faces/pallas_call | solution.py:514
  2.6 0.8 %collective-permute-start = (f32[16,768]{1,0:T(8,128)S(1)}, f32[16,768]{1,0:T(8,128)S(1)}, u32[]{:S(2)}, u32[]{:S(2)}) collective-permute-start(f32[16,768]{1,0:T(8,128)S(1)} %get-tuple-element.42), channel_id=1, source_target_pairs={{0,1},{1,0},{2,3},{3,2},{4,5},{5,4},{6,7},{7,6},{8,9},{9,8},{10,11... | collective-permute-start | bytes 147464 | tf_op jit(solution)/shard_map/ppermute | solution.py:498
  3.4 4.7 %collective-permute-start.1 = (f32[16,768]{1,0:T(8,128)S(1)}, f32[16,768]{1,0:T(8,128)S(1)}, u32[]{:S(2)}, u32[]{:S(2)}) collective-permute-start(f32[16,768]{1,0:T(8,128)S(1)} %get-tuple-element.43), channel_id=1, source_target_pairs={{1,2},{2,1},{3,4},{4,3},{5,6},{6,5},{7,8},{8,7},{9,10},{10,9},{11,... | collective-permute-start | bytes 147464 | tf_op jit(solution)/shard_map/ppermute | solution.py:498
  8.0 0.0 copy-done.1
  8.0 0.4 coefficients.1.refs_2_.refs_1_
  8.4 0.0 collective-permute-done.area_ev_ref.refs_3_.refs_2_
  8.5 1.5 %collective-permute-done.1.area_od_ref.refs_4_.refs_3_ = f32[16,768]{1,0:T(8,128)S(1)} collective-permute-done((f32[16,768]{1,0:T(8,128)S(1)}, f32[16,768]{1,0:T(8,128)S(1)}, u32[]{:S(2)}, u32[]{:S(2)}) %collective-permute-start.1) | collective-permute-done | bytes 49184 | tf_op jit(solution)/shard_map/ppermute | solution.py:498
  10.0 1.3 %collective-permute-start.2 = (f32[18,768]{1,0:T(8,128)S(1)}, f32[18,768]{1,0:T(8,128)S(1)}, u32[]{:S(2)}, u32[]{:S(2)}) collective-permute-start(f32[18,768]{1,0:T(8,128)S(1)} %get-tuple-element.53), channel_id=1, source_target_pairs={{0,16},{16,0},{32,48},{48,32},{64,80},{80,64},{96,112},{112,96},{1... | collective-permute-start | bytes 165896 | tf_op jit(solution)/shard_map/ppermute | solution.py:498
  11.3 3.4 %front_first.1 = (f32[8,16,16,768]{3,2,1,0:T(8,128)S(1)}, f32[16,16,768]{2,1,0:T(8,128)S(1)}, f32[16,16,768]{2,1,0:T(8,128)S(1)}, f32[16,16,768]{2,1,0:T(8,128)S...) custom-call(f32[8,16,16,768]{3,2,1,0:T(8,128)} %refs_0_.1, ...), custom_call_target="tpu_custom_call", output_to_operand_aliasing={{7}: (5, {})} | custom-call | flops 39321600 | bytes 3145728 | tf_op jit(solution)/shard_map/front_first/pallas_call | solution.py:416
  14.7 0.7 %collective-permute-start.3 = (f32[18,768]{1,0:T(8,128)S(1)}, f32[18,768]{1,0:T(8,128)S(1)}, u32[]{:S(2)}, u32[]{:S(2)}) collective-permute-start(f32[18,768]{1,0:T(8,128)S(1)} %get-tuple-element.54), channel_id=1, source_target_pairs={{16,32},{32,16},{48,64},{64,48},{80,96},{96,80},{112,128},{128,112... | collective-permute-start | bytes 165896 | tf_op jit(solution)/shard_map/ppermute | solution.py:498
  15.4 1.9 %back_first.1 = (f32[8,16,16,768]{3,2,1,0:T(8,128)S(1)}, f32[16,16,768]{2,1,0:T(8,128)S(1)}, f32[16,16,768]{2,1,0:T(8,128)S(1)}, f32[16,16,768]{2,1,0:T(8,128)S(...) custom-call(f32[16,16,768]{2,1,0:T(8,128)S(1)} %get-tuple-element.41, ...), custom_call_target="tpu_custom_call", output_to_operand_aliasing={{0}: (4, {}), {1}: (5, {}), {2}: (6, {}), {3}: (7, {}), {4}... | custom-call | flops 39321600 | bytes 3145728 | tf_op jit(solution)/shard_map/back_first/pallas_call | solution.py:441
  17.3 0.0 collective-permute-done.2.refs_3_
  17.3 0.0 collective-permute-done.3.refs_4_
  17.3 0.6 ends_first.1
  17.9 0.1 collective-permute-start.4
  18.0 5.0 %collective-permute-start.5 = (f32[16,768]{1,0:T(8,128)S(1)}, f32[16,768]{1,0:T(8,128)S(1)}, u32[]{:S(2)}, u32[]{:S(2)}) collective-permute-start(f32[16,768]{1,0:T(8,128)S(1)} %get-tuple-element.61), channel_id=1, source_target_pairs={{1,2},{2,1},{3,4},{4,3},{5,6},{6,5},{7,8},{8,7},{9,10},{10,9},{11,... | collective-permute-start | bytes 147464 | tf_op jit(solution)/shard_map/ppermute | solution.py:498
  22.9 0.0 collective-permute-done.4.area_ev_ref.refs_3_.refs_2_
  22.9 1.7 %collective-permute-done.5.area_od_ref.refs_4_.refs_3_ = f32[16,768]{1,0:T(8,128)S(1)} collective-permute-done((f32[16,768]{1,0:T(8,128)S(1)}, f32[16,768]{1,0:T(8,128)S(1)}, u32[]{:S(2)}, u32[]{:S(2)}) %collective-permute-start.5) | collective-permute-done | bytes 49184 | tf_op jit(solution)/shard_map/ppermute | solution.py:498
  24.7 4.1 %collective-permute-start.6 = (f32[18,768]{1,0:T(8,128)S(1)}, f32[18,768]{1,0:T(8,128)S(1)}, u32[]{:S(2)}, u32[]{:S(2)}) collective-permute-start(f32[18,768]{1,0:T(8,128)S(1)} %get-tuple-element.72), channel_id=1, source_target_pairs={{0,16},{16,0},{32,48},{48,32},{64,80},{80,64},{96,112},{112,96},{1... | collective-permute-start | bytes 165896 | tf_op jit(solution)/shard_map/ppermute | solution.py:498
  28.8 3.5 %front_last.1 = (f32[8,16,16,768]{3,2,1,0:T(8,128)S(1)}, f32[16,16,768]{2,1,0:T(8,128)S(1)}, f32[16,16,768]{2,1,0:T(8,128)S(1)}, f32[16,16,768]{2,1,0:T(8,128)S(...) custom-call(f32[8,16,16,768]{3,2,1,0:T(8,128)S(1)} %get-tuple-elemen, ...), custom_call_target="tpu_custom_call", output_to_operand_aliasing={{7}: (5, {}), {0}: (0, {})} | custom-call | flops 39321600 | bytes 3145728 | tf_op jit(solution)/shard_map/front_last/pallas_call | solution.py:416
  32.4 0.7 %collective-permute-start.7 = (f32[18,768]{1,0:T(8,128)S(1)}, f32[18,768]{1,0:T(8,128)S(1)}, u32[]{:S(2)}, u32[]{:S(2)}) collective-permute-start(f32[18,768]{1,0:T(8,128)S(1)} %get-tuple-element.73), channel_id=1, source_target_pairs={{16,32},{32,16},{48,64},{64,48},{80,96},{96,80},{112,128},{128,112... | collective-permute-start | bytes 165896 | tf_op jit(solution)/shard_map/ppermute | solution.py:498
  33.0 3.4 %back_last.1 = (f32[8,16,16,768]{3,2,1,0:T(8,128)S(1)}, f32[16,16,768]{2,1,0:T(8,128)S(1)}, f32[16,16,768]{2,1,0:T(8,128)S(1)}, f32[16,16,768]{2,1,0:T(8,128)S(1...) custom-call(f32[16,16,768]{2,1,0:T(8,128)S(1)} %get-tuple-element.59, ...), custom_call_target="tpu_custom_call", output_to_operand_aliasing={{0}: (4, {}), {1}: (5, {}), {2}: (6, {}), {3}: (7, {}), {4}... | custom-call | flops 39321600 | bytes 3145728 | tf_op jit(solution)/shard_map/back_last/pallas_call | solution.py:441
  36.5 0.0 collective-permute-done.6.refs_3_
  36.5 0.0 collective-permute-done.7.refs_4_
  36.5 1.2 %ends_last.1 = (f32[8,16,16,768]{3,2,1,0:T(8,128)S(1)}, f32[8,16,16,768]{3,2,1,0:T(8,128)}, f32[16,72,128]{2,1,0:T(8,128)S(1)}) custom-call(f32[16,768]{1,0:T(8,128)S(1)} %get-tuple-element.63.refs_0_, f32[16,768]{1,0:T(8,128)S(1)} %get-tuple-element.71.refs_1_, ...), custom_call_target="tpu_custom_call", output_to_operand_aliasing={{0}: (7, {}), {1}: (8, {})} | custom-call | tf_op jit(solution)/shard_map/ends_last/pallas_call | solution.py:469
  37.7 23.0 %all_to_all.5.strips_ref = f32[16,72,128]{2,1,0:T(8,128)S(1)} all-to-all(f32[16,72,128]{2,1,0:T(8,128)S(1)} %get-tuple-element.79), channel_id=1, replica_groups=mesh['depth'=16,'area'=16] {'depth'}, dimensions={0} | all-to-all | bytes 1179648 | tf_op jit(solution)/shard_map/all_to_all | solution.py:534
  60.7 0.9 %composite.1 = f32[2,2,4,16,48]{4,3,2,1,0:T(8,128)} custom-call(f32[16,72,128]{2,1,0:T(8,128)S(1)} %all_to_all.5.strips_ref), custom_call_target="tpu_custom_call" | custom-call | tf_op jit(solution)/shard_map/composite/pallas_call | solution.py:535
  (2 shorter events, 0.0 us)
Async XLA Ops:
  0.6 0.7 %copy-start = (s32[4,4,192]{2,1,0:T(4,128)S(1)}, s32[4,4,192]{2,1,0:T(4,128)}, u32[]{:S(2)}) copy-start(s32[4,4,192]{2,1,0:T(4,128)} %tissue_ref.3) | copy-start | bytes 36868
  1.3 6.7 %copy-start.1 = (s32[4,4,192]{2,1,0:T(4,128)S(1)}, s32[4,4,192]{2,1,0:T(4,128)}, u32[]{:S(2)}) copy-start(s32[4,4,192]{2,1,0:T(4,128)} %fiber_ref.1) | copy-start | bytes 36868
  2.6 5.9 %collective-permute-start = (f32[16,768]{1,0:T(8,128)S(1)}, f32[16,768]{1,0:T(8,128)S(1)}, u32[]{:S(2)}, u32[]{:S(2)}) collective-permute-start(f32[16,768]{1,0:T(8,128)S(1)} %get-tuple-element.42), channel_id=1, source_target_pairs={{0,1},{1,0},{2,3},{3,2},{4,5},{5,4},{6,7},{7,6},{8,9},{9,8},{10,11... | collective-permute-start | bytes 147464 | tf_op jit(solution)/shard_map/ppermute | solution.py:498
  3.4 6.6 %collective-permute-start.1 = (f32[16,768]{1,0:T(8,128)S(1)}, f32[16,768]{1,0:T(8,128)S(1)}, u32[]{:S(2)}, u32[]{:S(2)}) collective-permute-start(f32[16,768]{1,0:T(8,128)S(1)} %get-tuple-element.43), channel_id=1, source_target_pairs={{1,2},{2,1},{3,4},{4,3},{5,6},{6,5},{7,8},{8,7},{9,10},{10,9},{11,... | collective-permute-start | bytes 147464 | tf_op jit(solution)/shard_map/ppermute | solution.py:498
  10.0 7.3 %collective-permute-start.2 = (f32[18,768]{1,0:T(8,128)S(1)}, f32[18,768]{1,0:T(8,128)S(1)}, u32[]{:S(2)}, u32[]{:S(2)}) collective-permute-start(f32[18,768]{1,0:T(8,128)S(1)} %get-tuple-element.53), channel_id=1, source_target_pairs={{0,16},{16,0},{32,48},{48,32},{64,80},{80,64},{96,112},{112,96},{1... | collective-permute-start | bytes 165896 | tf_op jit(solution)/shard_map/ppermute | solution.py:498
  14.7 2.6 %collective-permute-start.3 = (f32[18,768]{1,0:T(8,128)S(1)}, f32[18,768]{1,0:T(8,128)S(1)}, u32[]{:S(2)}, u32[]{:S(2)}) collective-permute-start(f32[18,768]{1,0:T(8,128)S(1)} %get-tuple-element.54), channel_id=1, source_target_pairs={{16,32},{32,16},{48,64},{64,48},{80,96},{96,80},{112,128},{128,112... | collective-permute-start | bytes 165896 | tf_op jit(solution)/shard_map/ppermute | solution.py:498
  17.9 5.1 %collective-permute-start.4 = (f32[16,768]{1,0:T(8,128)S(1)}, f32[16,768]{1,0:T(8,128)S(1)}, u32[]{:S(2)}, u32[]{:S(2)}) collective-permute-start(f32[16,768]{1,0:T(8,128)S(1)} %get-tuple-element.60), channel_id=1, source_target_pairs={{0,1},{1,0},{2,3},{3,2},{4,5},{5,4},{6,7},{7,6},{8,9},{9,8},{10,11... | collective-permute-start | bytes 147464 | tf_op jit(solution)/shard_map/ppermute | solution.py:498
  18.0 6.7 %collective-permute-start.5 = (f32[16,768]{1,0:T(8,128)S(1)}, f32[16,768]{1,0:T(8,128)S(1)}, u32[]{:S(2)}, u32[]{:S(2)}) collective-permute-start(f32[16,768]{1,0:T(8,128)S(1)} %get-tuple-element.61), channel_id=1, source_target_pairs={{1,2},{2,1},{3,4},{4,3},{5,6},{6,5},{7,8},{8,7},{9,10},{10,9},{11,... | collective-permute-start | bytes 147464 | tf_op jit(solution)/shard_map/ppermute | solution.py:498
  24.7 11.8 %collective-permute-start.6 = (f32[18,768]{1,0:T(8,128)S(1)}, f32[18,768]{1,0:T(8,128)S(1)}, u32[]{:S(2)}, u32[]{:S(2)}) collective-permute-start(f32[18,768]{1,0:T(8,128)S(1)} %get-tuple-element.72), channel_id=1, source_target_pairs={{0,16},{16,0},{32,48},{48,32},{64,80},{80,64},{96,112},{112,96},{1... | collective-permute-start | bytes 165896 | tf_op jit(solution)/shard_map/ppermute | solution.py:498
  32.4 4.1 %collective-permute-start.7 = (f32[18,768]{1,0:T(8,128)S(1)}, f32[18,768]{1,0:T(8,128)S(1)}, u32[]{:S(2)}, u32[]{:S(2)}) collective-permute-start(f32[18,768]{1,0:T(8,128)S(1)} %get-tuple-element.73), channel_id=1, source_target_pairs={{16,32},{32,16},{48,64},{64,48},{80,96},{96,80},{112,128},{128,112... | collective-permute-start | bytes 165896 | tf_op jit(solution)/shard_map/ppermute | solution.py:498

commit v4 on v3

--- a/solution.py
+++ b/solution.py
@@ -16,8 +16,8 @@
 HALF = STRIP // 2
 CHUNK = 128
 MID = 8
-FACES_MIB = 4
-INTERIOR_MIB = 4
+GATES = 6
+RECORD = GATES * NX + 2 * (NX // BLK)
 
 TIME_STEP = 0.15
 SIGMA_LONG = 1.0
@@ -60,25 +60,34 @@
     return jnp.where(first, a, b)
 
 
-def faces_kernel(tissue_ref, states_ref, u_ref, ev_ref, od_ref, v_s, sem):
-    load = pltpu.make_async_copy(states_ref.at[0], v_s, sem)
-    load.start()
-    wide = jnp.dot(flat(tissue_ref).astype(f32).astype(jnp.bfloat16),
-                   lane_spread(NZ // BLK).astype(jnp.bfloat16), preferred_element_type=f32)
+def neighbours(axis, ev, od):
+    even = is_even(axis)
+    place = lax.axis_index(axis)
+    below = jnp.where(place == 0, 0.0, choose(even, od, ev))
+    above = jnp.where(place == lax.axis_size(axis) - 1, 0.0, choose(even, ev, od))
+    return below, above
+
+
+def faces_kernel(tissue_ref, states_ref, u_ref, ev_ref, od_ref, own_ref, tissue_s, v_s, sem):
+    loads = [pltpu.make_async_copy(tissue_ref, tissue_s, sem.at[0]),
+             pltpu.make_async_copy(states_ref.at[0], v_s, sem.at[1])]
+    for load in loads:
+        load.start()
+    onehot = lane_spread(NZ // BLK).astype(jnp.bfloat16)
+    loads[0].wait()
+    wide = jnp.dot(flat(tissue_s).astype(f32).astype(jnp.bfloat16), onehot, preferred_element_type=f32)
     masks = [spread_y(wide, BLK * block) for block in range(NX // BLK)]
-    load.wait()
+    even = is_even("area")
+    loads[1].wait()
     for x in range(NX):
-        u_ref[x] = v_s[x] * masks[x // BLK]
-    area_rows(u_ref, ev_ref, od_ref)
-
-
-def area_rows(u_ref, ev_ref, od_ref):
-    even = is_even("area")
-    for x in range(NX):
-        low = u_ref[x, 0:1]
-        high = u_ref[x, NY - 1:NY]
-        ev_ref[x:x + 1] = choose(even, high, low)
-        od_ref[x:x + 1] = choose(even, low, high)
+        u = v_s[x] * masks[x // BLK]
+        u_ref[x] = u
+        own_ref[0, x:x + 1] = u[0:1]
+        own_ref[1, x:x + 1] = u[NY - 1:NY]
+        ev_ref[NX + x:NX + x + 1] = choose(even, u[NY - 2:NY - 1], u[1:2])
+        od_ref[NX + x:NX + x + 1] = choose(even, u[1:2], u[NY - 2:NY - 1])
+    ev_ref[0:NX] = choose(even, own_ref[1], own_ref[0])
+    od_ref[0:NX] = choose(even, own_ref[0], own_ref[1])
 
 
 def class_tables():
@@ -95,7 +104,9 @@
     return tables
 
 
-def coefs_kernel(tissue_ref, fiber_ref, out_ref):
+def load_kernel(tissue_ref, fiber_ref, states_ref, _after, s_ref, coefs_ref, ev_ref, od_ref, sem):
+    load = pltpu.make_async_copy(states_ref, s_ref, sem)
+    load.start()
     kind = flat(fiber_ref)
     parts = [flat(tissue_ref).astype(f32)]
     for table in class_tables():
@@ -103,6 +114,7 @@
         for c in range(1, CLASSES):
             part = jnp.where(kind == c, table[c], part)
         parts.append(part)
+    parts.append(kind.astype(f32))
     rest = jnp.concatenate(parts, axis=0)
     onehot = lane_spread(NZ // BLK).astype(jnp.bfloat16)
     wide = None
@@ -113,19 +125,41 @@
         wide = product if wide is None else wide + product
     for k in range(7):
         for block in range(4):
-            out_ref[k, NY * block:NY * (block + 1)] = spread_y(wide, 16 * k + 4 * block)
-
-
-def message_kernel(area_ev_ref, area_od_ref, u_ref, ev_ref, od_ref):
-    area_even = is_even("area")
-    depth_even = is_even("depth")
-    ev_ref[0:NY] = choose(depth_even, u_ref[NX - 1], u_ref[0])
-    od_ref[0:NY] = choose(depth_even, u_ref[0], u_ref[NX - 1])
-    for place, first, second in ((NY, area_od_ref, area_ev_ref), (NY + 1, area_ev_ref, area_od_ref)):
-        low = choose(area_even, first[0:1], second[0:1])
-        high = choose(area_even, first[NX - 1:NX], second[NX - 1:NX])
-        ev_ref[place:place + 1] = choose(depth_even, high, low)
-        od_ref[place:place + 1] = choose(depth_even, low, high)
+            coefs_ref[k, NY * block:NY * (block + 1)] = spread_y(wide, 16 * k + 4 * block)
+    even = is_even("area")
+    for place, part in ((GATES * NX, 0), (GATES * NX + 4, 7)):
+        for block in range(4):
+            low = wide[16 * part + 4 * block:16 * part + 4 * block + 1]
+            high = wide[16 * part + 4 * block + 3:16 * part + 4 * block + 4]
+            ev_ref[place + block:place + block + 1] = choose(even, high, low)
+            od_ref[place + block:place + block + 1] = choose(even, low, high)
+    load.wait()
+    for k in range(GATES):
+        for x in range(NX):
+            place = NX * k + x
+            low = s_ref[k + 1, x, 0:1]
+            high = s_ref[k + 1, x, NY - 1:NY]
+            ev_ref[place:place + 1] = choose(even, high, low)
+            od_ref[place:place + 1] = choose(even, low, high)
+
+
+def message_kernel(area_ev_ref, area_od_ref, u_ref, _e, _o, ev_ref, od_ref, rows_ref, _gates_ev, _gates_od):
+    even = is_even("depth")
+    below, above = neighbours("area", area_ev_ref[...], area_od_ref[...])
+    rows_ref[0], rows_ref[2] = below[0:NX], below[NX:2 * NX]
+    rows_ref[1], rows_ref[3] = above[0:NX], above[NX:2 * NX]
+    depth_messages(even, u_ref, rows_ref, ev_ref, od_ref)
+
+
+def depth_messages(even, u_ref, rows_ref, ev_ref, od_ref):
+    low, high = u_ref[0], u_ref[NX - 1]
+    ev_ref[0:NY] = choose(even, high, low)
+    od_ref[0:NY] = choose(even, low, high)
+    for k in range(rows_ref.shape[0]):
+        place = NY + k
+        low, high = rows_ref[k, 0:1], rows_ref[k, NX - 1:NX]
+        ev_ref[place:place + 1] = choose(even, high, low)
+        od_ref[place:place + 1] = choose(even, low, high)
 
 
 def z_sides(u):
@@ -142,14 +176,21 @@
     return after, before
 
 
-def derive(planes, u_ref, coefs_ref, ev_ref, od_ref, uy_ref, uz_ref, w_ref):
-    even = is_even("area")
-    row_lo = choose(even, od_ref[...], ev_ref[...])
-    row_hi = choose(even, ev_ref[...], od_ref[...])
-    after, before = z_sides(row_lo)
-    rowz_lo = after - before
-    after, before = z_sides(row_hi)
-    rowz_hi = after - before
+def z_slope(u):
+    after, before = z_sides(u)
+    return after - before
+
+
+def y_slope(u, row_lo, row_hi):
+    after, before = y_sides(u, row_lo, row_hi)
+    return after - before
+
+
+def derive(planes, u_ref, coefs_ref, rows_ref, uy_ref, uz_ref, w_ref):
+    row_lo = rows_ref[0]
+    row_hi = rows_ref[1]
+    rowz_lo = z_slope(row_lo)
+    rowz_hi = z_slope(row_hi)
     for x in planes:
         rows = slice(x // BLK * NY, x // BLK * NY + NY)
         row = slice(x, x + 1)
@@ -239,72 +280,89 @@
     )
 
 
-def front_body(last, refs):
-    states_ref, u_ref, coefs_ref, area_ev_ref, area_od_ref, _ = refs[:6]
-    s_ref, next_ref, uy_ref, uz_ref, w_ref, shown_ref, base_ref, _ = refs[6:14]
-    loads = []
-    if last:
-        final_ref, sem = refs[14:]
-    else:
-        (sem,) = refs[14:]
-        for k in range(2):
-            half = pl.ds(k * MID, MID)
-            loads.append(pltpu.make_async_copy(states_ref.at[:, half], s_ref.at[:, half], sem.at[k]))
-            loads[k].start()
-    derive(range(MID + 1), u_ref, coefs_ref, area_ev_ref, area_od_ref, uy_ref, uz_ref, w_ref)
+def front_kernel(_s, u_ref, coefs_ref, rows_ref, _p,
+                 s_ref, next_ref, uy_ref, uz_ref, w_ref, shown_ref, base_ref, _passing):
+    derive(range(MID + 1), u_ref, coefs_ref, rows_ref, uy_ref, uz_ref, w_ref)
     base_ref[...] = base_of(0, 1, 1.0, u_ref, coefs_ref, uy_ref, uz_ref, w_ref)
-    if not last:
-        loads[0].wait()
     one = jnp.ones((NY, CHUNK), f32)
     zero = jnp.zeros((NY, CHUNK), f32)
     interior_planes(range(1, MID), lambda cols: [(one, zero, zero)] * 2,
                     s_ref, u_ref, next_ref, coefs_ref, uy_ref, uz_ref, w_ref, shown_ref)
-    if last:
+
+
+def back_kernel(u_ref, coefs_ref, rows_ref, _s, _n, _y, _z, _w, _a,
+                s_ref, next_ref, uy_ref, uz_ref, w_ref, shown_ref, base_ref, *storing):
+    if storing:
+        final_ref, sem = storing
         done = pl.ds(1, MID - 1)
         store = pltpu.make_async_copy(s_ref.at[:, done], final_ref.at[:, done], sem)
         store.start()
-        store.wait()
-    else:
-        loads[1].wait()
-
-
-def back_body(last, refs):
-    u_ref, coefs_ref, area_ev_ref, area_od_ref = refs[:4]
-    outs = refs[11:] if last else refs[10:]
-    s_ref, next_ref, uy_ref, uz_ref, w_ref, shown_ref, base_ref = outs[:7]
-    derive(range(MID + 1, NX), u_ref, coefs_ref, area_ev_ref, area_od_ref, uy_ref, uz_ref, w_ref)
+    derive(range(MID + 1, NX), u_ref, coefs_ref, rows_ref, uy_ref, uz_ref, w_ref)
     base_ref[...] = base_of(NX - 1, NX - 2, -1.0, u_ref, coefs_ref, uy_ref, uz_ref, w_ref)
     interior_planes(range(MID, NX - 1),
                     lambda cols: [tuple(shown_ref[3 * f + k, :, cols] for k in range(3)) for f in range(2)],
                     s_ref, u_ref, next_ref, coefs_ref, uy_ref, uz_ref, w_ref, shown_ref)
-    if last:
-        final_ref, sem = outs[7:]
-        done = pl.ds(MID, NX - 1 - MID)
-        store = pltpu.make_async_copy(s_ref.at[:, done], final_ref.at[:, done], sem)
-        store.start()
+    if storing:
         store.wait()
+
+
+def outer_row(side, halos, rows_ref, own_ref, record):
+    near, far, own = rows_ref[side], rows_ref[2 + side], own_ref[side]
+    turn = 1.0 if side else -1.0
+    near_place, far_place = NY + side, NY + 2 + side
+    own_place = NY - 1 if side else 0
+
+    def across(halo, place):
+        return halo[place:place + 1]
+
+    slope = turn * (far - own)
+    slopes = [turn * (across(h, far_place) - across(h, own_place)) for h in halos]
+    zs = [across(z_slope(h), near_place) for h in halos]
+    mask = spread_y(record[GATES * NX:GATES * NX + 4], 0)
+    kind = spread_y(record[GATES * NX + 4:GATES * NX + 8], 0)
+    coefs = []
+    for table in class_tables():
+        coef = jnp.full(kind.shape, table[0], f32)
+        for c in range(1, CLASSES):
+            coef = jnp.where(kind == float(c), table[c], coef)
+        coefs.append(coef)
+    x_after, x_before = y_sides(near, across(halos[0], near_place), across(halos[1], near_place))
+    z_after, z_before = z_sides(near)
+    w = (
+        0.52 * near
+        + coefs[0] * (x_after + x_before)
+        + coefs[1] * (own + far)
+        + coefs[2] * (z_after + z_before)
+        + coefs[3] * y_slope(slope, *slopes)
+        + coefs[4] * y_slope(z_after - z_before, *zs)
+        + coefs[5] * z_slope(slope)
+    )
+    gates = [record[NX * k:NX * (k + 1)] for k in range(GATES)]
+    return mask * ionic(w, gates, jnp.zeros_like(w))[0]
 
 
 def ends_body(last, refs):
     base_lo_ref, base_hi_ref, coefs_ref, depth_ev_ref, depth_od_ref, shown_ref = refs[:6]
     if last:
         earlier_ref, _, _, s_ref, final_ref, strips_ref, acc_s, uy_s, uz_s, sem = refs[6:]
+        done = pl.ds(MID, NX - 1 - MID)
+        stores = [pltpu.make_async_copy(s_ref.at[:, done], final_ref.at[:, done], sem.at[2])]
+        stores[0].start()
     else:
-        _, _, s_ref, next_ref, acc_s, ev_ref, od_ref, uy_s, uz_s = refs[6:]
+        (gates_ev_ref, gates_od_ref, rows_ref, own_ref, _, _,
+         s_ref, next_ref, acc_s, ahead_ref, ev_ref, od_ref, uy_s, uz_s) = refs[6:]
     even = is_even("depth")
-    stores = []
+    halos = neighbours("depth", depth_ev_ref[...], depth_od_ref[...])
+    if not last:
+        records = neighbours("area", gates_ev_ref[...], gates_od_ref[...])
+        for side in range(2):
+            ahead_ref[side] = outer_row(side, halos, rows_ref, own_ref, records[side])
     for end, x, base_ref, sign in ((0, 0, base_lo_ref, -1.0), (1, NX - 1, base_hi_ref, 1.0)):
-        if end == 1:
-            use_ev = even
-        else:
-            use_ev = jnp.logical_not(even)
         rows = slice(x // BLK * NY, x // BLK * NY + NY)
-        halo = choose(use_ev, depth_ev_ref[...], depth_od_ref[...])
+        halo = halos[end]
         u = halo[0:NY]
-        after, before = z_sides(u)
-        uz_s[...] = sign * (after - before)
-        after, before = y_sides(u, halo[NY:NY + 1], halo[NY + 1:NY + 2])
-        uy_s[...] = sign * (after - before)
+        uz_s[...] = sign * z_slope(u)
+        uy_s[...] = sign * y_slope(u, halo[NY:NY + 1], halo[NY + 1:NY + 2])
         for j in range(NZ // CHUNK):
             cols = slice(j * CHUNK, (j + 1) * CHUNK)
             m = coefs_ref[0, rows, cols]
@@ -336,9 +394,9 @@
                     acc_s[3 * f + k, :, cols] = item
         if last:
             stores.append(pltpu.make_async_copy(s_ref.at[:, x], final_ref.at[:, x], sem.at[end]))
-            stores[end].start()
+            stores[-1].start()
     if not last:
-        area_rows(next_ref, ev_ref, od_ref)
+        depth_messages(even, next_ref, ahead_ref, ev_ref, od_ref)
     else:
         for k in range(3):
             stack = jnp.concatenate(
@@ -402,135 +460,118 @@
     return pl.CostEstimate(flops=400 * voxels, bytes_accessed=32 * voxels, transcendentals=12 * voxels)
 
 
-def interior_front(last, states, u, coefs, area, passing):
-    out_shape = kept_in(pltpu.VMEM, VOLUME, FIELD, FIELD, FIELD, FIELD, SHOWN, PLANE) + shapes_of(passing.shape)
-    out_specs = [inside()] * 7 + [anywhere()]
-    aliases = {5: 7}
+def interior_front(states, u, coefs, rows, passing):
+    return pl.pallas_call(
+        front_kernel,
+        in_specs=[inside()] * 4 + [anywhere()],
+        out_specs=[inside()] * 7 + [anywhere()],
+        out_shape=kept_in(pltpu.VMEM, VOLUME, FIELD, FIELD, FIELD, FIELD, SHOWN, PLANE) + shapes_of(passing.shape),
+        input_output_aliases={0: 0, 4: 7},
+        compiler_params=params(4),
+        cost_estimate=cost(),
+        name="front",
+    )(states, u, coefs, rows, passing)
+
+
+def interior_back(last, u, coefs, rows, kept):
+    out_specs = [inside()] * 7
+    out_shape = kept_in(pltpu.VMEM, VOLUME, FIELD, FIELD, FIELD, FIELD, SHOWN, PLANE)
     if last:
-        aliases[0] = 0
+        out_specs += [anywhere()]
         out_shape += kept_in(pltpu.HBM, VOLUME)
-        out_specs += [anywhere()]
-        scratch = [COPY]
-    else:
-        scratch = [COPY((2,))]
     return pl.pallas_call(
-        lambda *refs: front_body(last, refs),
-        in_specs=[inside() if last else anywhere()] + [inside()] * 4 + [anywhere()],
+        back_kernel,
+        in_specs=[inside()] * 9,
         out_specs=out_specs,
         out_shape=out_shape,
-        scratch_shapes=scratch,
-        input_output_aliases=aliases,
-        compiler_params=params(INTERIOR_MIB),
+        scratch_shapes=[COPY] if last else [],
+        input_output_aliases={3 + k: k for k in range(6)},
+        compiler_params=params(4),
         cost_estimate=cost(),
-        name="front_last" if last else "front_first",
-    )(states, u, coefs, *area, passing)
-
-
-def interior_back(last, u, coefs, area, kept):
-    out_shape = kept_in(pltpu.VMEM, VOLUME, FIELD, FIELD, FIELD, FIELD, SHOWN, PLANE)
-    out_specs = [inside()] * 7
-    in_specs = [inside()] * 10
-    aliases = {4 + k: k for k in range(6)}
-    scratch = []
-    if last:
-        in_specs += [anywhere()]
-        out_shape += kept_in(pltpu.HBM, VOLUME)
-        out_specs += [anywhere()]
-        aliases[10] = 7
-        scratch = [COPY]
-    return pl.pallas_call(
-        lambda *refs: back_body(last, refs),
-        in_specs=in_specs,
-        out_specs=out_specs,
-        out_shape=out_shape,
-        scratch_shapes=scratch,
-        input_output_aliases=aliases,
-        compiler_params=params(INTERIOR_MIB),
-        cost_estimate=cost(),
-        name="back_last" if last else "back_first",
-    )(u, coefs, *area, *kept)
+        name="back",
+    )(u, coefs, rows, *kept)
 
 
 def ends(last, bases, coefs, depth, shown, rest):
     args = [*bases, coefs, *depth, shown, *rest]
     in_specs = [inside()] * len(args)
+    aliases = {len(args) - 2: 0, len(args) - 1: 1}
+    scratch = [pltpu.VMEM(PLANE, f32)] * 2
     if last:
+        out_shape = kept_in(pltpu.VMEM, VOLUME) + kept_in(pltpu.HBM, VOLUME)
+        out_shape += kept_in(pltpu.VMEM, (NZ // STRIP, 3 * HALF, 128))
+        scratch = [pltpu.VMEM(SHOWN, f32), *scratch, COPY((3,))]
         in_specs[-1] = anywhere()
-        out_shape = kept_in(pltpu.VMEM, VOLUME) + kept_in(pltpu.HBM, VOLUME) + shapes_of((NZ // STRIP, 3 * HALF, 128))
         out_specs = [inside(), anywhere(), inside()]
-        scratch = [pltpu.VMEM(SHOWN, f32)]
     else:
-        out_shape = kept_in(pltpu.VMEM, VOLUME, FIELD, SHOWN, (NX, NZ), (NX, NZ))
-        out_specs = [inside()] * 5
-        scratch = []
-    scratch += [pltpu.VMEM(PLANE, f32)] * 2
-    if last:
-        scratch += [COPY((2,))]
+        out_shape = kept_in(pltpu.VMEM, VOLUME, FIELD, SHOWN, (2, NX, NZ), (NY + 2, NZ), (NY + 2, NZ))
+        out_specs = [inside()] * 6
     return pl.pallas_call(
         lambda *refs: ends_body(last, refs),
         in_specs=in_specs,
         out_specs=out_specs,
         out_shape=out_shape,
         scratch_shapes=scratch,
-        input_output_aliases={len(args) - 2: 0, len(args) - 1: 1},
+        input_output_aliases=aliases,
         compiler_params=params(4),
         name="ends_last" if last else "ends_first",
     )(*args)
 
 
-def depth_messages(area, u):
-    return pl.pallas_call(
-        message_kernel,
-        out_shape=shapes_of((NY + 2, NZ), (NY + 2, NZ)),
-        compiler_params=params(1),
-        name="depth_message",
-    )(*area, u)
-
-
 def swaps(axis):
     count = lax.axis_size(axis)
-    even = [(i, i ^ 1) for i in range(count) if i ^ 1 < count]
-    odd = [(i, ((i - 1) ^ 1) + 1) for i in range(1, count) if ((i - 1) ^ 1) + 1 < count]
-    return even, odd
+    return [(i, i ^ 1) for i in range(count)], [(i, (((i - 1) ^ 1) + 1) % count) for i in range(count)]
 
 
 def swap(axis, which, message):
     return lax.ppermute(message, axis, swaps(axis)[which])
 
 
-def half_step(last, states, u, coefs, area):
-    messages = depth_messages(area, u)
+def half_step(last, states, u, coefs, rows, messages):
     even = swap("depth", 0, messages[0])
-    states, after, uy, uz, w, shown, low, passing, *final = interior_front(
-        last, states, u, coefs, area, messages[1])
+    *kept, low, passing = interior_front(states, u, coefs, rows, messages[1])
     odd = swap("depth", 1, passing)
-    kept = (states, after, uy, uz, w, shown, *final)
-    states, after, _, _, _, shown, high, *final = interior_back(last, u, coefs, area, kept)
+    states, after, _, _, _, shown, high, *final = interior_back(last, u, coefs, rows, kept)
     return states, after, shown, (low, high), (even, odd), final
 
 
 def per_device(states, tissue, fiber):
+    blocks = (NX // BLK, NY // BLK, NZ // BLK)
     states = pltpu.with_memory_space_constraint(states, pltpu.HBM)
-    u, ev, od = pl.pallas_call(
+    tissue = pltpu.with_memory_space_constraint(tissue, pltpu.HBM)
+    u, ev, od, own = pl.pallas_call(
         faces_kernel,
-        in_specs=[inside(), anywhere()],
-        out_shape=kept_in(pltpu.VMEM, FIELD, (NX, NZ), (NX, NZ)),
-        scratch_shapes=[pltpu.VMEM(FIELD, f32), COPY],
-        compiler_params=params(FACES_MIB),
+        in_specs=[anywhere(), anywhere()],
+        out_shape=kept_in(pltpu.VMEM, FIELD, (2 * NX, NZ), (2 * NX, NZ), (2, NX, NZ)),
+        scratch_shapes=[pltpu.VMEM(blocks, jnp.int32), pltpu.VMEM(FIELD, f32), COPY((2,))],
+        compiler_params=params(4),
         name="faces",
     )(tissue, states)
     area = swap("area", 0, ev), swap("area", 1, od)
-    coefs = pl.pallas_call(
-        coefs_kernel,
-        out_shape=jax.ShapeDtypeStruct((7, 64, NZ), f32),
+    states, coefs, ev, od = pl.pallas_call(
+        load_kernel,
+        in_specs=[inside(), inside(), anywhere(), anywhere()],
+        out_shape=kept_in(pltpu.VMEM, VOLUME, (7, 64, NZ), (RECORD, NZ), (RECORD, NZ)),
+        scratch_shapes=[COPY],
         compiler_params=params(4),
-        name="coefficients",
-    )(tissue, fiber)
-    states, u, shown, bases, depth, _ = half_step(False, states, u, coefs, area)
-    states, u, images, ev, od = ends(False, bases, coefs, depth, shown, (states, u))
-    area = swap("area", 0, ev), swap("area", 1, od)
-    states, _, shown, bases, depth, final = half_step(True, states, u, coefs, area)
-    _, states, strips = ends(True, bases, coefs, depth, shown, (images, states, final[0]))
+        cost_estimate=pl.CostEstimate(flops=10**7, bytes_accessed=8 * 10**6, transcendentals=0),
+        name="load",
+    )(tissue, fiber, states, own)
+    ev, od, rows, gates_ev, gates_od = pl.pallas_call(
+        message_kernel,
+        in_specs=[inside()] * 3 + [anywhere()] * 2,
+        out_specs=[inside()] * 3 + [anywhere()] * 2,
+        out_shape=kept_in(pltpu.VMEM, (NY + 4, NZ), (NY + 4, NZ), (4, NX, NZ), (RECORD, NZ), (RECORD, NZ)),
+        input_output_aliases={3: 3, 4: 4},
+        compiler_params=params(1),
+        name="depth_message",
+    )(*area, u, ev, od)
+    gates = swap("area", 0, gates_ev), swap("area", 1, gates_od)
+    states, after, shown, bases, depth, _ = half_step(False, states, u, coefs, rows, (ev, od))
+    states, u, images, rows, ev, od = ends(
+        False, bases, coefs, depth, shown, (*gates, rows, own, states, after))
+    states, _, shown, bases, depth, final = half_step(True, states, u, coefs, rows, (ev, od))
+    _, states, strips = ends(True, bases, coefs, depth, shown, (images, states, *final))
     strips = lax.all_to_all(strips, "depth", split_axis=0, concat_axis=0, tiled=True)
     images = pl.pallas_call(
         composite_kernel,

time: 62 us -> 54.2 us (0.87)
  the two profiles are of different devices: /device:TPU:97 before, /device:TPU:2 now
where the time goes in v4:
time: 54.2 us; the launch traced here: 54 us
  blocking collectives  18.1 us (33%)
  Pallas kernels  16.9 us (31%)
  starting transfers between devices  15.6 us (29%)
  waiting for transfers between devices  2.55 us (5%)
  between operations  0.75 us (1%)
    all_to_all x1, blocking collectives, per_device(): lax.all_to_all(strips, 'depth', split_axis=0, concat_axis=0, tiled=True)  18.1 us
    ppermute x8, starting transfers between devices, swap(): return lax.ppermute(message, axis, swaps(axis)[which])  15.6 us
    pallas_call x2, Pallas kernels, interior_front(): pl.pallas_call(front_kernel, in_specs=[inside()] * 4 + [anywhere()], out_...  4.03 us
    pallas_call x2, Pallas kernels, interior_back(): pl.pallas_call(back_kernel, in_specs=[inside()] * 9, out_specs=out_specs,...  3.83 us
    pallas_call x1, Pallas kernels, per_device(): pl.pallas_call(load_kernel, in_specs=[inside(), inside(), anywhere(), any...  3.73 us
    pallas_call x2, Pallas kernels, ends(): pl.pallas_call(lambda *refs: ends_body(last, refs), in_specs=in_specs, ou...  3.01 us
    ppermute x8, waiting for transfers between devices, swap(): return lax.ppermute(message, axis, swaps(axis)[which])  2.55 us
    pallas_call x1, Pallas kernels, per_device(): pl.pallas_call(faces_kernel, in_specs=[anywhere(), anywhere()], out_shape...  1.36 us
  transfers between devices with their start and end apart: 8, of which 2 were waited for; matrix products, arithmetic and copies ran while one was open for 0% of the time, Pallas kernels for 21%

profile of v4, /device:TPU:2, one launch (start us, length us, event | category | flops | bytes accessed | tf_op | source)
XLA Modules:
  0.0 54.0 jit_solution(16142513505784532347)
XLA Ops:
  0.6 0.0 copy-start
  0.6 1.4 %faces.1 = (f32[16,16,768]{2,1,0:T(8,128)S(1)}, f32[32,768]{1,0:T(8,128)S(1)}, f32[32,768]{1,0:T(8,128)S(1)}, f32[2,16,768]{2,1,0:T(8,128)S(1)}) custom-call(s32[4,4,192]{2,1,0:T(4,128)} %tissue_ref.3, f32[8,16,16,768]{3,2,1,0:T(8,128)} %states_ref.3), custom_call_target="tpu_custom_call" | custom-call | tf_op jit(solution)/shard_map/faces/pallas_call | solution.py:542
  2.0 0.1 collective-permute-start
  2.1 6.0 %collective-permute-start.1 = (f32[32,768]{1,0:T(8,128)S(1)}, f32[32,768]{1,0:T(8,128)S(1)}, u32[]{:S(2)}, u32[]{:S(2)}) collective-permute-start(f32[32,768]{1,0:T(8,128)S(1)} %get-tuple-element.52), channel_id=1, source_target_pairs={{0,15},{1,2},{2,1},{3,4},{4,3},{5,6},{6,5},{7,8},{8,7},{9,10},{10,... | collective-permute-start | bytes 294920 | tf_op jit(solution)/shard_map/ppermute | solution.py:527
  8.1 0.0 copy-done
  8.1 3.7 %load.1 = (f32[8,16,16,768]{3,2,1,0:T(8,128)S(1)}, f32[7,64,768]{2,1,0:T(8,128)S(1)}, f32[104,768]{1,0:T(8,128)S(1)}, f32[104,768]{1,0:T(8,128)S(1)}) custom-call(s32[4,4,192]{2,1,0:T(4,128)} %tissue_ref.3, s32[4,4,192]{2,1,0:T(4,128)S(1)} %copy-done, f32[8,16,16,768]{3,2,1,0:T(8,128)} %states_ref.3, f32[2,16,768]{2,1,0:T(8,128)S(1)} %get-tuple-element.47._after.refs_9_), custom_call_target="tpu_custom_call" | custom-call | flops 10000000 | bytes 8000000 | tf_op jit(solution)/shard_map/load/pallas_call | solution.py:551
  11.8 0.0 collective-permute-done.area_ev_ref
  11.8 0.0 collective-permute-done.1.area_od_ref
  11.9 0.1 collective-permute-start.4
  12.0 1.6 %collective-permute-start.5 = (f32[104,768]{1,0:T(8,128)S(1)}, f32[104,768]{1,0:T(8,128)S(1)}, u32[]{:S(2)}, u32[]{:S(2)}) collective-permute-start(f32[104,768]{1,0:T(8,128)S(1)} %get-tuple-element.69), channel_id=1, source_target_pairs={{0,15},{1,2},{2,1},{3,4},{4,3},{5,6},{6,5},{7,8},{8,7},{9,10},{10,... | collective-permute-start | bytes 958472 | tf_op jit(solution)/shard_map/ppermute | solution.py:527
  13.5 0.5 collective-permute-start.2
  14.1 2.0 %front.2 = (f32[8,16,16,768]{3,2,1,0:T(8,128)S(1)}, f32[16,16,768]{2,1,0:T(8,128)S(1)}, f32[16,16,768]{2,1,0:T(8,128)S(1)}, f32[16,16,768]{2,1,0:T(8,128)S(1)}, ...) custom-call(f32[8,16,16,768]{3,2,1,0:T(8,128)S(1)} %get-tuple-elemen, ...), custom_call_target="tpu_custom_call", output_to_operand_aliasing={{0}: (0, {}), {7}: (4, {})} | custom-call | flops 39321600 | bytes 3145728 | tf_op jit(solution)/shard_map/front/pallas_call | solution.py:464
  16.1 2.2 %collective-permute-start.3 = (f32[20,768]{1,0:T(8,128)S(1)}, f32[20,768]{1,0:T(8,128)S(1)}, u32[]{:S(2)}, u32[]{:S(2)}) collective-permute-start(f32[20,768]{1,0:T(8,128)S(1)} %get-tuple-element.66), channel_id=1, source_target_pairs={{0,240},{16,32},{32,16},{48,64},{64,48},{80,96},{96,80},{112,128},... | collective-permute-start | bytes 184328 | tf_op jit(solution)/shard_map/ppermute | solution.py:527
  18.3 1.9 %back.2 = (f32[8,16,16,768]{3,2,1,0:T(8,128)S(1)}, f32[16,16,768]{2,1,0:T(8,128)S(1)}, f32[16,16,768]{2,1,0:T(8,128)S(1)}, f32[16,16,768]{2,1,0:T(8,128)S(1)}, f...) custom-call(f32[16,16,768]{2,1,0:T(8,128)S(1)} %get-tuple-element.49, ...), custom_call_target="tpu_custom_call", output_to_operand_aliasing={{0}: (3, {}), {1}: (4, {}), {2}: (5, {}), {3}: (6, {}), {4}... | custom-call | flops 39321600 | bytes 3145728 | tf_op jit(solution)/shard_map/back/pallas_call | solution.py:482
  20.2 0.0 collective-permute-done.2.refs_3_
  20.3 0.4 collective-permute-done.3.refs_4_
  20.7 0.0 collective-permute-done.4.refs_6_
  20.7 0.0 collective-permute-done.5.refs_7_
  20.7 1.2 %ends_first.1 = (f32[8,16,16,768]{3,2,1,0:T(8,128)S(1)}, f32[16,16,768]{2,1,0:T(8,128)S(1)}, f32[6,16,768]{2,1,0:T(8,128)S(1)}, f32[2,16,768]{2,1,0:T(8,128)S(1)...) custom-call(f32[16,768]{1,0:T(8,128)S(1)} %get-tuple-element.57.refs_0_, ...), custom_call_target="tpu_custom_call", output_to_operand_aliasing={{0}: (10, {}), {1}: (11, {})} | custom-call | tf_op jit(solution)/shard_map/ends_first/pallas_call | solution.py:509
  21.9 4.8 %collective-permute-start.6 = (f32[18,768]{1,0:T(8,128)S(1)}, f32[18,768]{1,0:T(8,128)S(1)}, u32[]{:S(2)}, u32[]{:S(2)}) collective-permute-start(f32[18,768]{1,0:T(8,128)S(1)} %get-tuple-element.84), channel_id=1, source_target_pairs={{0,16},{16,0},{32,48},{48,32},{64,80},{80,64},{96,112},{112,96},{1... | collective-permute-start | bytes 165896 | tf_op jit(solution)/shard_map/ppermute | solution.py:527
  26.6 2.0 %front.3 = (f32[8,16,16,768]{3,2,1,0:T(8,128)S(1)}, f32[16,16,768]{2,1,0:T(8,128)S(1)}, f32[16,16,768]{2,1,0:T(8,128)S(1)}, f32[16,16,768]{2,1,0:T(8,128)S(1)}, ...) custom-call(f32[8,16,16,768]{3,2,1,0:T(8,128)S(1)} %get-tuple-elemen, ...), custom_call_target="tpu_custom_call", output_to_operand_aliasing={{0}: (0, {}), {7}: (4, {})} | custom-call | flops 39321600 | bytes 3145728 | tf_op jit(solution)/shard_map/front/pallas_call | solution.py:464
  28.7 0.4 collective-permute-start.7
  29.0 1.9 %back.3 = (f32[8,16,16,768]{3,2,1,0:T(8,128)S(1)}, f32[16,16,768]{2,1,0:T(8,128)S(1)}, f32[16,16,768]{2,1,0:T(8,128)S(1)}, f32[16,16,768]{2,1,0:T(8,128)S(1)}, f...) custom-call(f32[16,16,768]{2,1,0:T(8,128)S(1)} %get-tuple-element.73, ...), custom_call_target="tpu_custom_call", output_to_operand_aliasing={{0}: (3, {}), {1}: (4, {}), {2}: (5, {}), {3}: (6, {}), {4}... | custom-call | flops 39321600 | bytes 3145728 | tf_op jit(solution)/shard_map/back/pallas_call | solution.py:482
  31.0 0.0 collective-permute-done.6.refs_3_
  31.0 2.1 %collective-permute-done.7.refs_4_ = f32[18,768]{1,0:T(8,128)S(1)} collective-permute-done((f32[18,768]{1,0:T(8,128)S(1)}, f32[18,768]{1,0:T(8,128)S(1)}, u32[]{:S(2)}, u32[]{:S(2)}) %collective-permute-start.7) | collective-permute-done | bytes 55328 | tf_op jit(solution)/shard_map/ppermute | solution.py:527
  33.1 1.8 %ends_last.1 = (f32[8,16,16,768]{3,2,1,0:T(8,128)S(1)}, f32[8,16,16,768]{3,2,1,0:T(8,128)}, f32[16,72,128]{2,1,0:T(8,128)S(1)}) custom-call(f32[16,768]{1,0:T(8,128)S(1)} %get-tuple-element.76.refs_0_, f32[16,768]{1,0:T(8,128)S(1)} %get-tuple-element.83.refs_1_, ...), custom_call_target="tpu_custom_call", output_to_operand_aliasing={{0}: (7, {}), {1}: (8, {})} | custom-call | tf_op jit(solution)/shard_map/ends_last/pallas_call | solution.py:509
  34.9 18.1 %all_to_all.5.strips_ref = f32[16,72,128]{2,1,0:T(8,128)S(1)} all-to-all(f32[16,72,128]{2,1,0:T(8,128)S(1)} %get-tuple-element.91), channel_id=1, replica_groups=mesh['depth'=16,'area'=16] {'depth'}, dimensions={0} | all-to-all | bytes 1179648 | tf_op jit(solution)/shard_map/all_to_all | solution.py:575
  53.1 0.9 %composite.1 = f32[2,2,4,16,48]{4,3,2,1,0:T(8,128)} custom-call(f32[16,72,128]{2,1,0:T(8,128)S(1)} %all_to_all.5.strips_ref), custom_call_target="tpu_custom_call" | custom-call | tf_op jit(solution)/shard_map/composite/pallas_call | solution.py:576
  (1 shorter events, 0.0 us)
Async XLA Ops:
  0.6 7.4 %copy-start = (s32[4,4,192]{2,1,0:T(4,128)S(1)}, s32[4,4,192]{2,1,0:T(4,128)}, u32[]{:S(2)}) copy-start(s32[4,4,192]{2,1,0:T(4,128)} %fiber_ref.1) | copy-start | bytes 36868
  2.0 9.8 %collective-permute-start = (f32[32,768]{1,0:T(8,128)S(1)}, f32[32,768]{1,0:T(8,128)S(1)}, u32[]{:S(2)}, u32[]{:S(2)}) collective-permute-start(f32[32,768]{1,0:T(8,128)S(1)} %get-tuple-element.51), channel_id=1, source_target_pairs={{0,1},{1,0},{2,3},{3,2},{4,5},{5,4},{6,7},{7,6},{8,9},{9,8},{10,11... | collective-permute-start | bytes 294920 | tf_op jit(solution)/shard_map/ppermute | solution.py:527
  2.1 9.7 %collective-permute-start.1 = (f32[32,768]{1,0:T(8,128)S(1)}, f32[32,768]{1,0:T(8,128)S(1)}, u32[]{:S(2)}, u32[]{:S(2)}) collective-permute-start(f32[32,768]{1,0:T(8,128)S(1)} %get-tuple-element.52), channel_id=1, source_target_pairs={{0,15},{1,2},{2,1},{3,4},{4,3},{5,6},{6,5},{7,8},{8,7},{9,10},{10,... | collective-permute-start | bytes 294920 | tf_op jit(solution)/shard_map/ppermute | solution.py:527
  11.9 8.8 %collective-permute-start.4 = (f32[104,768]{1,0:T(8,128)S(1)}, f32[104,768]{1,0:T(8,128)S(1)}, u32[]{:S(2)}, u32[]{:S(2)}) collective-permute-start(f32[104,768]{1,0:T(8,128)S(1)} %get-tuple-element.68), channel_id=1, source_target_pairs={{0,1},{1,0},{2,3},{3,2},{4,5},{5,4},{6,7},{7,6},{8,9},{9,8},{10,11... | collective-permute-start | bytes 958472 | tf_op jit(solution)/shard_map/ppermute | solution.py:527
  12.0 8.7 %collective-permute-start.5 = (f32[104,768]{1,0:T(8,128)S(1)}, f32[104,768]{1,0:T(8,128)S(1)}, u32[]{:S(2)}, u32[]{:S(2)}) collective-permute-start(f32[104,768]{1,0:T(8,128)S(1)} %get-tuple-element.69), channel_id=1, source_target_pairs={{0,15},{1,2},{2,1},{3,4},{4,3},{5,6},{6,5},{7,8},{8,7},{9,10},{10,... | collective-permute-start | bytes 958472 | tf_op jit(solution)/shard_map/ppermute | solution.py:527
  13.5 6.7 %collective-permute-start.2 = (f32[20,768]{1,0:T(8,128)S(1)}, f32[20,768]{1,0:T(8,128)S(1)}, u32[]{:S(2)}, u32[]{:S(2)}) collective-permute-start(f32[20,768]{1,0:T(8,128)S(1)} %get-tuple-element.65), channel_id=1, source_target_pairs={{0,16},{16,0},{32,48},{48,32},{64,80},{80,64},{96,112},{112,96},{1... | collective-permute-start | bytes 184328 | tf_op jit(solution)/shard_map/ppermute | solution.py:527
  16.1 4.6 %collective-permute-start.3 = (f32[20,768]{1,0:T(8,128)S(1)}, f32[20,768]{1,0:T(8,128)S(1)}, u32[]{:S(2)}, u32[]{:S(2)}) collective-permute-start(f32[20,768]{1,0:T(8,128)S(1)} %get-tuple-element.66), channel_id=1, source_target_pairs={{0,240},{16,32},{32,16},{48,64},{64,48},{80,96},{96,80},{112,128},... | collective-permute-start | bytes 184328 | tf_op jit(solution)/shard_map/ppermute | solution.py:527
  21.9 9.1 %collective-permute-start.6 = (f32[18,768]{1,0:T(8,128)S(1)}, f32[18,768]{1,0:T(8,128)S(1)}, u32[]{:S(2)}, u32[]{:S(2)}) collective-permute-start(f32[18,768]{1,0:T(8,128)S(1)} %get-tuple-element.84), channel_id=1, source_target_pairs={{0,16},{16,0},{32,48},{48,32},{64,80},{80,64},{96,112},{112,96},{1... | collective-permute-start | bytes 165896 | tf_op jit(solution)/shard_map/ppermute | solution.py:527
  28.7 4.4 %collective-permute-start.7 = (f32[18,768]{1,0:T(8,128)S(1)}, f32[18,768]{1,0:T(8,128)S(1)}, u32[]{:S(2)}, u32[]{:S(2)}) collective-permute-start(f32[18,768]{1,0:T(8,128)S(1)} %get-tuple-element.85), channel_id=1, source_target_pairs={{0,240},{16,32},{32,16},{48,64},{64,48},{80,96},{96,80},{112,128},... | collective-permute-start | bytes 165896 | tf_op jit(solution)/shard_map/ppermute | solution.py:527

commit v5 on v4

--- a/solution.py
+++ b/solution.py
@@ -105,8 +105,9 @@
 
 
 def load_kernel(tissue_ref, fiber_ref, states_ref, _after, s_ref, coefs_ref, ev_ref, od_ref, sem):
-    load = pltpu.make_async_copy(states_ref, s_ref, sem)
-    load.start()
+    loads = [pltpu.make_async_copy(states_ref.at[k], s_ref.at[k], sem.at[k]) for k in range(8)]
+    for k in (1, 2, 3, 4, 5, 6, 0, 7):
+        loads[k].start()
     kind = flat(fiber_ref)
     parts = [flat(tissue_ref).astype(f32)]
     for table in class_tables():
@@ -133,14 +134,16 @@
             high = wide[16 * part + 4 * block + 3:16 * part + 4 * block + 4]
             ev_ref[place + block:place + block + 1] = choose(even, high, low)
             od_ref[place + block:place + block + 1] = choose(even, low, high)
-    load.wait()
     for k in range(GATES):
+        loads[k + 1].wait()
         for x in range(NX):
             place = NX * k + x
             low = s_ref[k + 1, x, 0:1]
             high = s_ref[k + 1, x, NY - 1:NY]
             ev_ref[place:place + 1] = choose(even, high, low)
             od_ref[place:place + 1] = choose(even, low, high)
+    loads[0].wait()
+    loads[7].wait()
 
 
 def message_kernel(area_ev_ref, area_od_ref, u_ref, _e, _o, ev_ref, od_ref, rows_ref, _gates_ev, _gates_od):
@@ -261,7 +264,8 @@
             new = advance(w, [s_ref[k, x, :, cols] for k in range(8)], m > 0.5)
             for k in range(8):
                 s_ref[k, x, :, cols] = new[k]
-            next_ref[x, :, cols] = m * new[0]
+            if next_ref is not None:
+                next_ref[x, :, cols] = m * new[0]
             marches = show(new, m, marches)
         for f in range(2):
             for k in range(3):
@@ -280,29 +284,29 @@
     )
 
 
-def front_kernel(_s, u_ref, coefs_ref, rows_ref, _p,
-                 s_ref, next_ref, uy_ref, uz_ref, w_ref, shown_ref, base_ref, _passing):
-    derive(range(MID + 1), u_ref, coefs_ref, rows_ref, uy_ref, uz_ref, w_ref)
-    base_ref[...] = base_of(0, 1, 1.0, u_ref, coefs_ref, uy_ref, uz_ref, w_ref)
+def interior_kernel(last, refs):
+    u_ref, coefs_ref, rows_ref = refs[1:4]
+    s_ref, shown_ref, base_ref = refs[4:7]
+    if last:
+        next_ref = None
+        final_ref, uy_s, uz_s, w_s, sem = refs[7:]
+    else:
+        next_ref, uy_s, uz_s, w_s = refs[7:]
+    derive(range(NX), u_ref, coefs_ref, rows_ref, uy_s, uz_s, w_s)
+    base_ref[0] = base_of(0, 1, 1.0, u_ref, coefs_ref, uy_s, uz_s, w_s)
+    base_ref[1] = base_of(NX - 1, NX - 2, -1.0, u_ref, coefs_ref, uy_s, uz_s, w_s)
     one = jnp.ones((NY, CHUNK), f32)
     zero = jnp.zeros((NY, CHUNK), f32)
     interior_planes(range(1, MID), lambda cols: [(one, zero, zero)] * 2,
-                    s_ref, u_ref, next_ref, coefs_ref, uy_ref, uz_ref, w_ref, shown_ref)
-
-
-def back_kernel(u_ref, coefs_ref, rows_ref, _s, _n, _y, _z, _w, _a,
-                s_ref, next_ref, uy_ref, uz_ref, w_ref, shown_ref, base_ref, *storing):
-    if storing:
-        final_ref, sem = storing
+                    s_ref, u_ref, next_ref, coefs_ref, uy_s, uz_s, w_s, shown_ref)
+    if last:
         done = pl.ds(1, MID - 1)
         store = pltpu.make_async_copy(s_ref.at[:, done], final_ref.at[:, done], sem)
         store.start()
-    derive(range(MID + 1, NX), u_ref, coefs_ref, rows_ref, uy_ref, uz_ref, w_ref)
-    base_ref[...] = base_of(NX - 1, NX - 2, -1.0, u_ref, coefs_ref, uy_ref, uz_ref, w_ref)
     interior_planes(range(MID, NX - 1),
                     lambda cols: [tuple(shown_ref[3 * f + k, :, cols] for k in range(3)) for f in range(2)],
-                    s_ref, u_ref, next_ref, coefs_ref, uy_ref, uz_ref, w_ref, shown_ref)
-    if storing:
+                    s_ref, u_ref, next_ref, coefs_ref, uy_s, uz_s, w_s, shown_ref)
+    if last:
         store.wait()
 
 
@@ -342,22 +346,22 @@
 
 
 def ends_body(last, refs):
-    base_lo_ref, base_hi_ref, coefs_ref, depth_ev_ref, depth_od_ref, shown_ref = refs[:6]
+    bases_ref, coefs_ref, depth_ev_ref, depth_od_ref, shown_ref = refs[:5]
     if last:
-        earlier_ref, _, _, s_ref, final_ref, strips_ref, acc_s, uy_s, uz_s, sem = refs[6:]
+        earlier_ref, _, _, s_ref, final_ref, strips_ref, acc_s, uy_s, uz_s, sem = refs[5:]
         done = pl.ds(MID, NX - 1 - MID)
         stores = [pltpu.make_async_copy(s_ref.at[:, done], final_ref.at[:, done], sem.at[2])]
         stores[0].start()
     else:
         (gates_ev_ref, gates_od_ref, rows_ref, own_ref, _, _,
-         s_ref, next_ref, acc_s, ahead_ref, ev_ref, od_ref, uy_s, uz_s) = refs[6:]
+         s_ref, next_ref, acc_s, ahead_ref, ev_ref, od_ref, uy_s, uz_s) = refs[5:]
     even = is_even("depth")
     halos = neighbours("depth", depth_ev_ref[...], depth_od_ref[...])
     if not last:
         records = neighbours("area", gates_ev_ref[...], gates_od_ref[...])
         for side in range(2):
             ahead_ref[side] = outer_row(side, halos, rows_ref, own_ref, records[side])
-    for end, x, base_ref, sign in ((0, 0, base_lo_ref, -1.0), (1, NX - 1, base_hi_ref, 1.0)):
+    for end, x, sign in ((0, 0, -1.0), (1, NX - 1, 1.0)):
         rows = slice(x // BLK * NY, x // BLK * NY + NY)
         halo = halos[end]
         u = halo[0:NY]
@@ -367,7 +371,7 @@
             cols = slice(j * CHUNK, (j + 1) * CHUNK)
             m = coefs_ref[0, rows, cols]
             w = (
-                base_ref[:, cols]
+                bases_ref[end, :, cols]
                 + coefs_ref[1, rows, cols] * u[:, cols]
                 + coefs_ref[4, rows, cols] * uy_s[:, cols]
                 + coefs_ref[5, rows, cols] * uz_s[:, cols]
@@ -456,44 +460,36 @@
 
 
 def cost():
-    voxels = NX * NY * NZ // 2
+    voxels = NX * NY * NZ
     return pl.CostEstimate(flops=400 * voxels, bytes_accessed=32 * voxels, transcendentals=12 * voxels)
 
 
-def interior_front(states, u, coefs, rows, passing):
-    return pl.pallas_call(
-        front_kernel,
-        in_specs=[inside()] * 4 + [anywhere()],
-        out_specs=[inside()] * 7 + [anywhere()],
-        out_shape=kept_in(pltpu.VMEM, VOLUME, FIELD, FIELD, FIELD, FIELD, SHOWN, PLANE) + shapes_of(passing.shape),
-        input_output_aliases={0: 0, 4: 7},
-        compiler_params=params(4),
-        cost_estimate=cost(),
-        name="front",
-    )(states, u, coefs, rows, passing)
-
-
-def interior_back(last, u, coefs, rows, kept):
-    out_specs = [inside()] * 7
-    out_shape = kept_in(pltpu.VMEM, VOLUME, FIELD, FIELD, FIELD, FIELD, SHOWN, PLANE)
+def interior(last, states, u, coefs, rows):
+    out_specs = [inside()] * 3
+    out_shape = kept_in(pltpu.VMEM, VOLUME, SHOWN, (2, NY, NZ))
+    scratch = [pltpu.VMEM(FIELD, f32)] * 3
     if last:
         out_specs += [anywhere()]
         out_shape += kept_in(pltpu.HBM, VOLUME)
+        scratch += [COPY]
+    else:
+        out_specs += [inside()]
+        out_shape += kept_in(pltpu.VMEM, FIELD)
     return pl.pallas_call(
-        back_kernel,
-        in_specs=[inside()] * 9,
+        lambda *refs: interior_kernel(last, refs),
+        in_specs=[inside()] * 4,
         out_specs=out_specs,
         out_shape=out_shape,
-        scratch_shapes=[COPY] if last else [],
-        input_output_aliases={3 + k: k for k in range(6)},
-        compiler_params=params(4),
+        scratch_shapes=scratch,
+        input_output_aliases={0: 0},
+        compiler_params=params(8),
         cost_estimate=cost(),
-        name="back",
-    )(u, coefs, rows, *kept)
+        name="interior_last" if last else "interior_first",
+    )(states, u, coefs, rows)
 
 
 def ends(last, bases, coefs, depth, shown, rest):
-    args = [*bases, coefs, *depth, shown, *rest]
+    args = [bases, coefs, *depth, shown, *rest]
     in_specs = [inside()] * len(args)
     aliases = {len(args) - 2: 0, len(args) - 1: 1}
     scratch = [pltpu.VMEM(PLANE, f32)] * 2
@@ -527,14 +523,6 @@
     return lax.ppermute(message, axis, swaps(axis)[which])
 
 
-def half_step(last, states, u, coefs, rows, messages):
-    even = swap("depth", 0, messages[0])
-    *kept, low, passing = interior_front(states, u, coefs, rows, messages[1])
-    odd = swap("depth", 1, passing)
-    states, after, _, _, _, shown, high, *final = interior_back(last, u, coefs, rows, kept)
-    return states, after, shown, (low, high), (even, odd), final
-
-
 def per_device(states, tissue, fiber):
     blocks = (NX // BLK, NY // BLK, NZ // BLK)
     states = pltpu.with_memory_space_constraint(states, pltpu.HBM)
@@ -552,7 +540,7 @@
         load_kernel,
         in_specs=[inside(), inside(), anywhere(), anywhere()],
         out_shape=kept_in(pltpu.VMEM, VOLUME, (7, 64, NZ), (RECORD, NZ), (RECORD, NZ)),
-        scratch_shapes=[COPY],
+        scratch_shapes=[COPY((8,))],
         compiler_params=params(4),
         cost_estimate=pl.CostEstimate(flops=10**7, bytes_accessed=8 * 10**6, transcendentals=0),
         name="load",
@@ -567,11 +555,13 @@
         name="depth_message",
     )(*area, u, ev, od)
     gates = swap("area", 0, gates_ev), swap("area", 1, gates_od)
-    states, after, shown, bases, depth, _ = half_step(False, states, u, coefs, rows, (ev, od))
+    depth = swap("depth", 0, ev), swap("depth", 1, od)
+    states, shown, bases, after = interior(False, states, u, coefs, rows)
     states, u, images, rows, ev, od = ends(
         False, bases, coefs, depth, shown, (*gates, rows, own, states, after))
-    states, _, shown, bases, depth, final = half_step(True, states, u, coefs, rows, (ev, od))
-    _, states, strips = ends(True, bases, coefs, depth, shown, (images, states, *final))
+    depth = swap("depth", 0, ev), swap("depth", 1, od)
+    states, shown, bases, final = interior(True, states, u, coefs, rows)
+    _, states, strips = ends(True, bases, coefs, depth, shown, (images, states, final))
     strips = lax.all_to_all(strips, "depth", split_axis=0, concat_axis=0, tiled=True)
     images = pl.pallas_call(
         composite_kernel,

time: 54.2 us -> 50.1 us (0.924)
  waiting for transfers between devices: 2.55 us -> 0.53 us
  starting transfers between devices: 15.6 us -> 14.5 us
  blocking collectives: 18.1 us -> 17.5 us
    ppermute x8, waiting for transfers between devices: 2.55 us -> 0.53 us  [swap(): return lax.ppermute(message, axis, swaps(axis)[which])]
    ppermute x8, starting transfers between devices: 15.6 us -> 14.5 us  [swap(): return lax.ppermute(message, axis, swaps(axis)[which])]
    all_to_all x1, blocking collectives: 18.1 us -> 17.5 us  [per_device(): lax.all_to_all(strips, 'depth', split_axis=0, concat_axis=0, tiled=True)]
    pallas_call x4 -> x2, Pallas kernels: 7.86 us -> 7.6 us  [interior(): pl.pallas_call(lambda *refs: interior_kernel(last, refs), in_specs=[insid...]
  transfers between devices with their start and end apart: 8 -> 8, of which waited for: 2 -> 1; matrix products, arithmetic and copies ran while one was open for 0% -> 0% of each run, Pallas kernels for 21% -> 23%
where the time goes in v5:
time: 50.1 us; the launch traced here: 49.8 us
  blocking collectives  17.5 us (35%)
  Pallas kernels  16.6 us (33%)
  starting transfers between devices  14.5 us (29%)
  between operations  0.76 us (2%)
  waiting for transfers between devices  0.53 us (1%)
    all_to_all x1, blocking collectives, per_device(): lax.all_to_all(strips, 'depth', split_axis=0, concat_axis=0, tiled=True)  17.5 us
    ppermute x8, starting transfers between devices, swap(): return lax.ppermute(message, axis, swaps(axis)[which])  14.5 us
    pallas_call x2, Pallas kernels, interior(): pl.pallas_call(lambda *refs: interior_kernel(last, refs), in_specs=[insid...  7.6 us
    pallas_call x1, Pallas kernels, per_device(): pl.pallas_call(load_kernel, in_specs=[inside(), inside(), anywhere(), any...  3.64 us
    pallas_call x2, Pallas kernels, ends(): pl.pallas_call(lambda *refs: ends_body(last, refs), in_specs=in_specs, ou...  3.02 us
    pallas_call x1, Pallas kernels, per_device(): pl.pallas_call(faces_kernel, in_specs=[anywhere(), anywhere()], out_shape...  1.36 us
  transfers between devices with their start and end apart: 8, of which 1 were waited for; matrix products, arithmetic and copies ran while one was open for 0% of the time, Pallas kernels for 23%

profile of v5, /device:TPU:2, one launch (start us, length us, event | category | flops | bytes accessed | tf_op | source)
XLA Modules:
  0.0 49.8 jit_solution(294296845692603549)
XLA Ops:
  0.6 0.0 copy-start
  0.6 1.4 %faces.1 = (f32[16,16,768]{2,1,0:T(8,128)S(1)}, f32[32,768]{1,0:T(8,128)S(1)}, f32[32,768]{1,0:T(8,128)S(1)}, f32[2,16,768]{2,1,0:T(8,128)S(1)}) custom-call(s32[4,4,192]{2,1,0:T(4,128)} %tissue_ref.3, f32[8,16,16,768]{3,2,1,0:T(8,128)} %states_ref.3), custom_call_target="tpu_custom_call" | custom-call | tf_op jit(solution)/shard_map/faces/pallas_call | solution.py:530
  2.0 0.1 collective-permute-start
  2.1 6.0 %collective-permute-start.1 = (f32[32,768]{1,0:T(8,128)S(1)}, f32[32,768]{1,0:T(8,128)S(1)}, u32[]{:S(2)}, u32[]{:S(2)}) collective-permute-start(f32[32,768]{1,0:T(8,128)S(1)} %get-tuple-element.36), channel_id=1, source_target_pairs={{0,15},{1,2},{2,1},{3,4},{4,3},{5,6},{6,5},{7,8},{8,7},{9,10},{10,... | collective-permute-start | bytes 294920 | tf_op jit(solution)/shard_map/ppermute | solution.py:523
  8.1 0.0 copy-done
  8.1 3.6 %load.1 = (f32[8,16,16,768]{3,2,1,0:T(8,128)S(1)}, f32[7,64,768]{2,1,0:T(8,128)S(1)}, f32[104,768]{1,0:T(8,128)S(1)}, f32[104,768]{1,0:T(8,128)S(1)}) custom-call(s32[4,4,192]{2,1,0:T(4,128)} %tissue_ref.3, s32[4,4,192]{2,1,0:T(4,128)S(1)} %copy-done, f32[8,16,16,768]{3,2,1,0:T(8,128)} %states_ref.3, f32[2,16,768]{2,1,0:T(8,128)S(1)} %get-tuple-element.31._after.refs_8_), custom_call_target="tpu_custom_call" | custom-call | flops 10000000 | bytes 8000000 | tf_op jit(solution)/shard_map/load/pallas_call | solution.py:539
  11.7 0.0 collective-permute-done.area_ev_ref
  11.7 0.0 collective-permute-done.1.area_od_ref
  11.7 0.1 depth_message.1
  11.8 0.1 collective-permute-start.4
  11.9 1.7 %collective-permute-start.5 = (f32[104,768]{1,0:T(8,128)S(1)}, f32[104,768]{1,0:T(8,128)S(1)}, u32[]{:S(2)}, u32[]{:S(2)}) collective-permute-start(f32[104,768]{1,0:T(8,128)S(1)} %get-tuple-element.45), channel_id=1, source_target_pairs={{0,15},{1,2},{2,1},{3,4},{4,3},{5,6},{6,5},{7,8},{8,7},{9,10},{10,... | collective-permute-start | bytes 958472 | tf_op jit(solution)/shard_map/ppermute | solution.py:523
  13.6 0.5 %collective-permute-start.2 = (f32[20,768]{1,0:T(8,128)S(1)}, f32[20,768]{1,0:T(8,128)S(1)}, u32[]{:S(2)}, u32[]{:S(2)}) collective-permute-start(f32[20,768]{1,0:T(8,128)S(1)} %get-tuple-element.41), channel_id=1, source_target_pairs={{0,16},{16,0},{32,48},{48,32},{64,80},{80,64},{96,112},{112,96},{1... | collective-permute-start | bytes 184328 | tf_op jit(solution)/shard_map/ppermute | solution.py:523
  14.1 2.2 %collective-permute-start.3 = (f32[20,768]{1,0:T(8,128)S(1)}, f32[20,768]{1,0:T(8,128)S(1)}, u32[]{:S(2)}, u32[]{:S(2)}) collective-permute-start(f32[20,768]{1,0:T(8,128)S(1)} %get-tuple-element.42), channel_id=1, source_target_pairs={{0,240},{16,32},{32,16},{48,64},{64,48},{80,96},{96,80},{112,128},... | collective-permute-start | bytes 184328 | tf_op jit(solution)/shard_map/ppermute | solution.py:523
  16.2 3.8 %interior_first.1 = (f32[8,16,16,768]{3,2,1,0:T(8,128)S(1)}, f32[6,16,768]{2,1,0:T(8,128)S(1)}, f32[2,16,768]{2,1,0:T(8,128)S(1)}, f32[16,16,768]{2,1,0:T(8,128)S(1)}) custom-call(f32[8,16,16,768]{3,2,1,0:T(8,128)S(1)} %get-tuple-element.32.refs_0_, f32[16,16,768]{2,1,0:T(8,128)S(1)} %get-tuple-element.33.u_ref.refs_1_, ...), custom_call_target="tpu_custom_call", output_to_operand_aliasing={{0}: (0, {})} | custom-call | flops 78643200 | bytes 6291456 | tf_op jit(solution)/shard_map/interior_first/pallas_call | solution.py:478
  20.0 0.0 collective-permute-done.2.refs_2_
  20.0 0.0 collective-permute-done.3.refs_3_
  20.1 0.0 collective-permute-done.4.refs_5_
  20.1 0.0 collective-permute-done.5.refs_6_
  20.1 1.2 %ends_first.1 = (f32[8,16,16,768]{3,2,1,0:T(8,128)S(1)}, f32[16,16,768]{2,1,0:T(8,128)S(1)}, f32[6,16,768]{2,1,0:T(8,128)S(1)}, f32[2,16,768]{2,1,0:T(8,128)S(1)...) custom-call(f32[2,16,768]{2,1,0:T(8,128)S(1)} %get-tuple-element.40.refs_0_, ...), custom_call_target="tpu_custom_call", output_to_operand_aliasing={{0}: (9, {}), {1}: (10, {})} | custom-call | tf_op jit(solution)/shard_map/ends_first/pallas_call | solution.py:505
  21.3 4.0 %collective-permute-start.6 = (f32[18,768]{1,0:T(8,128)S(1)}, f32[18,768]{1,0:T(8,128)S(1)}, u32[]{:S(2)}, u32[]{:S(2)}) collective-permute-start(f32[18,768]{1,0:T(8,128)S(1)} %get-tuple-element.52), channel_id=1, source_target_pairs={{0,16},{16,0},{32,48},{48,32},{64,80},{80,64},{96,112},{112,96},{1... | collective-permute-start | bytes 165896 | tf_op jit(solution)/shard_map/ppermute | solution.py:523
  25.2 0.0 collective-permute-start.7
  25.3 3.8 %interior_last.1 = (f32[8,16,16,768]{3,2,1,0:T(8,128)S(1)}, f32[6,16,768]{2,1,0:T(8,128)S(1)}, f32[2,16,768]{2,1,0:T(8,128)S(1)}, f32[8,16,16,768]{3,2,1,0:T(8,128)}) custom-call(f32[8,16,16,768]{3,2,1,0:T(8,128)S(1)} %get-tuple-element.48.refs_0_, f32[16,16,768]{2,1,0:T(8,128)S(1)} %get-tuple-element.49.refs_1_, ...), custom_call_target="tpu_custom_call", output_to_operand_aliasing={{0}: (0, {})} | custom-call | flops 78643200 | bytes 6291456 | tf_op jit(solution)/shard_map/interior_last/pallas_call | solution.py:478
  29.1 0.0 collective-permute-done.6.refs_2_
  29.1 0.5 %collective-permute-done.7.refs_3_ = f32[18,768]{1,0:T(8,128)S(1)} collective-permute-done((f32[18,768]{1,0:T(8,128)S(1)}, f32[18,768]{1,0:T(8,128)S(1)}, u32[]{:S(2)}, u32[]{:S(2)}) %collective-permute-start.7) | collective-permute-done | bytes 55328 | tf_op jit(solution)/shard_map/ppermute | solution.py:523
  29.6 1.8 %ends_last.1 = (f32[8,16,16,768]{3,2,1,0:T(8,128)S(1)}, f32[8,16,16,768]{3,2,1,0:T(8,128)}, f32[16,72,128]{2,1,0:T(8,128)S(1)}) custom-call(f32[2,16,768]{2,1,0:T(8,128)S(1)} %get-tuple-element.51.refs_0_, f32[7,64,768]{2,1,0:T(8,128)S(1)} %get-tuple-element.34.refs_2_.refs_1_, ...), custom_call_target="tpu_custom_call", output_to_operand_aliasing={{0}: (6, {}), {1}: (7, {})} | custom-call | tf_op jit(solution)/shard_map/ends_last/pallas_call | solution.py:505
  31.4 17.5 %all_to_all.5.strips_ref = f32[16,72,128]{2,1,0:T(8,128)S(1)} all-to-all(f32[16,72,128]{2,1,0:T(8,128)S(1)} %get-tuple-element.59), channel_id=1, replica_groups=mesh['depth'=16,'area'=16] {'depth'}, dimensions={0} | all-to-all | bytes 1179648 | tf_op jit(solution)/shard_map/all_to_all | solution.py:565
  48.9 0.9 %composite.1 = f32[2,2,4,16,48]{4,3,2,1,0:T(8,128)} custom-call(f32[16,72,128]{2,1,0:T(8,128)S(1)} %all_to_all.5.strips_ref), custom_call_target="tpu_custom_call" | custom-call | tf_op jit(solution)/shard_map/composite/pallas_call | solution.py:566
Async XLA Ops:
  0.6 7.4 %copy-start = (s32[4,4,192]{2,1,0:T(4,128)S(1)}, s32[4,4,192]{2,1,0:T(4,128)}, u32[]{:S(2)}) copy-start(s32[4,4,192]{2,1,0:T(4,128)} %fiber_ref.1) | copy-start | bytes 36868
  2.0 9.7 %collective-permute-start = (f32[32,768]{1,0:T(8,128)S(1)}, f32[32,768]{1,0:T(8,128)S(1)}, u32[]{:S(2)}, u32[]{:S(2)}) collective-permute-start(f32[32,768]{1,0:T(8,128)S(1)} %get-tuple-element.35), channel_id=1, source_target_pairs={{0,1},{1,0},{2,3},{3,2},{4,5},{5,4},{6,7},{7,6},{8,9},{9,8},{10,11... | collective-permute-start | bytes 294920 | tf_op jit(solution)/shard_map/ppermute | solution.py:523
  2.1 9.6 %collective-permute-start.1 = (f32[32,768]{1,0:T(8,128)S(1)}, f32[32,768]{1,0:T(8,128)S(1)}, u32[]{:S(2)}, u32[]{:S(2)}) collective-permute-start(f32[32,768]{1,0:T(8,128)S(1)} %get-tuple-element.36), channel_id=1, source_target_pairs={{0,15},{1,2},{2,1},{3,4},{4,3},{5,6},{6,5},{7,8},{8,7},{9,10},{10,... | collective-permute-start | bytes 294920 | tf_op jit(solution)/shard_map/ppermute | solution.py:523
  11.8 8.3 %collective-permute-start.4 = (f32[104,768]{1,0:T(8,128)S(1)}, f32[104,768]{1,0:T(8,128)S(1)}, u32[]{:S(2)}, u32[]{:S(2)}) collective-permute-start(f32[104,768]{1,0:T(8,128)S(1)} %get-tuple-element.44), channel_id=1, source_target_pairs={{0,1},{1,0},{2,3},{3,2},{4,5},{5,4},{6,7},{7,6},{8,9},{9,8},{10,11... | collective-permute-start | bytes 958472 | tf_op jit(solution)/shard_map/ppermute | solution.py:523
  11.9 8.2 %collective-permute-start.5 = (f32[104,768]{1,0:T(8,128)S(1)}, f32[104,768]{1,0:T(8,128)S(1)}, u32[]{:S(2)}, u32[]{:S(2)}) collective-permute-start(f32[104,768]{1,0:T(8,128)S(1)} %get-tuple-element.45), channel_id=1, source_target_pairs={{0,15},{1,2},{2,1},{3,4},{4,3},{5,6},{6,5},{7,8},{8,7},{9,10},{10,... | collective-permute-start | bytes 958472 | tf_op jit(solution)/shard_map/ppermute | solution.py:523
  13.6 6.5 %collective-permute-start.2 = (f32[20,768]{1,0:T(8,128)S(1)}, f32[20,768]{1,0:T(8,128)S(1)}, u32[]{:S(2)}, u32[]{:S(2)}) collective-permute-start(f32[20,768]{1,0:T(8,128)S(1)} %get-tuple-element.41), channel_id=1, source_target_pairs={{0,16},{16,0},{32,48},{48,32},{64,80},{80,64},{96,112},{112,96},{1... | collective-permute-start | bytes 184328 | tf_op jit(solution)/shard_map/ppermute | solution.py:523
  14.1 6.0 %collective-permute-start.3 = (f32[20,768]{1,0:T(8,128)S(1)}, f32[20,768]{1,0:T(8,128)S(1)}, u32[]{:S(2)}, u32[]{:S(2)}) collective-permute-start(f32[20,768]{1,0:T(8,128)S(1)} %get-tuple-element.42), channel_id=1, source_target_pairs={{0,240},{16,32},{32,16},{48,64},{64,48},{80,96},{96,80},{112,128},... | collective-permute-start | bytes 184328 | tf_op jit(solution)/shard_map/ppermute | solution.py:523
  21.3 7.8 %collective-permute-start.6 = (f32[18,768]{1,0:T(8,128)S(1)}, f32[18,768]{1,0:T(8,128)S(1)}, u32[]{:S(2)}, u32[]{:S(2)}) collective-permute-start(f32[18,768]{1,0:T(8,128)S(1)} %get-tuple-element.52), channel_id=1, source_target_pairs={{0,16},{16,0},{32,48},{48,32},{64,80},{80,64},{96,112},{112,96},{1... | collective-permute-start | bytes 165896 | tf_op jit(solution)/shard_map/ppermute | solution.py:523
  25.2 4.4 %collective-permute-start.7 = (f32[18,768]{1,0:T(8,128)S(1)}, f32[18,768]{1,0:T(8,128)S(1)}, u32[]{:S(2)}, u32[]{:S(2)}) collective-permute-start(f32[18,768]{1,0:T(8,128)S(1)} %get-tuple-element.53), channel_id=1, source_target_pairs={{0,240},{16,32},{32,16},{48,64},{64,48},{80,96},{96,80},{112,128},... | collective-permute-start | bytes 165896 | tf_op jit(solution)/shard_map/ppermute | solution.py:523

commit v6 on v5

--- a/solution.py
+++ b/solution.py
@@ -15,7 +15,7 @@
 STRIP = 48
 HALF = STRIP // 2
 CHUNK = 128
-MID = 8
+GROUPS = (1, 7, 10, 15)
 GATES = 6
 RECORD = GATES * NX + 2 * (NX // BLK)
 
@@ -68,9 +68,9 @@
     return below, above
 
 
-def faces_kernel(tissue_ref, states_ref, u_ref, ev_ref, od_ref, own_ref, tissue_s, v_s, sem):
+def faces_kernel(tissue_ref, states_ref, s_ref, u_ref, ev_ref, od_ref, own_ref, tissue_s, sem):
     loads = [pltpu.make_async_copy(tissue_ref, tissue_s, sem.at[0]),
-             pltpu.make_async_copy(states_ref.at[0], v_s, sem.at[1])]
+             pltpu.make_async_copy(states_ref.at[0], s_ref.at[0], sem.at[1])]
     for load in loads:
         load.start()
     onehot = lane_spread(NZ // BLK).astype(jnp.bfloat16)
@@ -80,7 +80,7 @@
     even = is_even("area")
     loads[1].wait()
     for x in range(NX):
-        u = v_s[x] * masks[x // BLK]
+        u = s_ref[0, x] * masks[x // BLK]
         u_ref[x] = u
         own_ref[0, x:x + 1] = u[0:1]
         own_ref[1, x:x + 1] = u[NY - 1:NY]
@@ -104,10 +104,10 @@
     return tables
 
 
-def load_kernel(tissue_ref, fiber_ref, states_ref, _after, s_ref, coefs_ref, ev_ref, od_ref, sem):
-    loads = [pltpu.make_async_copy(states_ref.at[k], s_ref.at[k], sem.at[k]) for k in range(8)]
-    for k in (1, 2, 3, 4, 5, 6, 0, 7):
-        loads[k].start()
+def load_kernel(tissue_ref, fiber_ref, states_ref, _kept, s_ref, coefs_ref, ev_ref, od_ref, sem):
+    loads = [pltpu.make_async_copy(states_ref.at[k + 1], s_ref.at[k + 1], sem.at[k]) for k in range(7)]
+    for load in loads:
+        load.start()
     kind = flat(fiber_ref)
     parts = [flat(tissue_ref).astype(f32)]
     for table in class_tables():
@@ -135,15 +135,14 @@
             ev_ref[place + block:place + block + 1] = choose(even, high, low)
             od_ref[place + block:place + block + 1] = choose(even, low, high)
     for k in range(GATES):
-        loads[k + 1].wait()
+        loads[k].wait()
         for x in range(NX):
             place = NX * k + x
             low = s_ref[k + 1, x, 0:1]
             high = s_ref[k + 1, x, NY - 1:NY]
             ev_ref[place:place + 1] = choose(even, high, low)
             od_ref[place:place + 1] = choose(even, low, high)
-    loads[0].wait()
-    loads[7].wait()
+    loads[6].wait()
 
 
 def message_kernel(area_ev_ref, area_od_ref, u_ref, _e, _o, ev_ref, od_ref, rows_ref, _gates_ev, _gates_od):
@@ -286,28 +285,31 @@
 
 def interior_kernel(last, refs):
     u_ref, coefs_ref, rows_ref = refs[1:4]
-    s_ref, shown_ref, base_ref = refs[4:7]
     if last:
         next_ref = None
-        final_ref, uy_s, uz_s, w_s, sem = refs[7:]
+        s_ref, shown_ref, base_ref, final_ref, uy_s, uz_s, w_s, sem = refs[4:]
     else:
-        next_ref, uy_s, uz_s, w_s = refs[7:]
+        s_ref, shown_ref, base_ref, next_ref, uy_s, uz_s, w_s = refs[4:]
     derive(range(NX), u_ref, coefs_ref, rows_ref, uy_s, uz_s, w_s)
     base_ref[0] = base_of(0, 1, 1.0, u_ref, coefs_ref, uy_s, uz_s, w_s)
     base_ref[1] = base_of(NX - 1, NX - 2, -1.0, u_ref, coefs_ref, uy_s, uz_s, w_s)
+    copies = []
     one = jnp.ones((NY, CHUNK), f32)
     zero = jnp.zeros((NY, CHUNK), f32)
-    interior_planes(range(1, MID), lambda cols: [(one, zero, zero)] * 2,
-                    s_ref, u_ref, next_ref, coefs_ref, uy_s, uz_s, w_s, shown_ref)
-    if last:
-        done = pl.ds(1, MID - 1)
-        store = pltpu.make_async_copy(s_ref.at[:, done], final_ref.at[:, done], sem)
-        store.start()
-    interior_planes(range(MID, NX - 1),
-                    lambda cols: [tuple(shown_ref[3 * f + k, :, cols] for k in range(3)) for f in range(2)],
-                    s_ref, u_ref, next_ref, coefs_ref, uy_s, uz_s, w_s, shown_ref)
-    if last:
-        store.wait()
+    for n in range(len(GROUPS) - 1):
+        def marches_of(cols):
+            if n == 0:
+                return [(one, zero, zero)] * 2
+            return [tuple(shown_ref[3 * f + k, :, cols] for k in range(3)) for f in range(2)]
+
+        interior_planes(range(GROUPS[n], GROUPS[n + 1]), marches_of,
+                        s_ref, u_ref, next_ref, coefs_ref, uy_s, uz_s, w_s, shown_ref)
+        if last and n < len(GROUPS) - 2:
+            done = pl.ds(GROUPS[n], GROUPS[n + 1] - GROUPS[n])
+            copies.append(pltpu.make_async_copy(s_ref.at[:, done], final_ref.at[:, done], sem.at[n]))
+            copies[n].start()
+    for copy in copies:
+        copy.wait()
 
 
 def outer_row(side, halos, rows_ref, own_ref, record):
@@ -349,7 +351,7 @@
     bases_ref, coefs_ref, depth_ev_ref, depth_od_ref, shown_ref = refs[:5]
     if last:
         earlier_ref, _, _, s_ref, final_ref, strips_ref, acc_s, uy_s, uz_s, sem = refs[5:]
-        done = pl.ds(MID, NX - 1 - MID)
+        done = pl.ds(GROUPS[-2], GROUPS[-1] - GROUPS[-2])
         stores = [pltpu.make_async_copy(s_ref.at[:, done], final_ref.at[:, done], sem.at[2])]
         stores[0].start()
     else:
@@ -402,13 +404,17 @@
     if not last:
         depth_messages(even, next_ref, ahead_ref, ev_ref, od_ref)
     else:
-        for k in range(3):
-            stack = jnp.concatenate(
-                [earlier_ref[k], earlier_ref[3 + k], acc_s[k], acc_s[3 + k]], axis=0)
-            stack = jnp.concatenate([stack, pltpu.roll(stack, NZ - HALF, axis=1)], axis=0)
-            turned = stack.T
-            for d in range(NZ // STRIP):
-                strips_ref[d, HALF * k:HALF * (k + 1)] = turned[STRIP * d:STRIP * d + HALF]
+        stacks = [jnp.concatenate([earlier_ref[k], earlier_ref[3 + k], acc_s[k], acc_s[3 + k]], axis=0)
+                  for k in range(3)]
+        turned = jnp.concatenate(stacks[:2], axis=0).T
+        greens = jnp.concatenate([stacks[2], pltpu.roll(stacks[2], NZ - HALF, axis=1)], axis=0).T
+        left = lax.broadcasted_iota(jnp.int32, (1, 128), 1) < 64
+        for d in range(NZ // STRIP):
+            start = STRIP * d
+            a, b = turned[start:start + HALF], turned[start + HALF:start + STRIP]
+            strips_ref[d, 0:HALF] = jnp.where(left, a, pltpu.roll(b, 64, axis=1))
+            strips_ref[d, HALF:2 * HALF] = jnp.where(left, pltpu.roll(a, 64, axis=1), b)
+            strips_ref[d, 2 * HALF:3 * HALF] = greens[start:start + HALF]
         for store in stores:
             store.wait()
 
@@ -471,7 +477,7 @@
     if last:
         out_specs += [anywhere()]
         out_shape += kept_in(pltpu.HBM, VOLUME)
-        scratch += [COPY]
+        scratch += [COPY((len(GROUPS) - 2,))]
     else:
         out_specs += [inside()]
         out_shape += kept_in(pltpu.VMEM, FIELD)
@@ -527,24 +533,25 @@
     blocks = (NX // BLK, NY // BLK, NZ // BLK)
     states = pltpu.with_memory_space_constraint(states, pltpu.HBM)
     tissue = pltpu.with_memory_space_constraint(tissue, pltpu.HBM)
-    u, ev, od, own = pl.pallas_call(
+    kept, u, ev, od, own = pl.pallas_call(
         faces_kernel,
         in_specs=[anywhere(), anywhere()],
-        out_shape=kept_in(pltpu.VMEM, FIELD, (2 * NX, NZ), (2 * NX, NZ), (2, NX, NZ)),
-        scratch_shapes=[pltpu.VMEM(blocks, jnp.int32), pltpu.VMEM(FIELD, f32), COPY((2,))],
+        out_shape=kept_in(pltpu.VMEM, VOLUME, FIELD, (2 * NX, NZ), (2 * NX, NZ), (2, NX, NZ)),
+        scratch_shapes=[pltpu.VMEM(blocks, jnp.int32), COPY((2,))],
         compiler_params=params(4),
         name="faces",
     )(tissue, states)
     area = swap("area", 0, ev), swap("area", 1, od)
     states, coefs, ev, od = pl.pallas_call(
         load_kernel,
-        in_specs=[inside(), inside(), anywhere(), anywhere()],
+        in_specs=[inside(), inside(), anywhere(), inside()],
         out_shape=kept_in(pltpu.VMEM, VOLUME, (7, 64, NZ), (RECORD, NZ), (RECORD, NZ)),
-        scratch_shapes=[COPY((8,))],
+        scratch_shapes=[COPY((7,))],
+        input_output_aliases={3: 0},
         compiler_params=params(4),
         cost_estimate=pl.CostEstimate(flops=10**7, bytes_accessed=8 * 10**6, transcendentals=0),
         name="load",
-    )(tissue, fiber, states, own)
+    )(tissue, fiber, states, kept)
     ev, od, rows, gates_ev, gates_od = pl.pallas_call(
         message_kernel,
         in_specs=[inside()] * 3 + [anywhere()] * 2,

time: 50.1 us -> 49.8 us (level)
  transfers between devices with their start and end apart: 8 -> 8, of which waited for: 1 -> 1; matrix products, arithmetic and copies ran while one was open for 0% -> 0% of each run, Pallas kernels for 23% -> 22%
where the time goes in v6:
time: 49.8 us; the launch traced here: 49.6 us
  blocking collectives  17.5 us (35%)
  Pallas kernels  16.2 us (33%)
  starting transfers between devices  14.7 us (30%)
  between operations  0.76 us (2%)
    all_to_all x1, blocking collectives, per_device(): lax.all_to_all(strips, 'depth', split_axis=0, concat_axis=0, tiled=True)  17.5 us
    ppermute x8, starting transfers between devices, swap(): return lax.ppermute(message, axis, swaps(axis)[which])  14.7 us
    pallas_call x2, Pallas kernels, interior(): pl.pallas_call(lambda *refs: interior_kernel(last, refs), in_specs=[insid...  7.72 us
    pallas_call x1, Pallas kernels, per_device(): pl.pallas_call(load_kernel, in_specs=[inside(), inside(), anywhere(), ins...  3.4 us
    pallas_call x2, Pallas kernels, ends(): pl.pallas_call(lambda *refs: ends_body(last, refs), in_specs=in_specs, ou...  2.75 us
    pallas_call x1, Pallas kernels, per_device(): pl.pallas_call(faces_kernel, in_specs=[anywhere(), anywhere()], out_shape...  1.36 us
  transfers between devices with their start and end apart: 8, of which 1 were waited for; matrix products, arithmetic and copies ran while one was open for 0% of the time, Pallas kernels for 22%

profile of v6, /device:TPU:2, one launch (start us, length us, event | category | flops | bytes accessed | tf_op | source)
XLA Modules:
  0.0 49.6 jit_solution(17638100187303599839)
XLA Ops:
  0.6 0.0 copy-start
  0.6 1.4 %faces.1 = (f32[8,16,16,768]{3,2,1,0:T(8,128)S(1)}, f32[16,16,768]{2,1,0:T(8,128)S(1)}, f32[32,768]{1,0:T(8,128)S(1)}, f32[32,768]{1,0:T(8,128)S(1)}, f32[2,16,768]{2,1,0:T(8,128)S(1)}) custom-call(s32[4,4,192]{2,1,0:T(4,128)} %tissue_ref.3, f32[8,16,16,768]{3,2,1,0:T(8,128)} %states_ref.3), custom_call_target="tpu_custom_call" | custom-call | tf_op jit(solution)/shard_map/faces/pallas_call | solution.py:536
  2.0 0.1 collective-permute-start
  2.1 6.0 %collective-permute-start.1 = (f32[32,768]{1,0:T(8,128)S(1)}, f32[32,768]{1,0:T(8,128)S(1)}, u32[]{:S(2)}, u32[]{:S(2)}) collective-permute-start(f32[32,768]{1,0:T(8,128)S(1)} %get-tuple-element.37), channel_id=1, source_target_pairs={{0,15},{1,2},{2,1},{3,4},{4,3},{5,6},{6,5},{7,8},{8,7},{9,10},{10,... | collective-permute-start | bytes 294920 | tf_op jit(solution)/shard_map/ppermute | solution.py:529
  8.1 0.0 copy-done
  8.1 3.4 %load.1 = (f32[8,16,16,768]{3,2,1,0:T(8,128)S(1)}, f32[7,64,768]{2,1,0:T(8,128)S(1)}, f32[104,768]{1,0:T(8,128)S(1)}, f32[104,768]{1,0:T(8,128)S(1)}) custom-call(s32[4,4,192]{2,1,0:T(4,128)} %tissue_ref.3, s32[4,4,192]{2,1,0:T(4,128)S(1)} %copy-done, f32[8,16,16,768]{3,2,1,0:T(8,128)} %states_ref.3, ...), custom_call_target="tpu_custom_call", output_to_operand_aliasing={{0}: (3, {})} | custom-call | flops 10000000 | bytes 8000000 | tf_op jit(solution)/shard_map/load/pallas_call | solution.py:545
  11.5 0.0 collective-permute-done.area_ev_ref
  11.5 0.0 collective-permute-done.1.area_od_ref
  11.5 0.1 collective-permute-start.4
  11.6 1.9 %collective-permute-start.5 = (f32[104,768]{1,0:T(8,128)S(1)}, f32[104,768]{1,0:T(8,128)S(1)}, u32[]{:S(2)}, u32[]{:S(2)}) collective-permute-start(f32[104,768]{1,0:T(8,128)S(1)} %get-tuple-element.46), channel_id=1, source_target_pairs={{0,15},{1,2},{2,1},{3,4},{4,3},{5,6},{6,5},{7,8},{8,7},{9,10},{10,... | collective-permute-start | bytes 958472 | tf_op jit(solution)/shard_map/ppermute | solution.py:529
  13.5 0.5 %collective-permute-start.2 = (f32[20,768]{1,0:T(8,128)S(1)}, f32[20,768]{1,0:T(8,128)S(1)}, u32[]{:S(2)}, u32[]{:S(2)}) collective-permute-start(f32[20,768]{1,0:T(8,128)S(1)} %get-tuple-element.42), channel_id=1, source_target_pairs={{0,16},{16,0},{32,48},{48,32},{64,80},{80,64},{96,112},{112,96},{1... | collective-permute-start | bytes 184328 | tf_op jit(solution)/shard_map/ppermute | solution.py:529
  14.1 2.2 %collective-permute-start.3 = (f32[20,768]{1,0:T(8,128)S(1)}, f32[20,768]{1,0:T(8,128)S(1)}, u32[]{:S(2)}, u32[]{:S(2)}) collective-permute-start(f32[20,768]{1,0:T(8,128)S(1)} %get-tuple-element.43), channel_id=1, source_target_pairs={{0,240},{16,32},{32,16},{48,64},{64,48},{80,96},{96,80},{112,128},... | collective-permute-start | bytes 184328 | tf_op jit(solution)/shard_map/ppermute | solution.py:529
  16.2 3.8 %interior_first.1 = (f32[8,16,16,768]{3,2,1,0:T(8,128)S(1)}, f32[6,16,768]{2,1,0:T(8,128)S(1)}, f32[2,16,768]{2,1,0:T(8,128)S(1)}, f32[16,16,768]{2,1,0:T(8,128)S(1)}) custom-call(f32[8,16,16,768]{3,2,1,0:T(8,128)S(1)} %get-tuple-element.33.refs_0_, f32[16,16,768]{2,1,0:T(8,128)S(1)} %get-tuple-element.34.u_ref.refs_1_, ...), custom_call_target="tpu_custom_call", output_to_operand_aliasing={{0}: (0, {})} | custom-call | flops 78643200 | bytes 6291456 | tf_op jit(solution)/shard_map/interior_first/pallas_call | solution.py:484
  20.1 0.0 collective-permute-done.2.refs_2_
  20.1 0.0 collective-permute-done.3.refs_3_
  20.1 0.0 collective-permute-done.4.refs_5_
  20.1 0.0 collective-permute-done.5.refs_6_
  20.1 1.2 %ends_first.1 = (f32[8,16,16,768]{3,2,1,0:T(8,128)S(1)}, f32[16,16,768]{2,1,0:T(8,128)S(1)}, f32[6,16,768]{2,1,0:T(8,128)S(1)}, f32[2,16,768]{2,1,0:T(8,128)S(1)...) custom-call(f32[2,16,768]{2,1,0:T(8,128)S(1)} %get-tuple-element.41.refs_0_, ...), custom_call_target="tpu_custom_call", output_to_operand_aliasing={{0}: (9, {}), {1}: (10, {})} | custom-call | tf_op jit(solution)/shard_map/ends_first/pallas_call | solution.py:511
  21.3 4.0 %collective-permute-start.6 = (f32[18,768]{1,0:T(8,128)S(1)}, f32[18,768]{1,0:T(8,128)S(1)}, u32[]{:S(2)}, u32[]{:S(2)}) collective-permute-start(f32[18,768]{1,0:T(8,128)S(1)} %get-tuple-element.54), channel_id=1, source_target_pairs={{0,16},{16,0},{32,48},{48,32},{64,80},{80,64},{96,112},{112,96},{1... | collective-permute-start | bytes 165896 | tf_op jit(solution)/shard_map/ppermute | solution.py:529
  25.3 0.0 collective-permute-start.7
  25.3 3.9 %interior_last.1 = (f32[8,16,16,768]{3,2,1,0:T(8,128)S(1)}, f32[6,16,768]{2,1,0:T(8,128)S(1)}, f32[2,16,768]{2,1,0:T(8,128)S(1)}, f32[8,16,16,768]{3,2,1,0:T(8,128)}) custom-call(f32[8,16,16,768]{3,2,1,0:T(8,128)S(1)} %get-tuple-element.50.refs_0_, f32[16,16,768]{2,1,0:T(8,128)S(1)} %get-tuple-element.51.refs_1_, ...), custom_call_target="tpu_custom_call", output_to_operand_aliasing={{0}: (0, {})} | custom-call | flops 78643200 | bytes 6291456 | tf_op jit(solution)/shard_map/interior_last/pallas_call | solution.py:484
  29.2 0.0 collective-permute-done.6.refs_2_
  29.2 0.4 collective-permute-done.7.refs_3_
  29.6 1.6 %ends_last.1 = (f32[8,16,16,768]{3,2,1,0:T(8,128)S(1)}, f32[8,16,16,768]{3,2,1,0:T(8,128)}, f32[16,72,128]{2,1,0:T(8,128)S(1)}) custom-call(f32[2,16,768]{2,1,0:T(8,128)S(1)} %get-tuple-element.53.refs_0_, f32[7,64,768]{2,1,0:T(8,128)S(1)} %get-tuple-element.35.refs_2_.refs_1_, ...), custom_call_target="tpu_custom_call", output_to_operand_aliasing={{0}: (6, {}), {1}: (7, {})} | custom-call | tf_op jit(solution)/shard_map/ends_last/pallas_call | solution.py:511
  31.2 17.5 %all_to_all.5.strips_ref = f32[16,72,128]{2,1,0:T(8,128)S(1)} all-to-all(f32[16,72,128]{2,1,0:T(8,128)S(1)} %get-tuple-element.61), channel_id=1, replica_groups=mesh['depth'=16,'area'=16] {'depth'}, dimensions={0} | all-to-all | bytes 1179648 | tf_op jit(solution)/shard_map/all_to_all | solution.py:572
  48.7 0.9 %composite.1 = f32[2,2,4,16,48]{4,3,2,1,0:T(8,128)} custom-call(f32[16,72,128]{2,1,0:T(8,128)S(1)} %all_to_all.5.strips_ref), custom_call_target="tpu_custom_call" | custom-call | tf_op jit(solution)/shard_map/composite/pallas_call | solution.py:573
  (1 shorter events, 0.0 us)
Async XLA Ops:
  0.6 7.4 %copy-start = (s32[4,4,192]{2,1,0:T(4,128)S(1)}, s32[4,4,192]{2,1,0:T(4,128)}, u32[]{:S(2)}) copy-start(s32[4,4,192]{2,1,0:T(4,128)} %fiber_ref.1) | copy-start | bytes 36868
  2.0 9.5 %collective-permute-start = (f32[32,768]{1,0:T(8,128)S(1)}, f32[32,768]{1,0:T(8,128)S(1)}, u32[]{:S(2)}, u32[]{:S(2)}) collective-permute-start(f32[32,768]{1,0:T(8,128)S(1)} %get-tuple-element.36), channel_id=1, source_target_pairs={{0,1},{1,0},{2,3},{3,2},{4,5},{5,4},{6,7},{7,6},{8,9},{9,8},{10,11... | collective-permute-start | bytes 294920 | tf_op jit(solution)/shard_map/ppermute | solution.py:529
  2.1 9.4 %collective-permute-start.1 = (f32[32,768]{1,0:T(8,128)S(1)}, f32[32,768]{1,0:T(8,128)S(1)}, u32[]{:S(2)}, u32[]{:S(2)}) collective-permute-start(f32[32,768]{1,0:T(8,128)S(1)} %get-tuple-element.37), channel_id=1, source_target_pairs={{0,15},{1,2},{2,1},{3,4},{4,3},{5,6},{6,5},{7,8},{8,7},{9,10},{10,... | collective-permute-start | bytes 294920 | tf_op jit(solution)/shard_map/ppermute | solution.py:529
  11.5 8.5 %collective-permute-start.4 = (f32[104,768]{1,0:T(8,128)S(1)}, f32[104,768]{1,0:T(8,128)S(1)}, u32[]{:S(2)}, u32[]{:S(2)}) collective-permute-start(f32[104,768]{1,0:T(8,128)S(1)} %get-tuple-element.45), channel_id=1, source_target_pairs={{0,1},{1,0},{2,3},{3,2},{4,5},{5,4},{6,7},{7,6},{8,9},{9,8},{10,11... | collective-permute-start | bytes 958472 | tf_op jit(solution)/shard_map/ppermute | solution.py:529
  11.6 8.5 %collective-permute-start.5 = (f32[104,768]{1,0:T(8,128)S(1)}, f32[104,768]{1,0:T(8,128)S(1)}, u32[]{:S(2)}, u32[]{:S(2)}) collective-permute-start(f32[104,768]{1,0:T(8,128)S(1)} %get-tuple-element.46), channel_id=1, source_target_pairs={{0,15},{1,2},{2,1},{3,4},{4,3},{5,6},{6,5},{7,8},{8,7},{9,10},{10,... | collective-permute-start | bytes 958472 | tf_op jit(solution)/shard_map/ppermute | solution.py:529
  13.5 6.5 %collective-permute-start.2 = (f32[20,768]{1,0:T(8,128)S(1)}, f32[20,768]{1,0:T(8,128)S(1)}, u32[]{:S(2)}, u32[]{:S(2)}) collective-permute-start(f32[20,768]{1,0:T(8,128)S(1)} %get-tuple-element.42), channel_id=1, source_target_pairs={{0,16},{16,0},{32,48},{48,32},{64,80},{80,64},{96,112},{112,96},{1... | collective-permute-start | bytes 184328 | tf_op jit(solution)/shard_map/ppermute | solution.py:529
  14.1 6.0 %collective-permute-start.3 = (f32[20,768]{1,0:T(8,128)S(1)}, f32[20,768]{1,0:T(8,128)S(1)}, u32[]{:S(2)}, u32[]{:S(2)}) collective-permute-start(f32[20,768]{1,0:T(8,128)S(1)} %get-tuple-element.43), channel_id=1, source_target_pairs={{0,240},{16,32},{32,16},{48,64},{64,48},{80,96},{96,80},{112,128},... | collective-permute-start | bytes 184328 | tf_op jit(solution)/shard_map/ppermute | solution.py:529
  21.3 7.9 %collective-permute-start.6 = (f32[18,768]{1,0:T(8,128)S(1)}, f32[18,768]{1,0:T(8,128)S(1)}, u32[]{:S(2)}, u32[]{:S(2)}) collective-permute-start(f32[18,768]{1,0:T(8,128)S(1)} %get-tuple-element.54), channel_id=1, source_target_pairs={{0,16},{16,0},{32,48},{48,32},{64,80},{80,64},{96,112},{112,96},{1... | collective-permute-start | bytes 165896 | tf_op jit(solution)/shard_map/ppermute | solution.py:529
  25.3 4.4 %collective-permute-start.7 = (f32[18,768]{1,0:T(8,128)S(1)}, f32[18,768]{1,0:T(8,128)S(1)}, u32[]{:S(2)}, u32[]{:S(2)}) collective-permute-start(f32[18,768]{1,0:T(8,128)S(1)} %get-tuple-element.55), channel_id=1, source_target_pairs={{0,240},{16,32},{32,16},{48,64},{64,48},{80,96},{96,80},{112,128},... | collective-permute-start | bytes 165896 | tf_op jit(solution)/shard_map/ppermute | solution.py:529

commit v7 on v6

--- a/solution.py
+++ b/solution.py
@@ -17,7 +17,7 @@
 CHUNK = 128
 GROUPS = (1, 7, 10, 15)
 GATES = 6
-RECORD = GATES * NX + 2 * (NX // BLK)
+RECORD = GATES * NX + 8 * (NX // BLK)
 
 TIME_STEP = 0.15
 SIGMA_LONG = 1.0
@@ -69,8 +69,10 @@
 
 
 def faces_kernel(tissue_ref, states_ref, s_ref, u_ref, ev_ref, od_ref, own_ref, tissue_s, sem):
-    loads = [pltpu.make_async_copy(tissue_ref, tissue_s, sem.at[0]),
-             pltpu.make_async_copy(states_ref.at[0], s_ref.at[0], sem.at[1])]
+    loads = [pltpu.make_async_copy(tissue_ref, tissue_s, sem.at[0])]
+    for block in range(NX // BLK):
+        part = pl.ds(BLK * block, BLK)
+        loads.append(pltpu.make_async_copy(states_ref.at[0, part], s_ref.at[0, part], sem.at[1 + block]))
     for load in loads:
         load.start()
     onehot = lane_spread(NZ // BLK).astype(jnp.bfloat16)
@@ -78,8 +80,9 @@
     wide = jnp.dot(flat(tissue_s).astype(f32).astype(jnp.bfloat16), onehot, preferred_element_type=f32)
     masks = [spread_y(wide, BLK * block) for block in range(NX // BLK)]
     even = is_even("area")
-    loads[1].wait()
     for x in range(NX):
+        if x % BLK == 0:
+            loads[1 + x // BLK].wait()
         u = s_ref[0, x] * masks[x // BLK]
         u_ref[x] = u
         own_ref[0, x:x + 1] = u[0:1]
@@ -115,7 +118,6 @@
         for c in range(1, CLASSES):
             part = jnp.where(kind == c, table[c], part)
         parts.append(part)
-    parts.append(kind.astype(f32))
     rest = jnp.concatenate(parts, axis=0)
     onehot = lane_spread(NZ // BLK).astype(jnp.bfloat16)
     wide = None
@@ -128,7 +130,8 @@
         for block in range(4):
             coefs_ref[k, NY * block:NY * (block + 1)] = spread_y(wide, 16 * k + 4 * block)
     even = is_even("area")
-    for place, part in ((GATES * NX, 0), (GATES * NX + 4, 7)):
+    for part in range(7):
+        place = GATES * NX + BLK * part
         for block in range(4):
             low = wide[16 * part + 4 * block:16 * part + 4 * block + 1]
             high = wide[16 * part + 4 * block + 3:16 * part + 4 * block + 4]
@@ -142,6 +145,9 @@
             high = s_ref[k + 1, x, NY - 1:NY]
             ev_ref[place:place + 1] = choose(even, high, low)
             od_ref[place:place + 1] = choose(even, low, high)
+    spare = pl.ds(GATES * NX + 7 * BLK, BLK)
+    ev_ref[spare] = jnp.zeros((BLK, NZ), f32)
+    od_ref[spare] = jnp.zeros((BLK, NZ), f32)
     loads[6].wait()
 
 
@@ -325,13 +331,7 @@
     slopes = [turn * (across(h, far_place) - across(h, own_place)) for h in halos]
     zs = [across(z_slope(h), near_place) for h in halos]
     mask = spread_y(record[GATES * NX:GATES * NX + 4], 0)
-    kind = spread_y(record[GATES * NX + 4:GATES * NX + 8], 0)
-    coefs = []
-    for table in class_tables():
-        coef = jnp.full(kind.shape, table[0], f32)
-        for c in range(1, CLASSES):
-            coef = jnp.where(kind == float(c), table[c], coef)
-        coefs.append(coef)
+    coefs = [spread_y(record[GATES * NX + BLK * k:GATES * NX + BLK * (k + 1)], 0) for k in range(1, 7)]
     x_after, x_before = y_sides(near, across(halos[0], near_place), across(halos[1], near_place))
     z_after, z_before = z_sides(near)
     w = (
@@ -537,7 +537,7 @@
         faces_kernel,
         in_specs=[anywhere(), anywhere()],
         out_shape=kept_in(pltpu.VMEM, VOLUME, FIELD, (2 * NX, NZ), (2 * NX, NZ), (2, NX, NZ)),
-        scratch_shapes=[pltpu.VMEM(blocks, jnp.int32), COPY((2,))],
+        scratch_shapes=[pltpu.VMEM(blocks, jnp.int32), COPY((1 + NX // BLK,))],
         compiler_params=params(4),
         name="faces",
     )(tissue, states)

time: 49.8 us -> 49.6 us (level)
  no operation moved by 1% of the time
where the time goes in v7:
time: 49.6 us; the launch traced here: 49.4 us
  blocking collectives  17.5 us (35%)
  Pallas kernels  15.9 us (32%)
  starting transfers between devices  14.7 us (30%)
  between operations  0.76 us (2%)
    all_to_all x1, blocking collectives, per_device(): lax.all_to_all(strips, 'depth', split_axis=0, concat_axis=0, tiled=True)  17.5 us
    ppermute x8, starting transfers between devices, swap(): return lax.ppermute(message, axis, swaps(axis)[which])  14.7 us
    pallas_call x2, Pallas kernels, interior(): pl.pallas_call(lambda *refs: interior_kernel(last, refs), in_specs=[insid...  7.7 us
    pallas_call x1, Pallas kernels, per_device(): pl.pallas_call(load_kernel, in_specs=[inside(), inside(), anywhere(), ins...  3.36 us
    pallas_call x2, Pallas kernels, ends(): pl.pallas_call(lambda *refs: ends_body(last, refs), in_specs=in_specs, ou...  2.57 us
    pallas_call x1, Pallas kernels, per_device(): pl.pallas_call(faces_kernel, in_specs=[anywhere(), anywhere()], out_shape...  1.33 us
  transfers between devices with their start and end apart: 8, of which 1 were waited for; matrix products, arithmetic and copies ran while one was open for 0% of the time, Pallas kernels for 22%

profile of v7, /device:TPU:2, one launch (start us, length us, event | category | flops | bytes accessed | tf_op | source)
XLA Modules:
  0.0 49.4 jit_solution(594581789834571257)
XLA Ops:
  0.6 0.0 copy-start
  0.6 1.3 %faces.1 = (f32[8,16,16,768]{3,2,1,0:T(8,128)S(1)}, f32[16,16,768]{2,1,0:T(8,128)S(1)}, f32[32,768]{1,0:T(8,128)S(1)}, f32[32,768]{1,0:T(8,128)S(1)}, f32[2,16,768]{2,1,0:T(8,128)S(1)}) custom-call(s32[4,4,192]{2,1,0:T(4,128)} %tissue_ref.3, f32[8,16,16,768]{3,2,1,0:T(8,128)} %states_ref.3), custom_call_target="tpu_custom_call" | custom-call | tf_op jit(solution)/shard_map/faces/pallas_call | solution.py:536
  2.0 0.1 collective-permute-start
  2.1 6.0 %collective-permute-start.1 = (f32[32,768]{1,0:T(8,128)S(1)}, f32[32,768]{1,0:T(8,128)S(1)}, u32[]{:S(2)}, u32[]{:S(2)}) collective-permute-start(f32[32,768]{1,0:T(8,128)S(1)} %get-tuple-element.37), channel_id=1, source_target_pairs={{0,15},{1,2},{2,1},{3,4},{4,3},{5,6},{6,5},{7,8},{8,7},{9,10},{10,... | collective-permute-start | bytes 294920 | tf_op jit(solution)/shard_map/ppermute | solution.py:529
  8.0 0.0 copy-done
  8.0 3.4 %load.1 = (f32[8,16,16,768]{3,2,1,0:T(8,128)S(1)}, f32[7,64,768]{2,1,0:T(8,128)S(1)}, f32[128,768]{1,0:T(8,128)S(1)}, f32[128,768]{1,0:T(8,128)S(1)}) custom-call(s32[4,4,192]{2,1,0:T(4,128)} %tissue_ref.3, s32[4,4,192]{2,1,0:T(4,128)S(1)} %copy-done, f32[8,16,16,768]{3,2,1,0:T(8,128)} %states_ref.3, ...), custom_call_target="tpu_custom_call", output_to_operand_aliasing={{0}: (3, {})} | custom-call | flops 10000000 | bytes 8000000 | tf_op jit(solution)/shard_map/load/pallas_call | solution.py:545
  11.4 0.0 collective-permute-done.area_ev_ref
  11.4 0.0 collective-permute-done.1.area_od_ref
  11.5 0.1 collective-permute-start.4
  11.6 1.9 %collective-permute-start.5 = (f32[128,768]{1,0:T(8,128)S(1)}, f32[128,768]{1,0:T(8,128)S(1)}, u32[]{:S(2)}, u32[]{:S(2)}) collective-permute-start(f32[128,768]{1,0:T(8,128)S(1)} %get-tuple-element.46), channel_id=1, source_target_pairs={{0,15},{1,2},{2,1},{3,4},{4,3},{5,6},{6,5},{7,8},{8,7},{9,10},{10,... | collective-permute-start | bytes 1179656 | tf_op jit(solution)/shard_map/ppermute | solution.py:529
  13.5 0.5 %collective-permute-start.2 = (f32[20,768]{1,0:T(8,128)S(1)}, f32[20,768]{1,0:T(8,128)S(1)}, u32[]{:S(2)}, u32[]{:S(2)}) collective-permute-start(f32[20,768]{1,0:T(8,128)S(1)} %get-tuple-element.42), channel_id=1, source_target_pairs={{0,16},{16,0},{32,48},{48,32},{64,80},{80,64},{96,112},{112,96},{1... | collective-permute-start | bytes 184328 | tf_op jit(solution)/shard_map/ppermute | solution.py:529
  14.1 2.2 %collective-permute-start.3 = (f32[20,768]{1,0:T(8,128)S(1)}, f32[20,768]{1,0:T(8,128)S(1)}, u32[]{:S(2)}, u32[]{:S(2)}) collective-permute-start(f32[20,768]{1,0:T(8,128)S(1)} %get-tuple-element.43), channel_id=1, source_target_pairs={{0,240},{16,32},{32,16},{48,64},{64,48},{80,96},{96,80},{112,128},... | collective-permute-start | bytes 184328 | tf_op jit(solution)/shard_map/ppermute | solution.py:529
  16.2 3.8 %interior_first.1 = (f32[8,16,16,768]{3,2,1,0:T(8,128)S(1)}, f32[6,16,768]{2,1,0:T(8,128)S(1)}, f32[2,16,768]{2,1,0:T(8,128)S(1)}, f32[16,16,768]{2,1,0:T(8,128)S(1)}) custom-call(f32[8,16,16,768]{3,2,1,0:T(8,128)S(1)} %get-tuple-element.33.refs_0_, f32[16,16,768]{2,1,0:T(8,128)S(1)} %get-tuple-element.34.u_ref.refs_1_, ...), custom_call_target="tpu_custom_call", output_to_operand_aliasing={{0}: (0, {})} | custom-call | flops 78643200 | bytes 6291456 | tf_op jit(solution)/shard_map/interior_first/pallas_call | solution.py:484
  20.0 0.0 collective-permute-done.2.refs_2_
  20.1 0.0 collective-permute-done.3.refs_3_
  20.1 0.0 collective-permute-done.4.refs_5_
  20.1 0.0 collective-permute-done.5.refs_6_
  20.1 1.0 %ends_first.1 = (f32[8,16,16,768]{3,2,1,0:T(8,128)S(1)}, f32[16,16,768]{2,1,0:T(8,128)S(1)}, f32[6,16,768]{2,1,0:T(8,128)S(1)}, f32[2,16,768]{2,1,0:T(8,128)S(1)...) custom-call(f32[2,16,768]{2,1,0:T(8,128)S(1)} %get-tuple-element.41.refs_0_, ...), custom_call_target="tpu_custom_call", output_to_operand_aliasing={{0}: (9, {}), {1}: (10, {})} | custom-call | tf_op jit(solution)/shard_map/ends_first/pallas_call | solution.py:511
  21.1 4.0 %collective-permute-start.6 = (f32[18,768]{1,0:T(8,128)S(1)}, f32[18,768]{1,0:T(8,128)S(1)}, u32[]{:S(2)}, u32[]{:S(2)}) collective-permute-start(f32[18,768]{1,0:T(8,128)S(1)} %get-tuple-element.54), channel_id=1, source_target_pairs={{0,16},{16,0},{32,48},{48,32},{64,80},{80,64},{96,112},{112,96},{1... | collective-permute-start | bytes 165896 | tf_op jit(solution)/shard_map/ppermute | solution.py:529
  25.1 0.0 collective-permute-start.7
  25.1 3.9 %interior_last.1 = (f32[8,16,16,768]{3,2,1,0:T(8,128)S(1)}, f32[6,16,768]{2,1,0:T(8,128)S(1)}, f32[2,16,768]{2,1,0:T(8,128)S(1)}, f32[8,16,16,768]{3,2,1,0:T(8,128)}) custom-call(f32[8,16,16,768]{3,2,1,0:T(8,128)S(1)} %get-tuple-element.50.refs_0_, f32[16,16,768]{2,1,0:T(8,128)S(1)} %get-tuple-element.51.refs_1_, ...), custom_call_target="tpu_custom_call", output_to_operand_aliasing={{0}: (0, {})} | custom-call | flops 78643200 | bytes 6291456 | tf_op jit(solution)/shard_map/interior_last/pallas_call | solution.py:484
  29.0 0.0 collective-permute-done.6.refs_2_
  29.0 0.5 collective-permute-done.7.refs_3_
  29.4 1.6 %ends_last.1 = (f32[8,16,16,768]{3,2,1,0:T(8,128)S(1)}, f32[8,16,16,768]{3,2,1,0:T(8,128)}, f32[16,72,128]{2,1,0:T(8,128)S(1)}) custom-call(f32[2,16,768]{2,1,0:T(8,128)S(1)} %get-tuple-element.53.refs_0_, f32[7,64,768]{2,1,0:T(8,128)S(1)} %get-tuple-element.35.refs_2_.refs_1_, ...), custom_call_target="tpu_custom_call", output_to_operand_aliasing={{0}: (6, {}), {1}: (7, {})} | custom-call | tf_op jit(solution)/shard_map/ends_last/pallas_call | solution.py:511
  31.0 17.5 %all_to_all.5.strips_ref = f32[16,72,128]{2,1,0:T(8,128)S(1)} all-to-all(f32[16,72,128]{2,1,0:T(8,128)S(1)} %get-tuple-element.61), channel_id=1, replica_groups=mesh['depth'=16,'area'=16] {'depth'}, dimensions={0} | all-to-all | bytes 1179648 | tf_op jit(solution)/shard_map/all_to_all | solution.py:572
  48.5 0.9 %composite.1 = f32[2,2,4,16,48]{4,3,2,1,0:T(8,128)} custom-call(f32[16,72,128]{2,1,0:T(8,128)S(1)} %all_to_all.5.strips_ref), custom_call_target="tpu_custom_call" | custom-call | tf_op jit(solution)/shard_map/composite/pallas_call | solution.py:573
  (1 shorter events, 0.0 us)
Async XLA Ops:
  0.6 7.4 %copy-start = (s32[4,4,192]{2,1,0:T(4,128)S(1)}, s32[4,4,192]{2,1,0:T(4,128)}, u32[]{:S(2)}) copy-start(s32[4,4,192]{2,1,0:T(4,128)} %fiber_ref.1) | copy-start | bytes 36868
  2.0 9.4 %collective-permute-start = (f32[32,768]{1,0:T(8,128)S(1)}, f32[32,768]{1,0:T(8,128)S(1)}, u32[]{:S(2)}, u32[]{:S(2)}) collective-permute-start(f32[32,768]{1,0:T(8,128)S(1)} %get-tuple-element.36), channel_id=1, source_target_pairs={{0,1},{1,0},{2,3},{3,2},{4,5},{5,4},{6,7},{7,6},{8,9},{9,8},{10,11... | collective-permute-start | bytes 294920 | tf_op jit(solution)/shard_map/ppermute | solution.py:529
  2.1 9.3 %collective-permute-start.1 = (f32[32,768]{1,0:T(8,128)S(1)}, f32[32,768]{1,0:T(8,128)S(1)}, u32[]{:S(2)}, u32[]{:S(2)}) collective-permute-start(f32[32,768]{1,0:T(8,128)S(1)} %get-tuple-element.37), channel_id=1, source_target_pairs={{0,15},{1,2},{2,1},{3,4},{4,3},{5,6},{6,5},{7,8},{8,7},{9,10},{10,... | collective-permute-start | bytes 294920 | tf_op jit(solution)/shard_map/ppermute | solution.py:529
  11.5 8.6 %collective-permute-start.4 = (f32[128,768]{1,0:T(8,128)S(1)}, f32[128,768]{1,0:T(8,128)S(1)}, u32[]{:S(2)}, u32[]{:S(2)}) collective-permute-start(f32[128,768]{1,0:T(8,128)S(1)} %get-tuple-element.45), channel_id=1, source_target_pairs={{0,1},{1,0},{2,3},{3,2},{4,5},{5,4},{6,7},{7,6},{8,9},{9,8},{10,11... | collective-permute-start | bytes 1179656 | tf_op jit(solution)/shard_map/ppermute | solution.py:529
  11.6 8.5 %collective-permute-start.5 = (f32[128,768]{1,0:T(8,128)S(1)}, f32[128,768]{1,0:T(8,128)S(1)}, u32[]{:S(2)}, u32[]{:S(2)}) collective-permute-start(f32[128,768]{1,0:T(8,128)S(1)} %get-tuple-element.46), channel_id=1, source_target_pairs={{0,15},{1,2},{2,1},{3,4},{4,3},{5,6},{6,5},{7,8},{8,7},{9,10},{10,... | collective-permute-start | bytes 1179656 | tf_op jit(solution)/shard_map/ppermute | solution.py:529
  13.5 6.5 %collective-permute-start.2 = (f32[20,768]{1,0:T(8,128)S(1)}, f32[20,768]{1,0:T(8,128)S(1)}, u32[]{:S(2)}, u32[]{:S(2)}) collective-permute-start(f32[20,768]{1,0:T(8,128)S(1)} %get-tuple-element.42), channel_id=1, source_target_pairs={{0,16},{16,0},{32,48},{48,32},{64,80},{80,64},{96,112},{112,96},{1... | collective-permute-start | bytes 184328 | tf_op jit(solution)/shard_map/ppermute | solution.py:529
  14.1 6.0 %collective-permute-start.3 = (f32[20,768]{1,0:T(8,128)S(1)}, f32[20,768]{1,0:T(8,128)S(1)}, u32[]{:S(2)}, u32[]{:S(2)}) collective-permute-start(f32[20,768]{1,0:T(8,128)S(1)} %get-tuple-element.43), channel_id=1, source_target_pairs={{0,240},{16,32},{32,16},{48,64},{64,48},{80,96},{96,80},{112,128},... | collective-permute-start | bytes 184328 | tf_op jit(solution)/shard_map/ppermute | solution.py:529
  21.1 7.9 %collective-permute-start.6 = (f32[18,768]{1,0:T(8,128)S(1)}, f32[18,768]{1,0:T(8,128)S(1)}, u32[]{:S(2)}, u32[]{:S(2)}) collective-permute-start(f32[18,768]{1,0:T(8,128)S(1)} %get-tuple-element.54), channel_id=1, source_target_pairs={{0,16},{16,0},{32,48},{48,32},{64,80},{80,64},{96,112},{112,96},{1... | collective-permute-start | bytes 165896 | tf_op jit(solution)/shard_map/ppermute | solution.py:529
  25.1 4.4 %collective-permute-start.7 = (f32[18,768]{1,0:T(8,128)S(1)}, f32[18,768]{1,0:T(8,128)S(1)}, u32[]{:S(2)}, u32[]{:S(2)}) collective-permute-start(f32[18,768]{1,0:T(8,128)S(1)} %get-tuple-element.55), channel_id=1, source_target_pairs={{0,240},{16,32},{32,16},{48,64},{64,48},{80,96},{96,80},{112,128},... | collective-permute-start | bytes 165896 | tf_op jit(solution)/shard_map/ppermute | solution.py:529

commit v8 on v7

--- a/solution.py
+++ b/solution.py
@@ -15,7 +15,7 @@
 STRIP = 48
 HALF = STRIP // 2
 CHUNK = 128
-GROUPS = (1, 7, 10, 15)
+GROUPS = (1, 6, 9, 12, 15)
 GATES = 6
 RECORD = GATES * NX + 8 * (NX // BLK)
 

time: 49.6 us -> 49.3 us (level)
  transfers between devices with their start and end apart: 8 -> 8, of which waited for: 1 -> 1; matrix products, arithmetic and copies ran while one was open for 0% -> 0% of each run, Pallas kernels for 22% -> 23%
where the time goes in v8:
time: 49.3 us; the launch traced here: 49.1 us
  blocking collectives  17.4 us (35%)
  Pallas kernels  16 us (32%)
  starting transfers between devices  14.7 us (30%)
  between operations  0.76 us (2%)
    all_to_all x1, blocking collectives, per_device(): lax.all_to_all(strips, 'depth', split_axis=0, concat_axis=0, tiled=True)  17.4 us
    ppermute x8, starting transfers between devices, swap(): return lax.ppermute(message, axis, swaps(axis)[which])  14.7 us
    pallas_call x2, Pallas kernels, interior(): pl.pallas_call(lambda *refs: interior_kernel(last, refs), in_specs=[insid...  8.1 us
    pallas_call x1, Pallas kernels, per_device(): pl.pallas_call(load_kernel, in_specs=[inside(), inside(), anywhere(), ins...  3.36 us
    pallas_call x2, Pallas kernels, ends(): pl.pallas_call(lambda *refs: ends_body(last, refs), in_specs=in_specs, ou...  2.31 us
    pallas_call x1, Pallas kernels, per_device(): pl.pallas_call(faces_kernel, in_specs=[anywhere(), anywhere()], out_shape...  1.33 us
  transfers between devices with their start and end apart: 8, of which 1 were waited for; matrix products, arithmetic and copies ran while one was open for 0% of the time, Pallas kernels for 23%

profile of v8, /device:TPU:2, one launch (start us, length us, event | category | flops | bytes accessed | tf_op | source)
XLA Modules:
  0.0 49.1 jit_solution(12742546607690083426)
XLA Ops:
  0.6 0.0 copy-start
  0.6 1.3 %faces.1 = (f32[8,16,16,768]{3,2,1,0:T(8,128)S(1)}, f32[16,16,768]{2,1,0:T(8,128)S(1)}, f32[32,768]{1,0:T(8,128)S(1)}, f32[32,768]{1,0:T(8,128)S(1)}, f32[2,16,768]{2,1,0:T(8,128)S(1)}) custom-call(s32[4,4,192]{2,1,0:T(4,128)} %tissue_ref.3, f32[8,16,16,768]{3,2,1,0:T(8,128)} %states_ref.3), custom_call_target="tpu_custom_call" | custom-call | tf_op jit(solution)/shard_map/faces/pallas_call | solution.py:536
  2.0 0.1 collective-permute-start
  2.1 6.0 %collective-permute-start.1 = (f32[32,768]{1,0:T(8,128)S(1)}, f32[32,768]{1,0:T(8,128)S(1)}, u32[]{:S(2)}, u32[]{:S(2)}) collective-permute-start(f32[32,768]{1,0:T(8,128)S(1)} %get-tuple-element.37), channel_id=1, source_target_pairs={{0,15},{1,2},{2,1},{3,4},{4,3},{5,6},{6,5},{7,8},{8,7},{9,10},{10,... | collective-permute-start | bytes 294920 | tf_op jit(solution)/shard_map/ppermute | solution.py:529
  8.0 0.0 copy-done
  8.0 3.4 %load.1 = (f32[8,16,16,768]{3,2,1,0:T(8,128)S(1)}, f32[7,64,768]{2,1,0:T(8,128)S(1)}, f32[128,768]{1,0:T(8,128)S(1)}, f32[128,768]{1,0:T(8,128)S(1)}) custom-call(s32[4,4,192]{2,1,0:T(4,128)} %tissue_ref.3, s32[4,4,192]{2,1,0:T(4,128)S(1)} %copy-done, f32[8,16,16,768]{3,2,1,0:T(8,128)} %states_ref.3, ...), custom_call_target="tpu_custom_call", output_to_operand_aliasing={{0}: (3, {})} | custom-call | flops 10000000 | bytes 8000000 | tf_op jit(solution)/shard_map/load/pallas_call | solution.py:545
  11.4 0.0 collective-permute-done.area_ev_ref
  11.4 0.0 collective-permute-done.1.area_od_ref
  11.5 0.1 collective-permute-start.4
  11.6 1.9 %collective-permute-start.5 = (f32[128,768]{1,0:T(8,128)S(1)}, f32[128,768]{1,0:T(8,128)S(1)}, u32[]{:S(2)}, u32[]{:S(2)}) collective-permute-start(f32[128,768]{1,0:T(8,128)S(1)} %get-tuple-element.46), channel_id=1, source_target_pairs={{0,15},{1,2},{2,1},{3,4},{4,3},{5,6},{6,5},{7,8},{8,7},{9,10},{10,... | collective-permute-start | bytes 1179656 | tf_op jit(solution)/shard_map/ppermute | solution.py:529
  13.5 0.5 %collective-permute-start.2 = (f32[20,768]{1,0:T(8,128)S(1)}, f32[20,768]{1,0:T(8,128)S(1)}, u32[]{:S(2)}, u32[]{:S(2)}) collective-permute-start(f32[20,768]{1,0:T(8,128)S(1)} %get-tuple-element.42), channel_id=1, source_target_pairs={{0,16},{16,0},{32,48},{48,32},{64,80},{80,64},{96,112},{112,96},{1... | collective-permute-start | bytes 184328 | tf_op jit(solution)/shard_map/ppermute | solution.py:529
  14.1 2.2 %collective-permute-start.3 = (f32[20,768]{1,0:T(8,128)S(1)}, f32[20,768]{1,0:T(8,128)S(1)}, u32[]{:S(2)}, u32[]{:S(2)}) collective-permute-start(f32[20,768]{1,0:T(8,128)S(1)} %get-tuple-element.43), channel_id=1, source_target_pairs={{0,240},{16,32},{32,16},{48,64},{64,48},{80,96},{96,80},{112,128},... | collective-permute-start | bytes 184328 | tf_op jit(solution)/shard_map/ppermute | solution.py:529
  16.2 3.9 %interior_first.1 = (f32[8,16,16,768]{3,2,1,0:T(8,128)S(1)}, f32[6,16,768]{2,1,0:T(8,128)S(1)}, f32[2,16,768]{2,1,0:T(8,128)S(1)}, f32[16,16,768]{2,1,0:T(8,128)S(1)}) custom-call(f32[8,16,16,768]{3,2,1,0:T(8,128)S(1)} %get-tuple-element.33.refs_0_, f32[16,16,768]{2,1,0:T(8,128)S(1)} %get-tuple-element.34.u_ref.refs_1_, ...), custom_call_target="tpu_custom_call", output_to_operand_aliasing={{0}: (0, {})} | custom-call | flops 78643200 | bytes 6291456 | tf_op jit(solution)/shard_map/interior_first/pallas_call | solution.py:484
  20.1 0.0 collective-permute-done.2.refs_2_
  20.1 0.0 collective-permute-done.3.refs_3_
  20.1 0.0 collective-permute-done.4.refs_5_
  20.1 0.0 collective-permute-done.5.refs_6_
  20.1 1.0 %ends_first.1 = (f32[8,16,16,768]{3,2,1,0:T(8,128)S(1)}, f32[16,16,768]{2,1,0:T(8,128)S(1)}, f32[6,16,768]{2,1,0:T(8,128)S(1)}, f32[2,16,768]{2,1,0:T(8,128)S(1)...) custom-call(f32[2,16,768]{2,1,0:T(8,128)S(1)} %get-tuple-element.41.refs_0_, ...), custom_call_target="tpu_custom_call", output_to_operand_aliasing={{0}: (9, {}), {1}: (10, {})} | custom-call | tf_op jit(solution)/shard_map/ends_first/pallas_call | solution.py:511
  21.2 4.0 %collective-permute-start.6 = (f32[18,768]{1,0:T(8,128)S(1)}, f32[18,768]{1,0:T(8,128)S(1)}, u32[]{:S(2)}, u32[]{:S(2)}) collective-permute-start(f32[18,768]{1,0:T(8,128)S(1)} %get-tuple-element.54), channel_id=1, source_target_pairs={{0,16},{16,0},{32,48},{48,32},{64,80},{80,64},{96,112},{112,96},{1... | collective-permute-start | bytes 165896 | tf_op jit(solution)/shard_map/ppermute | solution.py:529
  25.1 0.0 collective-permute-start.7
  25.1 4.2 %interior_last.1 = (f32[8,16,16,768]{3,2,1,0:T(8,128)S(1)}, f32[6,16,768]{2,1,0:T(8,128)S(1)}, f32[2,16,768]{2,1,0:T(8,128)S(1)}, f32[8,16,16,768]{3,2,1,0:T(8,128)}) custom-call(f32[8,16,16,768]{3,2,1,0:T(8,128)S(1)} %get-tuple-element.50.refs_0_, f32[16,16,768]{2,1,0:T(8,128)S(1)} %get-tuple-element.51.refs_1_, ...), custom_call_target="tpu_custom_call", output_to_operand_aliasing={{0}: (0, {})} | custom-call | flops 78643200 | bytes 6291456 | tf_op jit(solution)/shard_map/interior_last/pallas_call | solution.py:484
  29.4 0.0 collective-permute-done.6.refs_2_
  29.4 0.1 collective-permute-done.7.refs_3_
  29.5 1.3 %ends_last.1 = (f32[8,16,16,768]{3,2,1,0:T(8,128)S(1)}, f32[8,16,16,768]{3,2,1,0:T(8,128)}, f32[16,72,128]{2,1,0:T(8,128)S(1)}) custom-call(f32[2,16,768]{2,1,0:T(8,128)S(1)} %get-tuple-element.53.refs_0_, f32[7,64,768]{2,1,0:T(8,128)S(1)} %get-tuple-element.35.refs_2_.refs_1_, ...), custom_call_target="tpu_custom_call", output_to_operand_aliasing={{0}: (6, {}), {1}: (7, {})} | custom-call | tf_op jit(solution)/shard_map/ends_last/pallas_call | solution.py:511
  30.8 17.4 %all_to_all.5.strips_ref = f32[16,72,128]{2,1,0:T(8,128)S(1)} all-to-all(f32[16,72,128]{2,1,0:T(8,128)S(1)} %get-tuple-element.61), channel_id=1, replica_groups=mesh['depth'=16,'area'=16] {'depth'}, dimensions={0} | all-to-all | bytes 1179648 | tf_op jit(solution)/shard_map/all_to_all | solution.py:572
  48.2 0.9 %composite.1 = f32[2,2,4,16,48]{4,3,2,1,0:T(8,128)} custom-call(f32[16,72,128]{2,1,0:T(8,128)S(1)} %all_to_all.5.strips_ref), custom_call_target="tpu_custom_call" | custom-call | tf_op jit(solution)/shard_map/composite/pallas_call | solution.py:573
  (1 shorter events, 0.0 us)
Async XLA Ops:
  0.6 7.4 %copy-start = (s32[4,4,192]{2,1,0:T(4,128)S(1)}, s32[4,4,192]{2,1,0:T(4,128)}, u32[]{:S(2)}) copy-start(s32[4,4,192]{2,1,0:T(4,128)} %fiber_ref.1) | copy-start | bytes 36868
  2.0 9.4 %collective-permute-start = (f32[32,768]{1,0:T(8,128)S(1)}, f32[32,768]{1,0:T(8,128)S(1)}, u32[]{:S(2)}, u32[]{:S(2)}) collective-permute-start(f32[32,768]{1,0:T(8,128)S(1)} %get-tuple-element.36), channel_id=1, source_target_pairs={{0,1},{1,0},{2,3},{3,2},{4,5},{5,4},{6,7},{7,6},{8,9},{9,8},{10,11... | collective-permute-start | bytes 294920 | tf_op jit(solution)/shard_map/ppermute | solution.py:529
  2.1 9.3 %collective-permute-start.1 = (f32[32,768]{1,0:T(8,128)S(1)}, f32[32,768]{1,0:T(8,128)S(1)}, u32[]{:S(2)}, u32[]{:S(2)}) collective-permute-start(f32[32,768]{1,0:T(8,128)S(1)} %get-tuple-element.37), channel_id=1, source_target_pairs={{0,15},{1,2},{2,1},{3,4},{4,3},{5,6},{6,5},{7,8},{8,7},{9,10},{10,... | collective-permute-start | bytes 294920 | tf_op jit(solution)/shard_map/ppermute | solution.py:529
  11.5 8.6 %collective-permute-start.4 = (f32[128,768]{1,0:T(8,128)S(1)}, f32[128,768]{1,0:T(8,128)S(1)}, u32[]{:S(2)}, u32[]{:S(2)}) collective-permute-start(f32[128,768]{1,0:T(8,128)S(1)} %get-tuple-element.45), channel_id=1, source_target_pairs={{0,1},{1,0},{2,3},{3,2},{4,5},{5,4},{6,7},{7,6},{8,9},{9,8},{10,11... | collective-permute-start | bytes 1179656 | tf_op jit(solution)/shard_map/ppermute | solution.py:529
  11.6 8.6 %collective-permute-start.5 = (f32[128,768]{1,0:T(8,128)S(1)}, f32[128,768]{1,0:T(8,128)S(1)}, u32[]{:S(2)}, u32[]{:S(2)}) collective-permute-start(f32[128,768]{1,0:T(8,128)S(1)} %get-tuple-element.46), channel_id=1, source_target_pairs={{0,15},{1,2},{2,1},{3,4},{4,3},{5,6},{6,5},{7,8},{8,7},{9,10},{10,... | collective-permute-start | bytes 1179656 | tf_op jit(solution)/shard_map/ppermute | solution.py:529
  13.5 6.6 %collective-permute-start.2 = (f32[20,768]{1,0:T(8,128)S(1)}, f32[20,768]{1,0:T(8,128)S(1)}, u32[]{:S(2)}, u32[]{:S(2)}) collective-permute-start(f32[20,768]{1,0:T(8,128)S(1)} %get-tuple-element.42), channel_id=1, source_target_pairs={{0,16},{16,0},{32,48},{48,32},{64,80},{80,64},{96,112},{112,96},{1... | collective-permute-start | bytes 184328 | tf_op jit(solution)/shard_map/ppermute | solution.py:529
  14.1 6.1 %collective-permute-start.3 = (f32[20,768]{1,0:T(8,128)S(1)}, f32[20,768]{1,0:T(8,128)S(1)}, u32[]{:S(2)}, u32[]{:S(2)}) collective-permute-start(f32[20,768]{1,0:T(8,128)S(1)} %get-tuple-element.43), channel_id=1, source_target_pairs={{0,240},{16,32},{32,16},{48,64},{64,48},{80,96},{96,80},{112,128},... | collective-permute-start | bytes 184328 | tf_op jit(solution)/shard_map/ppermute | solution.py:529
  21.2 8.2 %collective-permute-start.6 = (f32[18,768]{1,0:T(8,128)S(1)}, f32[18,768]{1,0:T(8,128)S(1)}, u32[]{:S(2)}, u32[]{:S(2)}) collective-permute-start(f32[18,768]{1,0:T(8,128)S(1)} %get-tuple-element.54), channel_id=1, source_target_pairs={{0,16},{16,0},{32,48},{48,32},{64,80},{80,64},{96,112},{112,96},{1... | collective-permute-start | bytes 165896 | tf_op jit(solution)/shard_map/ppermute | solution.py:529
  25.1 4.4 %collective-permute-start.7 = (f32[18,768]{1,0:T(8,128)S(1)}, f32[18,768]{1,0:T(8,128)S(1)}, u32[]{:S(2)}, u32[]{:S(2)}) collective-permute-start(f32[18,768]{1,0:T(8,128)S(1)} %get-tuple-element.55), channel_id=1, source_target_pairs={{0,240},{16,32},{32,16},{48,64},{64,48},{80,96},{96,80},{112,128},... | collective-permute-start | bytes 165896 | tf_op jit(solution)/shard_map/ppermute | solution.py:529
